TPU v7x, 32 devices: a whole 2x2x4 slice. The times are simulated.
32 devices in a mesh: phase: 8 (over y, x, core), space: 4 (over z).
Axes of the slice: x: 2, y: 2, z: 4, core: 2. Of those that a mesh axis runs over, the one named last changes fastest.
Arguments:
- volume: bfloat16 [8, 16, 4, 32, 256], P('phase', 'space'), may hold values from -6 to 6
- gain_first: float32 [256], replicated, may hold values from 0.25 to 1.75
- phase_qkv: bfloat16 [256, 768], replicated, may hold values from -0.375 to 0.375
- phase_out: bfloat16 [256, 256], replicated, may hold values from -0.375 to 0.375
- bin_phase: int32 [8], replicated, may hold values from 0 to 7, each once
- phase_bias: float32 [8, 8], replicated, may hold values from -4 to 304
- gain_second: float32 [256], replicated, may hold values from 0.25 to 1.75
- window_qkv: bfloat16 [256, 768], replicated, may hold values from -0.375 to 0.375
- window_out: bfloat16 [256, 256], replicated, may hold values from -0.375 to 0.375
- window_corner: int32 [8, 3], replicated, may hold values from -3 to 0
- window_bias: float32 [8, 64], replicated, may hold values from -4 to 304
- gain_third: float32 [256], replicated, may hold values from 0.25 to 1.75
- mlp_up: bfloat16 [256, 1024], replicated, may hold values from -0.375 to 0.375
- mlp_down: bfloat16 [1024, 256], replicated, may hold values from -0.1875 to 0.1875
Outputs:
- layer_out: bfloat16 [8, 16, 4, 32, 256], P('phase', 'space')
Inputs may be any that keep to these rules, and one draw needn't show every extreme that they name: `bin_phase`: each phase 0 to 7 is held by exactly one bin. `window_corner`: head h's window covers corner to corner + 3 along each dimension.
All inputs are finite; a program needn't handle non-finite values.
Results may differ from a plain program's by a relative error of at most 0.012.
Values may be sent and summed in bfloat16 or wider, within the bound.
No kernel may reach another device: no remote copies, remote signals or barrier semaphores. Data moves between devices by JAX's collectives and lax.ppermute only.
A program may use at most 128 MiB of HBM per device.

v0:
```python
import functools
import math

import jax
import jax.numpy as jnp
from jax import lax
from jax.experimental import pallas as pl
from jax.experimental.pallas import tpu as pltpu
from jax.sharding import PartitionSpec as P

EPSILON = 1e-06
LOG2E = math.log2(math.e)
NEG = -1e30
SPAN = 4
REACH = SPAN - 1
ROWS = 16
VMEM_LIMIT = 56 * 1024 * 1024

NT = (((1,), (1,)), ((), ()))
TN = (((0,), (0,)), ((), ()))


def mm(a, b, dims=(((1,), (0,)), ((), ()))):
    return lax.dot_general(a, b, dims, preferred_element_type=jnp.float32)


def rms(values, gain):
    mean_sq = jnp.mean(values * values, axis=-1, keepdims=True)
    return (values * lax.rsqrt(mean_sq + EPSILON) * gain).astype(jnp.bfloat16)


def prep_kernel(
    bins,
    extent_x,
    extent_y,
    bin_phase,
    corner,
    window_bias,
    phase_bias,
    phase_qkv,
    window_qkv,
    phase_qv,
    window_qv,
    phase_table,
    window_table,
):
    width = phase_qkv.shape[0]
    heads = phase_bias.shape[0]
    for source, target in ((phase_qkv, phase_qv), (window_qkv, window_qv)):
        target[:width] = source[:, :width].T
        target[width:] = source[:, 2 * width :].T
    me = lax.axis_index("phase")
    tile = ROWS * bins
    slot = lax.broadcasted_iota(jnp.int32, (heads, tile), 1) // ROWS
    query_phase = jnp.zeros((heads, tile), jnp.int32)
    for member in range(bins):
        query_phase = jnp.where(slot == member, bin_phase[me ^ member], query_phase)
    same = (
        lax.broadcasted_iota(jnp.int32, (ROWS, tile), 0)
        == lax.broadcasted_iota(jnp.int32, (ROWS, tile), 1) % ROWS
    )
    bias = phase_bias[...] * LOG2E
    for member in range(bins):
        gap = bin_phase[me ^ member] - query_phase
        gap = jnp.where(gap < 0, gap + bins, gap)
        value = jnp.zeros((heads, tile), jnp.float32)
        for step in range(bins):
            value = jnp.where(gap == step, bias[:, step : step + 1], value)
        for head in range(heads):
            phase_table[
                head // 2,
                member * ROWS : (member + 1) * ROWS,
                (head % 2) * tile : (head % 2 + 1) * tile,
            ] = jnp.where(same, value[head : head + 1], NEG)
    plane = extent_x * extent_y
    shape = (extent_y, plane)
    lane = lax.broadcasted_iota(jnp.int32, shape, 1)
    lane_x = lane // extent_y
    delta_y = lax.broadcasted_iota(jnp.int32, shape, 0) - lane % extent_y
    for head in range(heads):
        first_x = corner[head, 1]
        first_y = corner[head, 2]
        y_masks = [delta_y == first_y + step for step in range(SPAN)]
        for step_z in range(SPAN):
            strips = []
            for step_x in range(SPAN):
                strip = jnp.full(shape, NEG, jnp.float32)
                for step_y in range(SPAN):
                    entry = window_bias[head, (step_z * SPAN + step_x) * SPAN + step_y] * LOG2E
                    strip = jnp.where(y_masks[step_y], entry, strip)
                strips.append(strip)
            for key_x in range(extent_x):
                block = jnp.full(shape, NEG, jnp.float32)
                for step_x in range(SPAN):
                    block = jnp.where(
                        lane_x == key_x - first_x - step_x, strips[step_x], block
                    )
                start = step_z * plane + key_x * extent_y
                window_table[
                    head // 2,
                    start : start + extent_y,
                    (head % 2) * plane : (head % 2 + 1) * plane,
                ] = block


def pair_attend(keys, queries, values, table, head_dim):
    count = queries.shape[1] // 2
    scores = mm(keys, queries) + table
    top = jnp.max(scores, axis=0, keepdims=True)
    weights = jnp.exp2(scores - top).astype(jnp.bfloat16)
    mixed = mm(values, weights)
    inverse = 1.0 / mixed[2 * head_dim : 2 * head_dim + 1]
    return jnp.concatenate(
        [
            mixed[:head_dim, :count] * inverse[:, :count],
            mixed[head_dim : 2 * head_dim, count:] * inverse[:, count:],
        ],
        axis=0,
    ).astype(jnp.bfloat16)


def block_diagonal(queries, base, head_dim, group):
    count = queries.shape[1]
    frame = base // group * group
    columns = []
    for member in range(2):
        first = base + member * head_dim - frame
        parts = []
        if first:
            parts.append(jnp.zeros((first, count), queries.dtype))
        parts.append(queries[frame + first : frame + first + head_dim])
        rest = group - first - head_dim
        if rest:
            parts.append(jnp.zeros((rest, count), queries.dtype))
        columns.append(jnp.concatenate(parts, axis=0))
    return jnp.concatenate(columns, axis=1)


def phase_kernel(bins, heads, *refs):
    blocks = refs[: bins // 2]
    gain, qkv, qv, table, out_weight = refs[bins // 2 : bins // 2 + 5]
    outs = refs[bins // 2 + 5 :]
    chunk, width = blocks[0].shape[1:]
    head_dim = width // heads
    scale = LOG2E / math.sqrt(head_dim)
    tile = ROWS * bins
    tiles = chunk // ROWS
    stream = jnp.concatenate(
        [
            blocks[slot // 2][slot % 2, step * ROWS : (step + 1) * ROWS]
            for step in range(tiles)
            for slot in range(bins)
        ],
        axis=0,
    ).astype(jnp.float32)
    normed = rms(stream, gain[...])
    keys = mm(normed, qkv[:, width : 2 * width]).astype(jnp.bfloat16)
    both = mm(qv[...], normed, NT)
    queries = (both[:width] * scale).astype(jnp.bfloat16)
    values = both[width:].astype(jnp.bfloat16)
    ones = jnp.ones((ROWS, tile), jnp.bfloat16)
    group = 128
    for step in range(tiles):
        span = slice(step * tile, (step + 1) * tile)
        parts = []
        for pair in range(heads // 2):
            base = pair * 2 * head_dim
            frame = base // group * group
            parts.append(
                pair_attend(
                    keys[span, frame : frame + group],
                    block_diagonal(queries[:, span], base, head_dim, group),
                    jnp.concatenate([values[base : base + 2 * head_dim, span], ones], axis=0),
                    table[pair],
                    head_dim,
                )
            )
        mixed = jnp.concatenate(parts, axis=0)
        result = (stream[span] + mm(mixed, out_weight[...], TN)).astype(jnp.bfloat16)
        for slot in range(bins):
            outs[slot // 2][slot % 2, step * ROWS : (step + 1) * ROWS] = result[
                slot * ROWS : (slot + 1) * ROWS
            ]


def window_kernel(
    plane,
    corner,
    own,
    low,
    high,
    gain_second,
    qkv,
    qv,
    table,
    out_weight,
    gain_third,
    mlp_up,
    mlp_down,
    out,
    key_store,
    value_store,
):
    tokens, width = own.shape
    planes = tokens // plane
    heads = corner.shape[0]
    head_dim = width // heads
    scale = LOG2E / math.sqrt(head_dim)
    reach = REACH * plane
    group = 128
    gain = gain_second[...]
    stream = own[...].astype(jnp.float32)
    normed = jnp.concatenate(
        [
            rms(low[...].astype(jnp.float32), gain),
            rms(stream, gain),
            rms(high[...].astype(jnp.float32), gain),
        ],
        axis=0,
    )
    key_store[...] = mm(normed, qkv[:, width : 2 * width]).astype(jnp.bfloat16)
    value_store[...] = mm(qv[width:], normed, NT).astype(jnp.bfloat16)
    queries = (mm(qv[:width], normed[reach : reach + tokens], NT) * scale).astype(jnp.bfloat16)
    z_first = lax.axis_index("space") * planes
    depth = lax.axis_size("space") * planes
    span = (planes + REACH) * plane
    reach_keys = SPAN * plane
    lane = lax.broadcasted_iota(jnp.int32, (1, group), 1)
    lane_head = lax.broadcasted_iota(jnp.int32, (1, 2 * plane), 1) // plane
    ones = jnp.ones((ROWS, span), jnp.bfloat16)
    pair_keys = []
    pair_values = []
    for pair in range(heads // 2):
        base = pair * 2 * head_dim
        frame = base // group * group
        first = [
            pl.multiple_of((corner[2 * pair + member, 0] + REACH) * plane, plane)
            for member in range(2)
        ]
        left = key_store[pl.ds(first[0], span), frame : frame + group]
        right = key_store[pl.ds(first[1], span), frame : frame + group]
        is_left = (lane < base + head_dim - frame).astype(jnp.bfloat16)
        pair_keys.append(left * is_left + right * (1 - is_left))
        pair_values.append(
            jnp.concatenate(
                [
                    value_store[
                        base + member * head_dim : base + (member + 1) * head_dim,
                        pl.ds(first[member], span),
                    ]
                    for member in range(2)
                ]
                + [ones],
                axis=0,
            )
        )
    for at in range(planes):
        here = slice(at * plane, (at + 1) * plane)
        parts = []
        for pair in range(heads // 2):
            base = pair * 2 * head_dim
            penalties = []
            for step in range(SPAN):
                outside = []
                for member in range(2):
                    z = z_first + at + step + corner[2 * pair + member, 0]
                    outside.append(jnp.where((z >= 0) & (z < depth), 0.0, NEG))
                penalties.append(
                    jnp.broadcast_to(
                        jnp.where(lane_head == 0, outside[0], outside[1]), (plane, 2 * plane)
                    )
                )
            parts.append(
                pair_attend(
                    pair_keys[pair][at * plane : at * plane + reach_keys],
                    block_diagonal(queries[:, here], base, head_dim, group),
                    pair_values[pair][:, at * plane : at * plane + reach_keys],
                    table[pair] + jnp.concatenate(penalties, axis=0),
                    head_dim,
                )
            )
        mixed = jnp.concatenate(parts, axis=0)
        residual = stream[here] + mm(mixed, out_weight[...], TN)
        hidden = jax.nn.gelu(mm(rms(residual, gain_third[...]), mlp_up[...]), approximate=True)
        out[here] = (residual + mm(hidden.astype(jnp.bfloat16), mlp_down[...])).astype(out.dtype)


VMEM = pl.BlockSpec(memory_space=pltpu.VMEM)
SMEM = pl.BlockSpec(memory_space=pltpu.SMEM)


def call(kernel, specs, shapes, args, scratch=(), flops=0, bytes_accessed=0):
    return pl.pallas_call(
        kernel,
        in_specs=specs,
        out_specs=[VMEM] * len(shapes),
        out_shape=[jax.ShapeDtypeStruct(shape, dtype) for shape, dtype in shapes],
        scratch_shapes=list(scratch),
        compiler_params=pltpu.CompilerParams(vmem_limit_bytes=VMEM_LIMIT),
        cost_estimate=pl.CostEstimate(
            flops=flops, bytes_accessed=bytes_accessed, transcendentals=0
        ),
    )(*args)


def local(
    volume,
    gain_first,
    phase_qkv,
    phase_out,
    bin_phase,
    phase_bias,
    gain_second,
    window_qkv,
    window_out,
    window_corner,
    window_bias,
    gain_third,
    mlp_up,
    mlp_down,
):
    planes, extent_x, extent_y, width = volume.shape[1:]
    plane = extent_x * extent_y
    tokens = planes * plane
    heads = window_corner.shape[0]
    bins = lax.axis_size("phase")
    half = bins // 2
    chunk = tokens // bins
    tile = ROWS * bins
    me = lax.axis_index("phase")
    bf16, f32 = jnp.bfloat16, jnp.float32

    def swap(block, mask):
        return lax.ppermute(block, "phase", [(i, i ^ mask) for i in range(bins)])

    own = volume.reshape(tokens, width)
    twin = swap(own, 1)

    def piece(mask):
        start = (me ^ mask) * chunk
        return jnp.stack(
            [lax.dynamic_slice_in_dim(source, start, chunk, axis=0) for source in (own, twin)]
        )

    blocks = [piece(0)] + [swap(piece(2 * step), 2 * step) for step in range(1, half)]

    phase_qv, window_qv, phase_table, window_table = call(
        functools.partial(prep_kernel, bins, extent_x, extent_y),
        [SMEM, SMEM, SMEM, VMEM, VMEM, VMEM],
        [
            ((2 * width, width), bf16),
            ((2 * width, width), bf16),
            ((heads // 2, tile, 2 * tile), f32),
            ((heads // 2, SPAN * plane, 2 * plane), f32),
        ],
        [bin_phase, window_corner, window_bias, phase_bias, phase_qkv, window_qkv],
        flops=2 * 10**9,
        bytes_accessed=4 * 2**20,
    )
    results = call(
        functools.partial(phase_kernel, bins, heads),
        [VMEM] * (half + 5),
        [((2, chunk, width), bf16)] * half,
        [*blocks, gain_first.reshape(1, width), phase_qkv, phase_qv, phase_table, phase_out],
        flops=2 * tokens * width * 5 * width,
        bytes_accessed=2**20,
    )
    got = [results[0]] + [swap(results[step], 2 * step) for step in range(1, half)]
    mine = jnp.stack([block[0] for block in got])
    theirs = swap(jnp.stack([block[1] for block in got]), 1)
    slots = jnp.stack([mine, theirs], axis=1).reshape(bins, chunk, width)
    residual = jnp.concatenate(
        [lax.dynamic_index_in_dim(slots, me ^ slot, 0, keepdims=True) for slot in range(bins)]
    ).reshape(planes, plane, width)

    count = lax.axis_size("space")
    place = lax.axis_index("space")
    first = 1 - place % 2
    even = [(i, i ^ 1) for i in range(count) if i ^ 1 < count]
    odd = [(i, ((i + 1) ^ 1) - 1) for i in range(count) if 0 <= ((i + 1) ^ 1) - 1 < count]
    inner = lax.ppermute(
        lax.dynamic_slice_in_dim(residual, first * (planes - REACH), REACH, axis=0), "space", even
    )
    outer = lax.ppermute(
        lax.dynamic_slice_in_dim(residual, (1 - first) * (planes - REACH), REACH, axis=0),
        "space",
        odd,
    )
    is_even = place % 2 == 0
    low = jnp.where(is_even, outer, inner)
    high = jnp.where(is_even, inner, outer)
    reach = REACH * plane
    ext = tokens + 2 * reach
    (out,) = call(
        functools.partial(window_kernel, plane),
        [SMEM] + [VMEM] * 11,
        [((tokens, width), bf16)],
        [
            window_corner,
            residual.reshape(tokens, width),
            low.reshape(reach, width),
            high.reshape(reach, width),
            gain_second.reshape(1, width),
            window_qkv,
            window_qv,
            window_table,
            window_out,
            gain_third.reshape(1, width),
            mlp_up,
            mlp_down,
        ],
        scratch=[pltpu.VMEM((ext, width), bf16), pltpu.VMEM((width, ext), bf16)],
        flops=2 * tokens * width * 14 * width,
        bytes_accessed=2**22,
    )
    return out.reshape(volume.shape)


def solution(mesh):
    split = P("phase", "space", None, None, None)
    in_specs = (split,) + (P(),) * 13
    return jax.shard_map(local, mesh=mesh, in_specs=in_specs, out_specs=split, check_vma=False)
```

profile of v0, /device:TPU:0, one launch (start us, length us, event | category | flops | bytes accessed | tf_op | source)
XLA Modules:
  0.0 51.7 jit_solution(14610194570270420438)
XLA Ops:
  0.0 0.5 collective-permute-start
  0.5 1.3 %copy.19.corner = s32[8,3]{1,0:T(8,128)} copy(s32[8,3]{0,1:T(4,128)} %param.23) | data formatting | bytes 192 | tf_op args[9]
  1.8 0.8 %dynamic-slice_bitcast_fusion.1 = (bf16[1,64,256]{2,1,0:T(8,128)(2,1)S(1)}, bf16[1,64,256]{2,1,0:T(8,128)(2,1)S(1)}, bf16[1,64,256]{2,1,0:T(8,128)(2,1)S(1)}, bf16[1,64,256]{2,1,0:T(8,128)(2,1)S(1)}) fusion(bf16[512,256]{1,0:T(8,128)(2,1)} %bitcast.43, s32[]{:T(128)S(6)} %select_n.71, s32[]{:T(128)S(6)} %select_n.70, s32[]{:T(128)S(6)} %select_n.69, ...), kind=kLoop, calls=%fused_computation.18 | loop fusion | bytes 262160 | tf_op jit(solution)/shard_map/stack | solution.py:341
  2.6 3.4 %shard_map.136 = (bf16[512,256]{1,0:T(8,128)(2,1)}, bf16[512,256]{1,0:T(8,128)(2,1)}, f32[4,128,256]{2,1,0:T(8,128)}, f32[4,512,256]{2,1,0:T(8,128)}) custom-call(s32[8]{0:T(128)} %bin_phase.1, s32[8,3]{1,0:T(8,128)} %copy.19.corner, f32[8,64]{1,0:T(8,128)} %window_bias.1, f32[8,8]{1,0:T(8,128)} %phase_bias.1, bf16[256,768]{1,0:T(8,128)(2,1)} %refs_5_.1, ...), custom_call_target="tpu_custom_call" | custom-call | flops 2000000000 | bytes 4194304 | tf_op jit(solution)/shard_map/pallas_call | solution.py:293
  6.0 0.0 collective-permute-done
  6.1 2.6 %collective-permute-start.1 = (bf16[2,64,256]{2,1,0:T(8,128)(2,1)S(1)}, bf16[2,64,256]{2,1,0:T(8,128)(2,1)S(1)}, u32[]{:S(2)}, u32[]{:S(2)}) collective-permute-start(bf16[2,64,256]{2,1,0:T(8,128)(2,1)S(1)} %pad_maximum_fusion.3), channel_id=1, source_target_pairs={{0,8},{4,12},{8,0},{12,4},{16,24},{20,28},{24,16},{28,20},{1,9},{5... | collective-permute-start | bytes 196616 | tf_op jit(solution)/shard_map/ppermute | solution.py:334
  8.6 1.6 %collective-permute-start.2 = (bf16[2,64,256]{2,1,0:T(8,128)(2,1)S(1)}, bf16[2,64,256]{2,1,0:T(8,128)(2,1)S(1)}, u32[]{:S(2)}, u32[]{:S(2)}) collective-permute-start(bf16[2,64,256]{2,1,0:T(8,128)(2,1)S(1)} %pad_maximum_fusion.4), channel_id=1, source_target_pairs={{0,16},{4,20},{8,24},{12,28},{16,0},{20,4},{24,8},{28,12},{1,17},{... | collective-permute-start | bytes 196616 | tf_op jit(solution)/shard_map/ppermute | solution.py:334
  10.2 0.1 collective-permute-start.3
  10.3 0.6 %pad_maximum_fusion.2.refs_0_ = bf16[2,64,256]{2,1,0:T(8,128)(2,1)} fusion(bf16[1,64,256]{2,1,0:T(8,128)(2,1)S(1)} %get-tuple-element.32, bf16[1,64,256]{2,1,0:T(8,128)(2,1)S(1)} %get-tuple-element.28), kind=kLoop, calls=%fused_computation.5 | loop fusion | flops 32768 | bytes 131072 | tf_op jit(solution)/shard_map/stack | solution.py:341
  10.9 0.5 collective-permute-done.1.refs_1_
  11.4 0.0 copy-start.1
  11.4 1.6 %collective-permute-done.2.refs_2_ = bf16[2,64,256]{2,1,0:T(8,128)(2,1)S(1)} collective-permute-done((bf16[2,64,256]{2,1,0:T(8,128)(2,1)S(1)}, bf16[2,64,256]{2,1,0:T(8,128)(2,1)S(1)}, u32[]{:S(2)}, u32[]{:S(2)}) %collective-permute-start.2) | collective-permute-done | bytes 65568 | tf_op jit(solution)/shard_map/ppermute | solution.py:334
  13.0 0.0 copy-start.2
  13.0 2.5 %collective-permute-done.3.refs_3_ = bf16[2,64,256]{2,1,0:T(8,128)(2,1)S(1)} collective-permute-done((bf16[2,64,256]{2,1,0:T(8,128)(2,1)S(1)}, bf16[2,64,256]{2,1,0:T(8,128)(2,1)S(1)}, u32[]{:S(2)}, u32[]{:S(2)}) %collective-permute-start.3) | collective-permute-done | bytes 65568 | tf_op jit(solution)/shard_map/ppermute | solution.py:334
  15.5 0.0 copy-start.3
  15.5 0.0 copy-done.1
  15.5 0.0 copy-done.2
  15.5 0.6 %copy-done.3 = bf16[2,64,256]{2,1,0:T(8,128)(2,1)} copy-done((bf16[2,64,256]{2,1,0:T(8,128)(2,1)}, bf16[2,64,256]{2,1,0:T(8,128)(2,1)S(1)}, u32[]{:S(2)}) %copy-start.3) | copy-done | bytes 65560
  16.1 5.5 %shard_map.137 = (bf16[2,64,256]{2,1,0:T(8,128)(2,1)}, bf16[2,64,256]{2,1,0:T(8,128)(2,1)}, bf16[2,64,256]{2,1,0:T(8,128)(2,1)}, bf16[2,64,256]{2,1,0:T(8,128)(2,1)}) custom-call(bf16[2,64,256]{2,1,0:T(8,128)(2,1)} %pad_maximum_fusion.2.refs_0_, bf16[2,64,256]{2,1,0:T(8,128)(2,1)} %copy-done.1, bf16[2,64,256]{2,1,0:T(8,128)(2,1)} %copy-done.2, ...), custom_call_target="tpu_custom_call" | custom-call | flops 335544320 | bytes 1048576 | tf_op jit(solution)/shard_map/pallas_call | solution.py:293
  21.5 0.5 %collective-permute-start.4 = (bf16[2,64,256]{2,1,0:T(8,128)(2,1)}, bf16[2,64,256]{2,1,0:T(8,128)(2,1)S(1)}, u32[]{:S(2)}, u32[]{:S(2)}) collective-permute-start(bf16[2,64,256]{2,1,0:T(8,128)(2,1)} %get-tuple-element.16), channel_id=1, source_target_pairs={{0,8},{4,12},{8,0},{12,4},{16,24},{20,28},{24,16},{28,20},{1,9},{5... | collective-permute-start | bytes 196616 | tf_op jit(solution)/shard_map/ppermute | solution.py:334
  22.1 0.5 collective-permute-start.5
  22.5 2.5 %collective-permute-start.6 = (bf16[2,64,256]{2,1,0:T(8,128)(2,1)}, bf16[2,64,256]{2,1,0:T(8,128)(2,1)S(1)}, u32[]{:S(2)}, u32[]{:S(2)}) collective-permute-start(bf16[2,64,256]{2,1,0:T(8,128)(2,1)} %get-tuple-element.18), channel_id=1, source_target_pairs={{0,24},{4,28},{8,16},{12,20},{16,8},{20,12},{24,0},{28,4},{1,25},{... | collective-permute-start | bytes 196616 | tf_op jit(solution)/shard_map/ppermute | solution.py:334
  25.0 0.8 %fusion = (bf16[1,64,256]{2,1,0:T(8,128)(2,1)S(1)}, bf16[1,64,256]{2,1,0:T(8,128)(2,1)S(1)}) fusion(bf16[2,64,256]{2,1,0:T(8,128)(2,1)} %get-tuple-element.15), kind=kLoop, calls=%fused_computation.27 | loop fusion | bytes 131072 | tf_op jit(solution)/shard_map/slice | solution.py:369
  25.8 0.2 collective-permute-done.4
  26.0 0.5 %collective-permute-done.5 = bf16[2,64,256]{2,1,0:T(8,128)(2,1)S(1)} collective-permute-done((bf16[2,64,256]{2,1,0:T(8,128)(2,1)}, bf16[2,64,256]{2,1,0:T(8,128)(2,1)S(1)}, u32[]{:S(2)}, u32[]{:S(2)}) %collective-permute-start.5) | collective-permute-done | bytes 65568 | tf_op jit(solution)/shard_map/ppermute | solution.py:334
  26.6 1.4 %collective-permute-done.6 = bf16[2,64,256]{2,1,0:T(8,128)(2,1)S(1)} collective-permute-done((bf16[2,64,256]{2,1,0:T(8,128)(2,1)}, bf16[2,64,256]{2,1,0:T(8,128)(2,1)S(1)}, u32[]{:S(2)}, u32[]{:S(2)}) %collective-permute-start.6) | collective-permute-done | bytes 65568 | tf_op jit(solution)/shard_map/ppermute | solution.py:334
  28.0 0.1 collective-permute-start.7
  28.1 1.2 %collective-permute-done.7 = bf16[4,64,256]{2,1,0:T(8,128)(2,1)S(1)} collective-permute-done((bf16[4,64,256]{2,1,0:T(8,128)(2,1)S(1)}, bf16[4,64,256]{2,1,0:T(8,128)(2,1)S(1)}, u32[]{:S(2)}, u32[]{:S(2)}) %collective-permute-start.7) | collective-permute-done | bytes 131104 | tf_op jit(solution)/shard_map/ppermute | solution.py:334
  29.6 0.0 copy-start
  29.6 0.7 %collective-permute-start.8 = (bf16[3,128,256]{2,1,0:T(8,128)(2,1)S(1)}, bf16[3,128,256]{2,1,0:T(8,128)(2,1)S(1)}, u32[]{:S(2)}, u32[]{:S(2)}) collective-permute-start(bf16[3,128,256]{2,1,0:T(8,128)(2,1)S(1)} %get-tuple-element.24), channel_id=1, source_target_pairs={{1,2},{2,1},{5,6},{6,5},{9,10},{10,9},{13,14},{14,13},{17,18},{18,... | collective-permute-start | bytes 589832 | tf_op jit(solution)/shard_map/ppermute | solution.py:384
  30.3 4.5 %collective-permute-start.9 = (bf16[3,128,256]{2,1,0:T(8,128)(2,1)S(1)}, bf16[3,128,256]{2,1,0:T(8,128)(2,1)S(1)}, u32[]{:S(2)}, u32[]{:S(2)}) collective-permute-start(bf16[3,128,256]{2,1,0:T(8,128)(2,1)S(1)} %get-tuple-element.23), channel_id=1, source_target_pairs={{0,1},{1,0},{2,3},{3,2},{4,5},{5,4},{6,7},{7,6},{8,9},{9,8},{10,11... | collective-permute-start | bytes 589832 | tf_op jit(solution)/shard_map/ppermute | solution.py:381
  34.8 0.0 collective-permute-done.8
  34.8 4.9 %collective-permute-done.9 = bf16[3,128,256]{2,1,0:T(8,128)(2,1)S(1)} collective-permute-done((bf16[3,128,256]{2,1,0:T(8,128)(2,1)S(1)}, bf16[3,128,256]{2,1,0:T(8,128)(2,1)S(1)}, u32[]{:S(2)}, u32[]{:S(2)}) %collective-permute-start.9) | collective-permute-done | bytes 196640 | tf_op jit(solution)/shard_map/ppermute | solution.py:381
  39.7 0.8 %broadcast_select_fusion = (bf16[3,128,256]{2,1,0:T(8,128)(2,1)}, bf16[3,128,256]{2,1,0:T(8,128)(2,1)}) fusion(bf16[3,128,256]{2,1,0:T(8,128)(2,1)S(1)} %collective-permute-done.9, bf16[3,128,256]{2,1,0:T(8,128)(2,1)S(1)} %collective-permute-done.8, pred[]{:T(512)S(6)} %eq.6), kind=kLoop, calls=%fused_computation.1 | loop fusion | flops 196608 | bytes 786433 | tf_op jit(solution)/shard_map/jit(_where)/select_n | solution.py:391
  40.5 0.0 copy-done
  40.5 11.2 %shard_map.138 = bf16[512,256]{1,0:T(8,128)(2,1)} custom-call(s32[8,3]{1,0:T(8,128)} %copy.19.corner, bf16[512,256]{1,0:T(8,128)(2,1)} %bitcast.30, bf16[384,256]{1,0:T(8,128)(2,1)} %bitcast.40, bf16[384,256]{1,0:T(8,128)(2,1)} %bitcast.39, f32[1,256]{1,0:T(1,128)} %bitcast.44, bf16[256,768]{1,0:T(8,128)(2,1)} %qkv.1, ...), custom_call_target="tpu_custom_call" | custom-call | flops 939524096 | bytes 4194304 | tf_op jit(solution)/shard_map/pallas_call | solution.py:293
  (20 shorter events, 0.3 us)
Async XLA Ops:
  0.0 6.0 %collective-permute-start = (bf16[512,256]{1,0:T(8,128)(2,1)}, bf16[512,256]{1,0:T(8,128)(2,1)S(1)}, u32[]{:S(2)}, u32[]{:S(2)}) collective-permute-start(bf16[512,256]{1,0:T(8,128)(2,1)} %bitcast.42), channel_id=1, source_target_pairs={{0,4},{4,0},{8,12},{12,8},{16,20},{20,16},{24,28},{28,24},{1,5},{5... | collective-permute-start | bytes 786440 | tf_op jit(solution)/shard_map/ppermute | solution.py:334
  6.1 5.3 %collective-permute-start.1 = (bf16[2,64,256]{2,1,0:T(8,128)(2,1)S(1)}, bf16[2,64,256]{2,1,0:T(8,128)(2,1)S(1)}, u32[]{:S(2)}, u32[]{:S(2)}) collective-permute-start(bf16[2,64,256]{2,1,0:T(8,128)(2,1)S(1)} %pad_maximum_fusion.3), channel_id=1, source_target_pairs={{0,8},{4,12},{8,0},{12,4},{16,24},{20,28},{24,16},{28,20},{1,9},{5... | collective-permute-start | bytes 196616 | tf_op jit(solution)/shard_map/ppermute | solution.py:334
  8.6 4.3 %collective-permute-start.2 = (bf16[2,64,256]{2,1,0:T(8,128)(2,1)S(1)}, bf16[2,64,256]{2,1,0:T(8,128)(2,1)S(1)}, u32[]{:S(2)}, u32[]{:S(2)}) collective-permute-start(bf16[2,64,256]{2,1,0:T(8,128)(2,1)S(1)} %pad_maximum_fusion.4), channel_id=1, source_target_pairs={{0,16},{4,20},{8,24},{12,28},{16,0},{20,4},{24,8},{28,12},{1,17},{... | collective-permute-start | bytes 196616 | tf_op jit(solution)/shard_map/ppermute | solution.py:334
  10.2 5.2 %collective-permute-start.3 = (bf16[2,64,256]{2,1,0:T(8,128)(2,1)S(1)}, bf16[2,64,256]{2,1,0:T(8,128)(2,1)S(1)}, u32[]{:S(2)}, u32[]{:S(2)}) collective-permute-start(bf16[2,64,256]{2,1,0:T(8,128)(2,1)S(1)} %pad_maximum_fusion.5), channel_id=1, source_target_pairs={{0,24},{4,28},{8,16},{12,20},{16,8},{20,12},{24,0},{28,4},{1,25},{... | collective-permute-start | bytes 196616 | tf_op jit(solution)/shard_map/ppermute | solution.py:334
  11.4 4.1 %copy-start.1 = (bf16[2,64,256]{2,1,0:T(8,128)(2,1)}, bf16[2,64,256]{2,1,0:T(8,128)(2,1)S(1)}, u32[]{:S(2)}) copy-start(bf16[2,64,256]{2,1,0:T(8,128)(2,1)S(1)} %collective-permute-done.1.refs_1_) | copy-start | bytes 196612
  13.0 2.5 %copy-start.2 = (bf16[2,64,256]{2,1,0:T(8,128)(2,1)}, bf16[2,64,256]{2,1,0:T(8,128)(2,1)S(1)}, u32[]{:S(2)}) copy-start(bf16[2,64,256]{2,1,0:T(8,128)(2,1)S(1)} %collective-permute-done.2.refs_2_) | copy-start | bytes 196612
  15.5 0.6 %copy-start.3 = (bf16[2,64,256]{2,1,0:T(8,128)(2,1)}, bf16[2,64,256]{2,1,0:T(8,128)(2,1)S(1)}, u32[]{:S(2)}) copy-start(bf16[2,64,256]{2,1,0:T(8,128)(2,1)S(1)} %collective-permute-done.3.refs_3_) | copy-start | bytes 196612
  21.5 4.5 %collective-permute-start.4 = (bf16[2,64,256]{2,1,0:T(8,128)(2,1)}, bf16[2,64,256]{2,1,0:T(8,128)(2,1)S(1)}, u32[]{:S(2)}, u32[]{:S(2)}) collective-permute-start(bf16[2,64,256]{2,1,0:T(8,128)(2,1)} %get-tuple-element.16), channel_id=1, source_target_pairs={{0,8},{4,12},{8,0},{12,4},{16,24},{20,28},{24,16},{28,20},{1,9},{5... | collective-permute-start | bytes 196616 | tf_op jit(solution)/shard_map/ppermute | solution.py:334
  22.1 4.5 %collective-permute-start.5 = (bf16[2,64,256]{2,1,0:T(8,128)(2,1)}, bf16[2,64,256]{2,1,0:T(8,128)(2,1)S(1)}, u32[]{:S(2)}, u32[]{:S(2)}) collective-permute-start(bf16[2,64,256]{2,1,0:T(8,128)(2,1)} %get-tuple-element.17), channel_id=1, source_target_pairs={{0,16},{4,20},{8,24},{12,28},{16,0},{20,4},{24,8},{28,12},{1,17},{... | collective-permute-start | bytes 196616 | tf_op jit(solution)/shard_map/ppermute | solution.py:334
  22.5 5.4 %collective-permute-start.6 = (bf16[2,64,256]{2,1,0:T(8,128)(2,1)}, bf16[2,64,256]{2,1,0:T(8,128)(2,1)S(1)}, u32[]{:S(2)}, u32[]{:S(2)}) collective-permute-start(bf16[2,64,256]{2,1,0:T(8,128)(2,1)} %get-tuple-element.18), channel_id=1, source_target_pairs={{0,24},{4,28},{8,16},{12,20},{16,8},{20,12},{24,0},{28,4},{1,25},{... | collective-permute-start | bytes 196616 | tf_op jit(solution)/shard_map/ppermute | solution.py:334
  28.0 1.4 %collective-permute-start.7 = (bf16[4,64,256]{2,1,0:T(8,128)(2,1)S(1)}, bf16[4,64,256]{2,1,0:T(8,128)(2,1)S(1)}, u32[]{:S(2)}, u32[]{:S(2)}) collective-permute-start(bf16[4,64,256]{2,1,0:T(8,128)(2,1)S(1)} %pad_maximum_fusion.1), channel_id=1, source_target_pairs={{0,4},{4,0},{8,12},{12,8},{16,20},{20,16},{24,28},{28,24},{1,5},{5... | collective-permute-start | bytes 393224 | tf_op jit(solution)/shard_map/ppermute | solution.py:334
  29.6 10.9 %copy-start = (bf16[8,64,256]{2,1,0:T(8,128)(2,1)}, bf16[8,64,256]{2,1,0:T(8,128)(2,1)S(1)}, u32[]{:S(2)}) copy-start(bf16[8,64,256]{2,1,0:T(8,128)(2,1)S(1)} %dynamic-slice_dynamic-update-slice_fusion) | copy-start | bytes 786436
  29.6 5.2 %collective-permute-start.8 = (bf16[3,128,256]{2,1,0:T(8,128)(2,1)S(1)}, bf16[3,128,256]{2,1,0:T(8,128)(2,1)S(1)}, u32[]{:S(2)}, u32[]{:S(2)}) collective-permute-start(bf16[3,128,256]{2,1,0:T(8,128)(2,1)S(1)} %get-tuple-element.24), channel_id=1, source_target_pairs={{1,2},{2,1},{5,6},{6,5},{9,10},{10,9},{13,14},{14,13},{17,18},{18,... | collective-permute-start | bytes 589832 | tf_op jit(solution)/shard_map/ppermute | solution.py:384
  30.3 9.4 %collective-permute-start.9 = (bf16[3,128,256]{2,1,0:T(8,128)(2,1)S(1)}, bf16[3,128,256]{2,1,0:T(8,128)(2,1)S(1)}, u32[]{:S(2)}, u32[]{:S(2)}) collective-permute-start(bf16[3,128,256]{2,1,0:T(8,128)(2,1)S(1)} %get-tuple-element.23), channel_id=1, source_target_pairs={{0,1},{1,0},{2,3},{3,2},{4,5},{5,4},{6,7},{7,6},{8,9},{9,8},{10,11... | collective-permute-start | bytes 589832 | tf_op jit(solution)/shard_map/ppermute | solution.py:381
where the time goes:
time: 52 us; the launch traced here: 51.7 us
  Pallas kernels  20 us (38%)
  starting transfers between devices  13.4 us (26%)
  waiting for transfers between devices  12.8 us (25%)
  local copies, waits for them, and re-layouts  3.74 us (7%)
  other arithmetic  1.49 us (3%)
    pallas_call x3, Pallas kernels, call(): pl.pallas_call(kernel, in_specs=specs, out_specs=[VMEM] * len(shapes), ou...  20 us
    ppermute x8, starting transfers between devices, swap(): return lax.ppermute(block, 'phase', [(i, i ^ mask) for i in range(bins)])  8.21 us
    ppermute x8, waiting for transfers between devices, swap(): return lax.ppermute(block, 'phase', [(i, i ^ mask) for i in range(bins)])  7.86 us
    ppermute x1, waiting for transfers between devices, local(): lax.ppermute(lax.dynamic_slice_in_dim(residual, first * (planes - REACH),...  4.93 us
    ppermute x1, starting transfers between devices, local(): lax.ppermute(lax.dynamic_slice_in_dim(residual, first * (planes - REACH),...  4.48 us
    unnamed x16, local copies, waits for them, and re-layouts  2.05 us
  transfers between devices with their start and end apart: 10, of which 8 were waited for; matrix products, arithmetic and copies ran while one was open for 7% of the time, Pallas kernels for 7%

commit v1 on v0

v1 whole, which is shorter than its diff:
```python
import functools
import math

import jax
import jax.numpy as jnp
from jax import lax
from jax.experimental import pallas as pl
from jax.experimental.pallas import tpu as pltpu
from jax.sharding import PartitionSpec as P

EPSILON = 1e-06
LOG2E = math.log2(math.e)
NEG = -1e30
SPAN = 4
REACH = SPAN - 1
ROWS = 16
MIB = 2**20

NT = (((1,), (1,)), ((), ()))
TN = (((0,), (0,)), ((), ()))


def mm(a, b, dims=(((1,), (0,)), ((), ()))):
    return lax.dot_general(a, b, dims, preferred_element_type=jnp.float32)


def rms(values, gain):
    mean_sq = jnp.mean(values * values, axis=-1, keepdims=True)
    return (values * lax.rsqrt(mean_sq + EPSILON) * gain).astype(jnp.bfloat16)


def prep_kernel(
    bins,
    extent_x,
    extent_y,
    bin_phase_at,
    corner_at,
    window_bias_at,
    phase_bias_at,
    phase_qkv_at,
    _,
    phase_weights,
    phase_table,
    window_table,
    bin_phase,
    corner,
    window_bias,
    phase_bias,
    phase_qkv,
    sems,
):
    copies = [
        pltpu.make_async_copy(source, target, sems.at[index])
        for index, (source, target) in enumerate(
            (
                (bin_phase_at, bin_phase),
                (corner_at, corner),
                (window_bias_at, window_bias),
                (phase_bias_at, phase_bias),
                (phase_qkv_at, phase_qkv),
            )
        )
    ]
    for copy in copies:
        copy.start()
    for copy in copies:
        copy.wait()
    width = phase_qkv.shape[0]
    heads = phase_bias.shape[0]
    phase_weights[:width] = phase_qkv[:, :width].T
    phase_weights[width : 2 * width] = phase_qkv[:, 2 * width :].T
    phase_weights[2 * width :] = phase_qkv[:, width : 2 * width]
    me = lax.axis_index("phase")
    tile = ROWS * bins
    slot = lax.broadcasted_iota(jnp.int32, (heads, tile), 1) // ROWS
    query_phase = jnp.zeros((heads, tile), jnp.int32)
    for member in range(bins):
        query_phase = jnp.where(slot == member, bin_phase[me ^ member], query_phase)
    same = (
        lax.broadcasted_iota(jnp.int32, (ROWS, tile), 0)
        == lax.broadcasted_iota(jnp.int32, (ROWS, tile), 1) % ROWS
    )
    bias = phase_bias[...] * LOG2E
    for member in range(bins):
        gap = bin_phase[me ^ member] - query_phase
        gap = jnp.where(gap < 0, gap + bins, gap)
        value = jnp.zeros((heads, tile), jnp.float32)
        for step in range(bins):
            value = jnp.where(gap == step, bias[:, step : step + 1], value)
        for head in range(heads):
            phase_table[
                head // 2,
                member * ROWS : (member + 1) * ROWS,
                (head % 2) * tile : (head % 2 + 1) * tile,
            ] = jnp.where(same, value[head : head + 1], NEG)
    plane = extent_x * extent_y
    shape = (extent_y, plane)
    lane = lax.broadcasted_iota(jnp.int32, shape, 1)
    lane_x = lane // extent_y
    delta_y = lax.broadcasted_iota(jnp.int32, shape, 0) - lane % extent_y
    for head in range(heads):
        first_x = corner[1, head]
        first_y = corner[2, head]
        y_masks = [delta_y == first_y + step for step in range(SPAN)]
        for step_z in range(SPAN):
            strips = []
            for step_x in range(SPAN):
                strip = jnp.full(shape, NEG, jnp.float32)
                for step_y in range(SPAN):
                    entry = window_bias[head, (step_z * SPAN + step_x) * SPAN + step_y] * LOG2E
                    strip = jnp.where(y_masks[step_y], entry, strip)
                strips.append(strip)
            for key_x in range(extent_x):
                block = jnp.full(shape, NEG, jnp.float32)
                for step_x in range(SPAN):
                    block = jnp.where(
                        lane_x == key_x - first_x - step_x, strips[step_x], block
                    )
                start = step_z * plane + key_x * extent_y
                window_table[
                    head // 2,
                    start : start + extent_y,
                    (head % 2) * plane : (head % 2 + 1) * plane,
                ] = block


def score(keys, queries, table):
    scores = mm(keys, queries) + table
    return scores, jnp.max(scores, axis=0, keepdims=True)


def soften(scores, top):
    return jnp.exp2(scores - top).astype(jnp.bfloat16)


def blend(values, weights, head_dim):
    count = weights.shape[1] // 2
    mixed = mm(values, weights)
    inverse = 1.0 / mixed[2 * head_dim : 2 * head_dim + 1]
    return jnp.concatenate(
        [
            mixed[:head_dim, :count] * inverse[:, :count],
            mixed[head_dim : 2 * head_dim, count:] * inverse[:, count:],
        ],
        axis=0,
    ).astype(jnp.bfloat16)


def run_pipeline(units, first, second, third, after):
    held = first(units[0])
    weights = None
    for index, unit in enumerate(units):
        following = first(units[index + 1]) if index + 1 < len(units) else None
        now = second(held)
        if index:
            third(units[index - 1], weights)
            after(index - 1)
        weights = now
        held = following
    third(units[-1], weights)
    after(len(units) - 1)


def block_diagonal(queries, base, head_dim, group, extra=None):
    count = queries.shape[1]
    first = base % group
    left = queries[base : base + head_dim]
    right = queries[base + head_dim : base + 2 * head_dim]
    zero = jnp.zeros((head_dim, count), queries.dtype)
    body = jnp.concatenate(
        [jnp.concatenate([left, zero], axis=1), jnp.concatenate([zero, right], axis=1)], axis=0
    )
    spare = group - 2 * head_dim
    if extra is None:
        pad = jnp.zeros((spare, 2 * count), queries.dtype)
    else:
        pad = jnp.concatenate(
            [extra, jnp.zeros((spare - ROWS, 2 * count), queries.dtype)], axis=0
        )
    return jnp.concatenate([body, pad] if first == 0 else [pad, body], axis=0)


def phase_kernel(bins, heads, *refs):
    blocks = refs[: bins // 2]
    gain, weights_in, table, out_weight = refs[bins // 2 : bins // 2 + 4]
    outs = refs[bins // 2 + 4 :]
    chunk, width = blocks[0].shape[1:]
    head_dim = width // heads
    scale = LOG2E / math.sqrt(head_dim)
    tile = ROWS * bins
    tiles = chunk // ROWS
    pairs = heads // 2
    group = 128
    stream = jnp.concatenate(
        [
            blocks[slot // 2][slot % 2, step * ROWS : (step + 1) * ROWS]
            for step in range(tiles)
            for slot in range(bins)
        ],
        axis=0,
    ).astype(jnp.float32)
    normed = rms(stream, gain[...])
    keys = mm(normed, weights_in[2 * width :]).astype(jnp.bfloat16)
    both = mm(weights_in[: 2 * width], normed, NT)
    queries = (both[:width] * scale).astype(jnp.bfloat16)
    values = both[width:].astype(jnp.bfloat16)
    ones = jnp.ones((ROWS, tile), jnp.bfloat16)
    units = [(step, pair) for step in range(tiles) for pair in range(pairs)]
    parts = []

    def first(unit):
        step, pair = unit
        span = slice(step * tile, (step + 1) * tile)
        base = pair * 2 * head_dim
        frame = base // group * group
        return score(
            keys[span, frame : frame + group],
            block_diagonal(queries[:, span], base, head_dim, group),
            table[pair],
        )

    def third(unit, weights):
        step, pair = unit
        span = slice(step * tile, (step + 1) * tile)
        base = pair * 2 * head_dim
        stack = jnp.concatenate([values[base : base + 2 * head_dim, span], ones], axis=0)
        parts.append(blend(stack, weights, head_dim))

    def after(index):
        if index % pairs != pairs - 1:
            return
        step = index // pairs
        mixed = jnp.concatenate(parts[step * pairs :], axis=0)
        span = slice(step * tile, (step + 1) * tile)
        result = (stream[span] + mm(mixed, out_weight[...], TN)).astype(jnp.bfloat16)
        for slot in range(bins):
            outs[slot // 2][slot % 2, step * ROWS : (step + 1) * ROWS] = result[
                slot * ROWS : (slot + 1) * ROWS
            ]

    run_pipeline(units, first, lambda held: soften(*held), third, after)


def gather_kernel(plane, half, *refs):
    got, twins = refs[:half], refs[half : 2 * half]
    residual, inner, outer = refs[2 * half :]
    me = lax.axis_index("phase")
    chunk = got[0].shape[1]
    for step in range(half):
        for part, source in enumerate((got[step], twins[step])):
            start = pl.multiple_of((me ^ (2 * step + part)) * chunk, ROWS)
            residual[pl.ds(start, chunk)] = source[part]
    reach = inner.shape[0]
    extra = residual.shape[0] - reach
    odd = lax.axis_index("space") % 2
    inner[...] = residual[pl.ds(pl.multiple_of((1 - odd) * extra, plane), reach)]
    outer[...] = residual[pl.ds(pl.multiple_of(odd * extra, plane), reach)]


def window_kernel(
    plane,
    corner,
    own,
    inner,
    outer,
    gain_second,
    qkv,
    table,
    out_weight,
    gain_third,
    mlp_up,
    mlp_down,
    out,
    key_store,
    value_store,
    pair_store,
):
    tokens, width = own.shape
    planes = tokens // plane
    heads = corner.shape[1]
    pairs = heads // 2
    head_dim = width // heads
    scale = LOG2E / math.sqrt(head_dim)
    reach = REACH * plane
    group = 128
    gain = gain_second[...]
    place = lax.axis_index("space")
    is_even = place % 2 == 0
    stream = own[...].astype(jnp.float32)
    own_normed = rms(stream, gain)
    key_weight = qkv[:, width : 2 * width]
    value_weight = qkv[:, 2 * width :].T
    query_weight = qkv[:, :width].T

    def project(normed, start, count):
        key_store[pl.ds(start, count)] = mm(normed, key_weight).astype(jnp.bfloat16)
        value_store[:, pl.ds(start, count)] = mm(value_weight, normed, NT).astype(jnp.bfloat16)

    project(own_normed, reach, tokens)
    queries = (mm(query_weight, own_normed, NT) * scale).astype(jnp.bfloat16)
    for source, at_end in ((inner, is_even), (outer, jnp.logical_not(is_even))):
        start = pl.multiple_of(jnp.where(at_end, reach + tokens, 0), plane)
        project(rms(source[...].astype(jnp.float32), gain), start, reach)
    z_first = place * planes
    depth = lax.axis_size("space") * planes
    span = (planes + REACH) * plane
    reach_keys = SPAN * plane
    lane = lax.broadcasted_iota(jnp.int32, (1, group), 1)
    ones = jnp.ones((ROWS, span), jnp.bfloat16)
    row = lax.broadcasted_iota(jnp.int32, (ROWS, 2 * plane), 0)
    lane_head = lax.broadcasted_iota(jnp.int32, (ROWS, 2 * plane), 1) // plane
    block_out = jnp.where(row == lane_head, NEG, 0.0).astype(jnp.bfloat16)
    pair_values = []
    for pair in range(pairs):
        base = pair * 2 * head_dim
        frame = base // group * group
        spare = 2 * head_dim if base == frame else 0
        first_z = [corner[0, 2 * pair + member] for member in range(2)]
        start = [pl.multiple_of((z + REACH) * plane, plane) for z in first_z]
        keep = [
            (
                (lane >= base + member * head_dim - frame)
                & (lane < base + (member + 1) * head_dim - frame)
            ).astype(jnp.bfloat16)
            for member in range(2)
        ]
        for at in range(planes + REACH):
            flags = jnp.zeros((1, group), jnp.float32)
            for member in range(2):
                z = z_first + at + first_z[member]
                flag = jnp.where((z >= 0) & (z < depth), 0.0, 1.0)
                flags = jnp.where(lane == spare + member, flag, flags)
            rows = [pl.ds(pl.multiple_of(start[m] + at * plane, plane), plane) for m in range(2)]
            pair_store[pair, at * plane : (at + 1) * plane] = (
                key_store[rows[0], frame : frame + group] * keep[0]
                + key_store[rows[1], frame : frame + group] * keep[1]
                + flags.astype(jnp.bfloat16)
            )
        pair_values.append(
            jnp.concatenate(
                [
                    value_store[
                        base + member * head_dim : base + (member + 1) * head_dim,
                        pl.ds(start[member], span),
                    ]
                    for member in range(2)
                ]
                + [ones],
                axis=0,
            )
        )
    units = [(at, pair) for at in range(planes) for pair in range(pairs)]
    parts = []
    residuals = {}
    hiddens = {}

    def first(unit):
        at, pair = unit
        here = slice(at * plane, (at + 1) * plane)
        return score(
            pair_store[pair, at * plane : at * plane + reach_keys],
            block_diagonal(queries[:, here], pair * 2 * head_dim, head_dim, group, block_out),
            table[pair],
        )

    def third(unit, weights):
        at, pair = unit
        values = pair_values[pair][:, at * plane : at * plane + reach_keys]
        parts.append(blend(values, weights, head_dim))

    def mix(at):
        mixed = jnp.concatenate(parts[at * pairs : (at + 1) * pairs], axis=0)
        here = slice(at * plane, (at + 1) * plane)
        residuals[at] = stream[here] + mm(mixed, out_weight[...], TN)

    def expand(at):
        hidden = mm(rms(residuals[at], gain_third[...]), mlp_up[...])
        hiddens[at] = jax.nn.gelu(hidden, approximate=True).astype(jnp.bfloat16)

    def finish(at):
        here = slice(at * plane, (at + 1) * plane)
        out[here] = (residuals[at] + mm(hiddens[at], mlp_down[...])).astype(out.dtype)

    def after(index):
        at, stage = index // pairs, index % pairs
        if stage == pairs - 1:
            mix(at)
        if at and stage == 0:
            expand(at - 1)
        if at and stage == 1:
            finish(at - 1)

    run_pipeline(units, first, lambda held: soften(*held), third, after)
    expand(planes - 1)
    finish(planes - 1)


VMEM = pl.BlockSpec(memory_space=pltpu.VMEM)
SMEM = pl.BlockSpec(memory_space=pltpu.SMEM)
ANY = pl.BlockSpec(memory_space=pl.ANY)
HBM = pl.BlockSpec(memory_space=pltpu.HBM)


def call(kernel, specs, shapes, args, limit, scratch=(), flops=0, bytes_accessed=0):
    return pl.pallas_call(
        kernel,
        in_specs=specs,
        out_specs=[VMEM] * len(shapes),
        out_shape=[jax.ShapeDtypeStruct(shape, dtype) for shape, dtype in shapes],
        scratch_shapes=list(scratch),
        compiler_params=pltpu.CompilerParams(vmem_limit_bytes=limit * MIB),
        cost_estimate=pl.CostEstimate(
            flops=flops, bytes_accessed=bytes_accessed, transcendentals=0
        ),
    )(*args)


def local(
    volume,
    gain_first,
    phase_qkv,
    phase_out,
    bin_phase,
    phase_bias,
    gain_second,
    window_qkv,
    window_out,
    window_corner,
    window_bias,
    gain_third,
    mlp_up,
    mlp_down,
):
    planes, extent_x, extent_y, width = volume.shape[1:]
    plane = extent_x * extent_y
    tokens = planes * plane
    heads = window_corner.shape[0]
    bins = lax.axis_size("phase")
    half = bins // 2
    chunk = tokens // bins
    tile = ROWS * bins
    me = lax.axis_index("phase")
    bf16, f32 = jnp.bfloat16, jnp.float32

    def swap(block, mask):
        return lax.ppermute(block, "phase", [(i, i ^ mask) for i in range(bins)])

    own = volume.reshape(tokens, width)
    twin = swap(own, 1)

    def piece(mask):
        start = (me ^ mask) * chunk
        return jnp.stack(
            [lax.dynamic_slice_in_dim(source, start, chunk, axis=0) for source in (own, twin)]
        )

    pieces = [piece(2 * step) for step in range(half)]
    blocks = pieces[:1] + [swap(pieces[step], 2 * step) for step in range(1, half)]
    corner = window_corner.T

    phase_weights, phase_table, window_table = call(
        functools.partial(prep_kernel, bins, extent_x, extent_y),
        [HBM] * 5 + [ANY],
        [
            ((3 * width, width), bf16),
            ((heads // 2, tile, 2 * tile), f32),
            ((heads // 2, SPAN * plane, 2 * plane), f32),
        ],
        [
            *(
                pltpu.with_memory_space_constraint(array, pltpu.HBM)
                for array in (bin_phase, corner, window_bias, phase_bias, phase_qkv)
            ),
            pieces[-1],
        ],
        12,
        scratch=[
            pltpu.SMEM(bin_phase.shape, jnp.int32),
            pltpu.SMEM(corner.shape, jnp.int32),
            pltpu.SMEM(window_bias.shape, f32),
            pltpu.VMEM(phase_bias.shape, f32),
            pltpu.VMEM(phase_qkv.shape, bf16),
            pltpu.SemaphoreType.DMA((5,)),
        ],
        flops=2 * 10**9,
        bytes_accessed=4 * 2**20,
    )
    results = call(
        functools.partial(phase_kernel, bins, heads),
        [VMEM] * (half + 4),
        [((2, chunk, width), bf16)] * half,
        [*blocks, gain_first.reshape(1, width), phase_weights, phase_table, phase_out],
        12,
        flops=2 * tokens * width * 5 * width,
        bytes_accessed=2**20,
    )
    got = [results[0]] + [swap(results[step], 2 * step) for step in range(1, half)]
    twins = [swap(block, 1) for block in got]
    reach = REACH * plane
    ext = tokens + 2 * reach
    residual, inner, outer = call(
        functools.partial(gather_kernel, plane, half),
        [VMEM] * (2 * half),
        [((tokens, width), bf16), ((reach, width), bf16), ((reach, width), bf16)],
        [*got, *twins],
        4,
    )
    count = lax.axis_size("space")
    even = [(i, i ^ 1) for i in range(count) if i ^ 1 < count]
    odd = [(i, ((i + 1) ^ 1) - 1) for i in range(count) if 0 <= ((i + 1) ^ 1) - 1 < count]
    inner = lax.ppermute(inner, "space", even)
    outer = lax.ppermute(outer, "space", odd)
    (out,) = call(
        functools.partial(window_kernel, plane),
        [SMEM] + [VMEM] * 10,
        [((tokens, width), bf16)],
        [
            corner,
            residual,
            inner,
            outer,
            gain_second.reshape(1, width),
            window_qkv,
            window_table,
            window_out,
            gain_third.reshape(1, width),
            mlp_up,
            mlp_down,
        ],
        24,
        scratch=[
            pltpu.VMEM((ext, width), bf16),
            pltpu.VMEM((width, ext), bf16),
            pltpu.VMEM((heads // 2, (planes + REACH) * plane, 128), bf16),
        ],
        flops=2 * tokens * width * 14 * width,
        bytes_accessed=2**22,
    )
    return out.reshape(volume.shape)


def solution(mesh):
    split = P("phase", "space", None, None, None)
    in_specs = (split,) + (P(),) * 13
    return jax.shard_map(local, mesh=mesh, in_specs=in_specs, out_specs=split, check_vma=False)
```

time: 52 us -> 37.5 us (0.72)
  the two profiles are of different devices: /device:TPU:0 before, /device:TPU:16 now
where the time goes in v1:
time: 37.5 us; the launch traced here: 37.3 us
  waiting for transfers between devices  14.1 us (38%)
  Pallas kernels  11.3 us (30%)
  starting transfers between devices  10.8 us (29%)
  local copies, waits for them, and re-layouts  0.87 us (2%)
    pallas_call x4, Pallas kernels, call(): pl.pallas_call(kernel, in_specs=specs, out_specs=[VMEM] * len(shapes), ou...  11.3 us
    ppermute x11, waiting for transfers between devices, swap(): return lax.ppermute(block, 'phase', [(i, i ^ mask) for i in range(bins)])  7.46 us
    ppermute x11, starting transfers between devices, swap(): return lax.ppermute(block, 'phase', [(i, i ^ mask) for i in range(bins)])  7.24 us
    ppermute x1, waiting for transfers between devices, local(): inner = lax.ppermute(inner, 'space', even)  3.47 us
    ppermute x1, waiting for transfers between devices, local(): outer = lax.ppermute(outer, 'space', odd)  3.18 us
    ppermute x1, starting transfers between devices, local(): outer = lax.ppermute(outer, 'space', odd)  1.91 us
    ppermute x1, starting transfers between devices, local(): inner = lax.ppermute(inner, 'space', even)  1.64 us
    another operation x2, local copies, waits for them, and re-layouts, piece(): jnp.stack([lax.dynamic_slice_in_dim(source, start, chunk, axis=0) for sou...  0.83 us
  transfers between devices with their start and end apart: 13, of which 9 were waited for; matrix products, arithmetic and copies ran while one was open for 2% of the time, Pallas kernels for 5%

profile of v1, /device:TPU:16, one launch (start us, length us, event | category | flops | bytes accessed | tf_op | source)
XLA Modules:
  0.0 37.3 jit_solution(13123586101183495198)
XLA Ops:
  0.0 0.0 collective-permute-start
  0.0 0.8 %dynamic-slice_bitcast_fusion.1 = (bf16[1,64,256]{2,1,0:T(8,128)(2,1)S(1)}, bf16[1,64,256]{2,1,0:T(8,128)(2,1)S(1)}, bf16[1,64,256]{2,1,0:T(8,128)(2,1)S(1)}, bf16[1,64,256]{2,1,0:T(8,128)(2,1)S(1)}) fusion(bf16[512,256]{1,0:T(8,128)(2,1)} %bitcast.28, s32[]{:T(128)S(6)} %select_n.19, s32[]{:T(128)S(6)} %select_n.18, s32[]{:T(128)S(6)} %select_n.17, ...), kind=kLoop, calls=%fused_computation.5 | loop fusion | bytes 262160 | tf_op jit(solution)/shard_map/stack | solution.py:453
  0.8 0.9 %collective-permute-done = bf16[512,256]{1,0:T(8,128)(2,1)S(1)} collective-permute-done((bf16[512,256]{1,0:T(8,128)(2,1)}, bf16[512,256]{1,0:T(8,128)(2,1)S(1)}, u32[]{:S(2)}, u32[]{:S(2)}) %collective-permute-start) | collective-permute-done | bytes 262176 | tf_op jit(solution)/shard_map/ppermute | solution.py:446
  1.8 1.6 %collective-permute-start.1 = (bf16[2,64,256]{2,1,0:T(8,128)(2,1)S(1)}, bf16[2,64,256]{2,1,0:T(8,128)(2,1)S(1)}, u32[]{:S(2)}, u32[]{:S(2)}) collective-permute-start(bf16[2,64,256]{2,1,0:T(8,128)(2,1)S(1)} %pad_maximum_fusion.1), channel_id=1, source_target_pairs={{0,8},{4,12},{8,0},{12,4},{16,24},{20,28},{24,16},{28,20},{1,9},{5... | collective-permute-start | bytes 196616 | tf_op jit(solution)/shard_map/ppermute | solution.py:446
  3.3 1.6 %collective-permute-start.2 = (bf16[2,64,256]{2,1,0:T(8,128)(2,1)S(1)}, bf16[2,64,256]{2,1,0:T(8,128)(2,1)S(1)}, u32[]{:S(2)}, u32[]{:S(2)}) collective-permute-start(bf16[2,64,256]{2,1,0:T(8,128)(2,1)S(1)} %pad_maximum_fusion.2), channel_id=1, source_target_pairs={{0,16},{4,20},{8,24},{12,28},{16,0},{20,4},{24,8},{28,12},{1,17},{... | collective-permute-start | bytes 196616 | tf_op jit(solution)/shard_map/ppermute | solution.py:446
  4.9 0.5 %collective-permute-start.3 = (bf16[2,64,256]{2,1,0:T(8,128)(2,1)S(1)}, bf16[2,64,256]{2,1,0:T(8,128)(2,1)S(1)}, u32[]{:S(2)}, u32[]{:S(2)}) collective-permute-start(bf16[2,64,256]{2,1,0:T(8,128)(2,1)S(1)} %pad_maximum_fusion.3._), channel_id=1, source_target_pairs={{0,24},{4,28},{8,16},{12,20},{16,8},{20,12},{24,0},{28,4},{1,25},{... | collective-permute-start | bytes 196616 | tf_op jit(solution)/shard_map/ppermute | solution.py:446
  5.5 0.0 copy-start.3
  5.5 0.0 copy-start.6
  5.5 0.0 copy-start.4
  5.5 0.0 copy-start.5
  5.5 0.0 copy-start.7
  5.5 0.0 copy-start.8
  5.5 2.0 %shard_map.136 = (bf16[768,256]{1,0:T(8,128)(2,1)S(1)}, f32[4,128,256]{2,1,0:T(8,128)S(1)}, f32[4,512,256]{2,1,0:T(8,128)S(1)}) custom-call(s32[8]{0:T(128)} %bin_phase_at.1, s32[3,8]{1,0:T(4,128)} %bitcast.22, f32[8,64]{1,0:T(8,128)} %window_bias_at.1, f32[8,8]{1,0:T(8,128)} %phase_bias_at.1, bf16[256,768]{1,0:T(8,128)(2,1)} %phase_qkv_at.1, ...), custom_call_target="tpu_custom_call" | custom-call | flops 2000000000 | bytes 4194304 | tf_op jit(solution)/shard_map/pallas_call | solution.py:405
  7.5 0.0 copy-start
  7.5 0.0 copy-start.1
  7.5 0.0 copy-start.2
  7.6 0.0 collective-permute-done.1.refs_1_
  7.6 0.1 collective-permute-done.2.refs_2_
  7.7 2.5 %collective-permute-done.3.refs_3_ = bf16[2,64,256]{2,1,0:T(8,128)(2,1)S(1)} collective-permute-done((bf16[2,64,256]{2,1,0:T(8,128)(2,1)S(1)}, bf16[2,64,256]{2,1,0:T(8,128)(2,1)S(1)}, u32[]{:S(2)}, u32[]{:S(2)}) %collective-permute-start.3) | collective-permute-done | bytes 65568 | tf_op jit(solution)/shard_map/ppermute | solution.py:446
  10.2 0.0 copy-done.3
  10.2 0.0 copy-done.6
  10.2 2.2 %shard_map.137 = (bf16[2,64,256]{2,1,0:T(8,128)(2,1)S(1)}, bf16[2,64,256]{2,1,0:T(8,128)(2,1)S(1)}, bf16[2,64,256]{2,1,0:T(8,128)(2,1)S(1)}, bf16[2,64,256]{2,1,0:T(8,128)(2,1)S(1)}) custom-call(bf16[2,64,256]{2,1,0:T(8,128)(2,1)S(1)} %pad_maximum_fusion.refs_0_, bf16[2,64,256]{2,1,0:T(8,128)(2,1)S(1)} %collective-permute-done.1.refs_1_, ...), custom_call_target="tpu_custom_call" | custom-call | flops 335544320 | bytes 1048576 | tf_op jit(solution)/shard_map/pallas_call | solution.py:405
  12.4 0.6 %collective-permute-start.4 = (bf16[2,64,256]{2,1,0:T(8,128)(2,1)S(1)}, bf16[2,64,256]{2,1,0:T(8,128)(2,1)S(1)}, u32[]{:S(2)}, u32[]{:S(2)}) collective-permute-start(bf16[2,64,256]{2,1,0:T(8,128)(2,1)S(1)} %get-tuple-element.18), channel_id=1, source_target_pairs={{0,8},{4,12},{8,0},{12,4},{16,24},{20,28},{24,16},{28,20},{1,9},{5... | collective-permute-start | bytes 196616 | tf_op jit(solution)/shard_map/ppermute | solution.py:446
  13.0 0.5 %collective-permute-start.5 = (bf16[2,64,256]{2,1,0:T(8,128)(2,1)S(1)}, bf16[2,64,256]{2,1,0:T(8,128)(2,1)S(1)}, u32[]{:S(2)}, u32[]{:S(2)}) collective-permute-start(bf16[2,64,256]{2,1,0:T(8,128)(2,1)S(1)} %get-tuple-element.19), channel_id=1, source_target_pairs={{0,16},{4,20},{8,24},{12,28},{16,0},{20,4},{24,8},{28,12},{1,17},{... | collective-permute-start | bytes 196616 | tf_op jit(solution)/shard_map/ppermute | solution.py:446
  13.5 2.5 %collective-permute-start.6 = (bf16[2,64,256]{2,1,0:T(8,128)(2,1)S(1)}, bf16[2,64,256]{2,1,0:T(8,128)(2,1)S(1)}, u32[]{:S(2)}, u32[]{:S(2)}) collective-permute-start(bf16[2,64,256]{2,1,0:T(8,128)(2,1)S(1)} %get-tuple-element.20), channel_id=1, source_target_pairs={{0,24},{4,28},{8,16},{12,20},{16,8},{20,12},{24,0},{28,4},{1,25},{... | collective-permute-start | bytes 196616 | tf_op jit(solution)/shard_map/ppermute | solution.py:446
  15.9 0.0 collective-permute-start.7
  15.9 0.8 %collective-permute-done.4.refs_1_ = bf16[2,64,256]{2,1,0:T(8,128)(2,1)S(1)} collective-permute-done((bf16[2,64,256]{2,1,0:T(8,128)(2,1)S(1)}, bf16[2,64,256]{2,1,0:T(8,128)(2,1)S(1)}, u32[]{:S(2)}, u32[]{:S(2)}) %collective-permute-start.4) | collective-permute-done | bytes 65568 | tf_op jit(solution)/shard_map/ppermute | solution.py:446
  16.7 0.0 collective-permute-start.8
  16.7 0.5 %collective-permute-done.5.refs_2_ = bf16[2,64,256]{2,1,0:T(8,128)(2,1)S(1)} collective-permute-done((bf16[2,64,256]{2,1,0:T(8,128)(2,1)S(1)}, bf16[2,64,256]{2,1,0:T(8,128)(2,1)S(1)}, u32[]{:S(2)}, u32[]{:S(2)}) %collective-permute-start.5) | collective-permute-done | bytes 65568 | tf_op jit(solution)/shard_map/ppermute | solution.py:446
  17.2 0.0 collective-permute-start.9
  17.2 1.4 %collective-permute-done.6.refs_3_ = bf16[2,64,256]{2,1,0:T(8,128)(2,1)S(1)} collective-permute-done((bf16[2,64,256]{2,1,0:T(8,128)(2,1)S(1)}, bf16[2,64,256]{2,1,0:T(8,128)(2,1)S(1)}, u32[]{:S(2)}, u32[]{:S(2)}) %collective-permute-start.6) | collective-permute-done | bytes 65568 | tf_op jit(solution)/shard_map/ppermute | solution.py:446
  18.6 0.0 collective-permute-start.10
  18.6 0.0 collective-permute-done.7.refs_4_
  18.6 0.0 collective-permute-done.8.refs_5_
  18.6 0.0 collective-permute-done.9.refs_6_
  18.6 1.2 %collective-permute-done.10.refs_7_ = bf16[2,64,256]{2,1,0:T(8,128)(2,1)S(1)} collective-permute-done((bf16[2,64,256]{2,1,0:T(8,128)(2,1)S(1)}, bf16[2,64,256]{2,1,0:T(8,128)(2,1)S(1)}, u32[]{:S(2)}, u32[]{:S(2)}) %collective-permute-start.10) | collective-permute-done | bytes 65568 | tf_op jit(solution)/shard_map/ppermute | solution.py:446
  19.9 0.1 shard_map.138
  19.9 1.6 %collective-permute-start.11 = (bf16[384,256]{1,0:T(8,128)(2,1)S(1)}, bf16[384,256]{1,0:T(8,128)(2,1)S(1)}, u32[]{:S(2)}, u32[]{:S(2)}) collective-permute-start(bf16[384,256]{1,0:T(8,128)(2,1)S(1)} %get-tuple-element.22), channel_id=1, source_target_pairs={{0,1},{1,0},{2,3},{3,2},{4,5},{5,4},{6,7},{7,6},{8,9},{9,8},{10,11... | collective-permute-start | bytes 589832 | tf_op jit(solution)/shard_map/ppermute | solution.py:511
  21.6 1.9 %collective-permute-start.12 = (bf16[384,256]{1,0:T(8,128)(2,1)S(1)}, bf16[384,256]{1,0:T(8,128)(2,1)S(1)}, u32[]{:S(2)}, u32[]{:S(2)}) collective-permute-start(bf16[384,256]{1,0:T(8,128)(2,1)S(1)} %get-tuple-element.23), channel_id=1, source_target_pairs={{1,2},{2,1},{5,6},{6,5},{9,10},{10,9},{13,14},{14,13},{17,18},{18,... | collective-permute-start | bytes 589832 | tf_op jit(solution)/shard_map/ppermute | solution.py:512
  23.5 3.5 %collective-permute-done.11.inner = bf16[384,256]{1,0:T(8,128)(2,1)S(1)} collective-permute-done((bf16[384,256]{1,0:T(8,128)(2,1)S(1)}, bf16[384,256]{1,0:T(8,128)(2,1)S(1)}, u32[]{:S(2)}, u32[]{:S(2)}) %collective-permute-start.11) | collective-permute-done | bytes 196640 | tf_op jit(solution)/shard_map/ppermute | solution.py:511
  27.0 3.2 %collective-permute-done.12.outer = bf16[384,256]{1,0:T(8,128)(2,1)S(1)} collective-permute-done((bf16[384,256]{1,0:T(8,128)(2,1)S(1)}, bf16[384,256]{1,0:T(8,128)(2,1)S(1)}, u32[]{:S(2)}, u32[]{:S(2)}) %collective-permute-start.12) | collective-permute-done | bytes 196640 | tf_op jit(solution)/shard_map/ppermute | solution.py:512
  30.1 0.0 copy-done.4
  30.2 0.0 copy-done.5
  30.2 0.0 copy-done.7
  30.2 0.0 copy-done.8
  30.2 0.0 copy-done
  30.2 0.0 copy-done.1
  30.2 0.0 copy-done.2
  30.2 7.1 %shard_map.139 = bf16[512,256]{1,0:T(8,128)(2,1)} custom-call(s32[3,8]{1,0:T(4,128)S(1)} %bitcast.23, bf16[512,256]{1,0:T(8,128)(2,1)S(1)} %get-tuple-element.21.own, bf16[384,256]{1,0:T(8,128)(2,1)S(1)} %collective-permute-done.11.inner, bf16[384,256]{1,0:T(8,128)(2,1)S(1)} %collective-permute-done.12.outer, f32[1,256]{1,0:T(1,128)S(1)} %bitcast.25, ...), custom_call_target="tpu_custom_call" | custom-call | flops 939524096 | bytes 4194304 | tf_op jit(solution)/shard_map/pallas_call | solution.py:405
  (5 shorter events, 0.0 us)
Async XLA Ops:
  0.0 1.7 %collective-permute-start = (bf16[512,256]{1,0:T(8,128)(2,1)}, bf16[512,256]{1,0:T(8,128)(2,1)S(1)}, u32[]{:S(2)}, u32[]{:S(2)}) collective-permute-start(bf16[512,256]{1,0:T(8,128)(2,1)} %bitcast.27), channel_id=1, source_target_pairs={{0,4},{4,0},{8,12},{12,8},{16,20},{20,16},{24,28},{28,24},{1,5},{5... | collective-permute-start | bytes 786440 | tf_op jit(solution)/shard_map/ppermute | solution.py:446
  1.8 5.8 %collective-permute-start.1 = (bf16[2,64,256]{2,1,0:T(8,128)(2,1)S(1)}, bf16[2,64,256]{2,1,0:T(8,128)(2,1)S(1)}, u32[]{:S(2)}, u32[]{:S(2)}) collective-permute-start(bf16[2,64,256]{2,1,0:T(8,128)(2,1)S(1)} %pad_maximum_fusion.1), channel_id=1, source_target_pairs={{0,8},{4,12},{8,0},{12,4},{16,24},{20,28},{24,16},{28,20},{1,9},{5... | collective-permute-start | bytes 196616 | tf_op jit(solution)/shard_map/ppermute | solution.py:446
  3.3 4.3 %collective-permute-start.2 = (bf16[2,64,256]{2,1,0:T(8,128)(2,1)S(1)}, bf16[2,64,256]{2,1,0:T(8,128)(2,1)S(1)}, u32[]{:S(2)}, u32[]{:S(2)}) collective-permute-start(bf16[2,64,256]{2,1,0:T(8,128)(2,1)S(1)} %pad_maximum_fusion.2), channel_id=1, source_target_pairs={{0,16},{4,20},{8,24},{12,28},{16,0},{20,4},{24,8},{28,12},{1,17},{... | collective-permute-start | bytes 196616 | tf_op jit(solution)/shard_map/ppermute | solution.py:446
  4.9 5.2 %collective-permute-start.3 = (bf16[2,64,256]{2,1,0:T(8,128)(2,1)S(1)}, bf16[2,64,256]{2,1,0:T(8,128)(2,1)S(1)}, u32[]{:S(2)}, u32[]{:S(2)}) collective-permute-start(bf16[2,64,256]{2,1,0:T(8,128)(2,1)S(1)} %pad_maximum_fusion.3._), channel_id=1, source_target_pairs={{0,24},{4,28},{8,16},{12,20},{16,8},{20,12},{24,0},{28,4},{1,25},{... | collective-permute-start | bytes 196616 | tf_op jit(solution)/shard_map/ppermute | solution.py:446
  5.5 4.7 %copy-start.3 = (bf16[256,256]{1,0:T(8,128)(2,1)S(1)}, bf16[256,256]{1,0:T(8,128)(2,1)}, u32[]{:S(2)}) copy-start(bf16[256,256]{1,0:T(8,128)(2,1)} %refs_7_.1) | copy-start | bytes 393220
  5.5 4.7 %copy-start.6 = (f32[256]{0:T(256)S(1)}, f32[256]{0:T(256)}, u32[]{:S(2)}) copy-start(f32[256]{0:T(256)} %param.15) | copy-start | bytes 3076
  5.5 24.7 %copy-start.4 = (bf16[256,256]{1,0:T(8,128)(2,1)S(1)}, bf16[256,256]{1,0:T(8,128)(2,1)}, u32[]{:S(2)}) copy-start(bf16[256,256]{1,0:T(8,128)(2,1)} %out_weight.1) | copy-start | bytes 393220
  5.5 24.7 %copy-start.5 = (s32[8,3]{0,1:T(4,128)S(1)}, s32[8,3]{0,1:T(4,128)}, u32[]{:S(2)}) copy-start(s32[8,3]{0,1:T(4,128)} %param.23) | copy-start | bytes 292
  5.5 24.7 %copy-start.7 = (f32[256]{0:T(256)S(1)}, f32[256]{0:T(256)}, u32[]{:S(2)}) copy-start(f32[256]{0:T(256)} %param.20) | copy-start | bytes 3076
  5.5 24.7 %copy-start.8 = (f32[256]{0:T(256)S(1)}, f32[256]{0:T(256)}, u32[]{:S(2)}) copy-start(f32[256]{0:T(256)} %param.25) | copy-start | bytes 3076
  7.5 22.7 %copy-start = (bf16[256,1024]{1,0:T(8,128)(2,1)S(1)}, bf16[256,1024]{1,0:T(8,128)(2,1)}, u32[]{:S(2)}) copy-start(bf16[256,1024]{1,0:T(8,128)(2,1)} %mlp_up.1) | copy-start | bytes 1572868
  7.5 22.7 %copy-start.1 = (bf16[1024,256]{1,0:T(8,128)(2,1)S(1)}, bf16[1024,256]{1,0:T(8,128)(2,1)}, u32[]{:S(2)}) copy-start(bf16[1024,256]{1,0:T(8,128)(2,1)} %mlp_down.1) | copy-start | bytes 1572868
  7.5 22.7 %copy-start.2 = (bf16[256,768]{1,0:T(8,128)(2,1)S(1)}, bf16[256,768]{1,0:T(8,128)(2,1)}, u32[]{:S(2)}) copy-start(bf16[256,768]{1,0:T(8,128)(2,1)} %qkv.1) | copy-start | bytes 1179652
  12.4 4.3 %collective-permute-start.4 = (bf16[2,64,256]{2,1,0:T(8,128)(2,1)S(1)}, bf16[2,64,256]{2,1,0:T(8,128)(2,1)S(1)}, u32[]{:S(2)}, u32[]{:S(2)}) collective-permute-start(bf16[2,64,256]{2,1,0:T(8,128)(2,1)S(1)} %get-tuple-element.18), channel_id=1, source_target_pairs={{0,8},{4,12},{8,0},{12,4},{16,24},{20,28},{24,16},{28,20},{1,9},{5... | collective-permute-start | bytes 196616 | tf_op jit(solution)/shard_map/ppermute | solution.py:446
  13.0 4.3 %collective-permute-start.5 = (bf16[2,64,256]{2,1,0:T(8,128)(2,1)S(1)}, bf16[2,64,256]{2,1,0:T(8,128)(2,1)S(1)}, u32[]{:S(2)}, u32[]{:S(2)}) collective-permute-start(bf16[2,64,256]{2,1,0:T(8,128)(2,1)S(1)} %get-tuple-element.19), channel_id=1, source_target_pairs={{0,16},{4,20},{8,24},{12,28},{16,0},{20,4},{24,8},{28,12},{1,17},{... | collective-permute-start | bytes 196616 | tf_op jit(solution)/shard_map/ppermute | solution.py:446
  13.5 5.2 %collective-permute-start.6 = (bf16[2,64,256]{2,1,0:T(8,128)(2,1)S(1)}, bf16[2,64,256]{2,1,0:T(8,128)(2,1)S(1)}, u32[]{:S(2)}, u32[]{:S(2)}) collective-permute-start(bf16[2,64,256]{2,1,0:T(8,128)(2,1)S(1)} %get-tuple-element.20), channel_id=1, source_target_pairs={{0,24},{4,28},{8,16},{12,20},{16,8},{20,12},{24,0},{28,4},{1,25},{... | collective-permute-start | bytes 196616 | tf_op jit(solution)/shard_map/ppermute | solution.py:446
  15.9 2.7 %collective-permute-start.7 = (bf16[2,64,256]{2,1,0:T(8,128)(2,1)S(1)}, bf16[2,64,256]{2,1,0:T(8,128)(2,1)S(1)}, u32[]{:S(2)}, u32[]{:S(2)}) collective-permute-start(bf16[2,64,256]{2,1,0:T(8,128)(2,1)S(1)} %get-tuple-element.17.refs_0_), channel_id=1, source_target_pairs={{0,4},{4,0},{8,12},{12,8},{16,20},{20,16},{24,28},{28,24},{1,5},{5... | collective-permute-start | bytes 196616 | tf_op jit(solution)/shard_map/ppermute | solution.py:446
  16.7 1.9 %collective-permute-start.8 = (bf16[2,64,256]{2,1,0:T(8,128)(2,1)S(1)}, bf16[2,64,256]{2,1,0:T(8,128)(2,1)S(1)}, u32[]{:S(2)}, u32[]{:S(2)}) collective-permute-start(bf16[2,64,256]{2,1,0:T(8,128)(2,1)S(1)} %collective-permute-done.4.refs_1_), channel_id=1, source_target_pairs={{0,4},{4,0},{8,12},{12,8},{16,20},{20,16},{24,28},{28,24},{1,5},{5... | collective-permute-start | bytes 196616 | tf_op jit(solution)/shard_map/ppermute | solution.py:446
  17.2 1.4 %collective-permute-start.9 = (bf16[2,64,256]{2,1,0:T(8,128)(2,1)S(1)}, bf16[2,64,256]{2,1,0:T(8,128)(2,1)S(1)}, u32[]{:S(2)}, u32[]{:S(2)}) collective-permute-start(bf16[2,64,256]{2,1,0:T(8,128)(2,1)S(1)} %collective-permute-done.5.refs_2_), channel_id=1, source_target_pairs={{0,4},{4,0},{8,12},{12,8},{16,20},{20,16},{24,28},{28,24},{1,5},{5... | collective-permute-start | bytes 196616 | tf_op jit(solution)/shard_map/ppermute | solution.py:446
  18.6 1.3 %collective-permute-start.10 = (bf16[2,64,256]{2,1,0:T(8,128)(2,1)S(1)}, bf16[2,64,256]{2,1,0:T(8,128)(2,1)S(1)}, u32[]{:S(2)}, u32[]{:S(2)}) collective-permute-start(bf16[2,64,256]{2,1,0:T(8,128)(2,1)S(1)} %collective-permute-done.6.refs_3_), channel_id=1, source_target_pairs={{0,4},{4,0},{8,12},{12,8},{16,20},{20,16},{24,28},{28,24},{1,5},{5... | collective-permute-start | bytes 196616 | tf_op jit(solution)/shard_map/ppermute | solution.py:446
  19.9 7.0 %collective-permute-start.11 = (bf16[384,256]{1,0:T(8,128)(2,1)S(1)}, bf16[384,256]{1,0:T(8,128)(2,1)S(1)}, u32[]{:S(2)}, u32[]{:S(2)}) collective-permute-start(bf16[384,256]{1,0:T(8,128)(2,1)S(1)} %get-tuple-element.22), channel_id=1, source_target_pairs={{0,1},{1,0},{2,3},{3,2},{4,5},{5,4},{6,7},{7,6},{8,9},{9,8},{10,11... | collective-permute-start | bytes 589832 | tf_op jit(solution)/shard_map/ppermute | solution.py:511
  21.6 8.6 %collective-permute-start.12 = (bf16[384,256]{1,0:T(8,128)(2,1)S(1)}, bf16[384,256]{1,0:T(8,128)(2,1)S(1)}, u32[]{:S(2)}, u32[]{:S(2)}) collective-permute-start(bf16[384,256]{1,0:T(8,128)(2,1)S(1)} %get-tuple-element.23), channel_id=1, source_target_pairs={{1,2},{2,1},{5,6},{6,5},{9,10},{10,9},{13,14},{14,13},{17,18},{18,... | collective-permute-start | bytes 589832 | tf_op jit(solution)/shard_map/ppermute | solution.py:512

commit v2 on v1

--- a/solution.py
+++ b/solution.py
@@ -15,6 +15,8 @@
 REACH = SPAN - 1
 ROWS = 16
 MIB = 2**20
+GELU_LINEAR = math.sqrt(2.0 / math.pi)
+GELU_CUBIC = 0.044715 * GELU_LINEAR
 
 NT = (((1,), (1,)), ((), ()))
 TN = (((0,), (0,)), ((), ()))
@@ -94,6 +96,9 @@
                 (head % 2) * tile : (head % 2 + 1) * tile,
             ] = jnp.where(same, value[head : head + 1], NEG)
     plane = extent_x * extent_y
+    window_table[:, SPAN * plane :] = jnp.full(
+        (heads // 2, plane, 2 * plane), NEG, window_table.dtype
+    )
     shape = (extent_y, plane)
     lane = lax.broadcasted_iota(jnp.int32, shape, 1)
     lane_x = lane // extent_y
@@ -124,18 +129,29 @@
                 ] = block
 
 
-def score(keys, queries, table):
-    scores = mm(keys, queries) + table
-    return scores, jnp.max(scores, axis=0, keepdims=True)
-
-
-def soften(scores, top):
-    return jnp.exp2(scores - top).astype(jnp.bfloat16)
-
-
-def blend(values, weights, head_dim):
-    count = weights.shape[1] // 2
-    mixed = mm(values, weights)
+def score_steps(keys, queries, tiles, store):
+    pieces = []
+    tops = []
+    for start, stop, table in tiles:
+        piece = mm(keys[start:stop], queries) + table
+        pieces.append(piece)
+        tops.append(jnp.max(piece.reshape(-1, 8, piece.shape[1]), axis=0))
+        yield
+    top = functools.reduce(jnp.maximum, tops)
+    store["pieces"] = pieces
+    store["top"] = jnp.max(top, axis=0, keepdims=True)
+
+
+def soften_steps(store):
+    weights = []
+    for piece in store.pop("pieces"):
+        weights.append(jnp.exp2((piece - store["top"]).astype(jnp.bfloat16)))
+        yield
+    store["weights"] = jnp.concatenate(weights, axis=0) if len(weights) > 1 else weights[0]
+
+
+def blend(mixed, head_dim):
+    count = mixed.shape[1] // 2
     inverse = 1.0 / mixed[2 * head_dim : 2 * head_dim + 1]
     return jnp.concatenate(
         [
@@ -146,22 +162,37 @@
     ).astype(jnp.bfloat16)
 
 
-def run_pipeline(units, first, second, third, after):
-    held = first(units[0])
-    weights = None
-    for index, unit in enumerate(units):
-        following = first(units[index + 1]) if index + 1 < len(units) else None
-        now = second(held)
-        if index:
-            third(units[index - 1], weights)
-            after(index - 1)
-        weights = now
-        held = following
-    third(units[-1], weights)
-    after(len(units) - 1)
-
-
-def block_diagonal(queries, base, head_dim, group, extra=None):
+def interleave(*steps):
+    running = list(steps)
+    while running:
+        for step in list(running):
+            try:
+                next(step)
+            except StopIteration:
+                running.remove(step)
+
+
+def run_pipeline(units, size, first, second, third, side):
+    groups = [units[start : start + size] for start in range(0, len(units), size)]
+    stores = {unit: {} for unit in units}
+
+    def steps(action, index):
+        if not 0 <= index < len(groups):
+            return []
+        return [action(unit, stores[unit]) for unit in groups[index]]
+
+    interleave(*steps(first, 0))
+    for index in range(len(groups)):
+        interleave(
+            *steps(first, index + 1),
+            *steps(second, index),
+            *steps(third, index - 1),
+            side(index),
+        )
+    interleave(*steps(third, len(groups) - 1))
+
+
+def block_diagonal(queries, base, head_dim, group):
     count = queries.shape[1]
     first = base % group
     left = queries[base : base + head_dim]
@@ -170,13 +201,7 @@
     body = jnp.concatenate(
         [jnp.concatenate([left, zero], axis=1), jnp.concatenate([zero, right], axis=1)], axis=0
     )
-    spare = group - 2 * head_dim
-    if extra is None:
-        pad = jnp.zeros((spare, 2 * count), queries.dtype)
-    else:
-        pad = jnp.concatenate(
-            [extra, jnp.zeros((spare - ROWS, 2 * count), queries.dtype)], axis=0
-        )
+    pad = jnp.zeros((group - 2 * head_dim, 2 * count), queries.dtype)
     return jnp.concatenate([body, pad] if first == 0 else [pad, body], axis=0)
 
 
@@ -208,29 +233,28 @@
     units = [(step, pair) for step in range(tiles) for pair in range(pairs)]
     parts = []
 
-    def first(unit):
+    def first(unit, store):
         step, pair = unit
         span = slice(step * tile, (step + 1) * tile)
         base = pair * 2 * head_dim
         frame = base // group * group
-        return score(
+        return score_steps(
             keys[span, frame : frame + group],
             block_diagonal(queries[:, span], base, head_dim, group),
-            table[pair],
+            [(0, tile, table[pair])],
+            store,
         )
 
-    def third(unit, weights):
+    def third(unit, store):
         step, pair = unit
         span = slice(step * tile, (step + 1) * tile)
         base = pair * 2 * head_dim
         stack = jnp.concatenate([values[base : base + 2 * head_dim, span], ones], axis=0)
-        parts.append(blend(stack, weights, head_dim))
-
-    def after(index):
-        if index % pairs != pairs - 1:
-            return
-        step = index // pairs
-        mixed = jnp.concatenate(parts[step * pairs :], axis=0)
+        parts.append(blend(mm(stack, store.pop("weights")), head_dim))
+        yield
+
+    def finish(step):
+        mixed = jnp.concatenate(parts[step * pairs : (step + 1) * pairs], axis=0)
         span = slice(step * tile, (step + 1) * tile)
         result = (stream[span] + mm(mixed, out_weight[...], TN)).astype(jnp.bfloat16)
         for slot in range(bins):
@@ -238,18 +262,34 @@
                 slot * ROWS : (slot + 1) * ROWS
             ]
 
-    run_pipeline(units, first, lambda held: soften(*held), third, after)
+    size = pairs
+
+    def side(index):
+        if index * size >= pairs and index * size % pairs == 0:
+            yield
+            finish(index * size // pairs - 1)
+
+    run_pipeline(units, size, first, lambda _, store: soften_steps(store), third, side)
+    finish(tiles - 1)
+
+
+def pack_kernel(*refs):
+    give = refs[-1]
+    chunk = refs[0].shape[1]
+    for step, source in enumerate(refs[:-1]):
+        give[step * chunk : (step + 1) * chunk] = source[1]
 
 
 def gather_kernel(plane, half, *refs):
-    got, twins = refs[:half], refs[half : 2 * half]
-    residual, inner, outer = refs[2 * half :]
+    got = refs[:half]
+    twin, residual, inner, outer = refs[half:]
     me = lax.axis_index("phase")
     chunk = got[0].shape[1]
     for step in range(half):
-        for part, source in enumerate((got[step], twins[step])):
-            start = pl.multiple_of((me ^ (2 * step + part)) * chunk, ROWS)
-            residual[pl.ds(start, chunk)] = source[part]
+        start = pl.multiple_of((me ^ (2 * step)) * chunk, ROWS)
+        residual[pl.ds(start, chunk)] = got[step][0]
+        start = pl.multiple_of((me ^ (2 * step + 1)) * chunk, ROWS)
+        residual[pl.ds(start, chunk)] = twin[step * chunk : (step + 1) * chunk]
     reach = inner.shape[0]
     extra = residual.shape[0] - reach
     odd = lax.axis_index("space") % 2
@@ -257,7 +297,84 @@
     outer[...] = residual[pl.ds(pl.multiple_of(odd * extra, plane), reach)]
 
 
-def window_kernel(
+def frame_of(keys, pair, head_dim, group):
+    frame = pair * 2 * head_dim // group * group
+    return keys[:, frame : frame + group]
+
+
+def table_tiles(table, corner, pair, at, members, plane, z_first, depth):
+    tiles = []
+    for index, member in enumerate(members):
+        z = z_first + member - REACH
+        halves = []
+        for side in range(2):
+            step = member - REACH - at - corner[0, 2 * pair + side]
+            inside = (step >= 0) & (step < SPAN) & (z >= 0) & (z < depth)
+            start = pl.multiple_of(jnp.where(inside, step, SPAN) * plane, plane)
+            halves.append(table[pair, pl.ds(start, plane), side * plane : (side + 1) * plane])
+        tiles.append((index * plane, (index + 1) * plane, jnp.concatenate(halves, axis=1)))
+    return tiles
+
+
+def inside_kernel(
+    plane, corner, own, gain_second, qkv, table, queries_out, values_out,
+    part_mixed, part_top, part_sum
+):
+    tokens, width = own.shape
+    planes = tokens // plane
+    heads = corner.shape[1]
+    pairs = heads // 2
+    head_dim = width // heads
+    scale = LOG2E / math.sqrt(head_dim)
+    group = 128
+    members = list(range(REACH, REACH + planes))
+    z_first = lax.axis_index("space") * planes
+    depth = lax.axis_size("space") * planes
+    normed = rms(own[...].astype(jnp.float32), gain_second[...])
+    keys = mm(normed, qkv[:, width : 2 * width]).astype(jnp.bfloat16)
+    value_weight = qkv[:, 2 * width :].T
+    values_out[...] = value_weight
+    values = mm(value_weight, normed, NT).astype(jnp.bfloat16)
+    queries = (mm(qkv[:, :width].T, normed, NT) * scale).astype(jnp.bfloat16)
+    queries_out[...] = queries
+    ones = jnp.ones((ROWS, tokens), jnp.bfloat16)
+    frames = [frame_of(keys, pair, head_dim, group) for pair in range(pairs)]
+    stacks = [
+        jnp.concatenate([values[pair * 2 * head_dim : (pair + 1) * 2 * head_dim], ones], axis=0)
+        for pair in range(pairs)
+    ]
+    units = [(at, pair) for at in range(planes) for pair in range(pairs)]
+
+    def first(unit, store):
+        at, pair = unit
+        return score_steps(
+            frames[pair],
+            block_diagonal(
+                queries[:, at * plane : (at + 1) * plane],
+                pair * 2 * head_dim,
+                head_dim,
+                group,
+            ),
+            table_tiles(table, corner, pair, at, members, plane, z_first, depth),
+            store,
+        )
+
+    def third(unit, store):
+        at, pair = unit
+        mixed = mm(stacks[pair], store.pop("weights"))
+        base = pair * 2 * head_dim
+        part_mixed[at, base : base + head_dim] = mixed[:head_dim, :plane]
+        part_mixed[at, base + head_dim : base + 2 * head_dim] = mixed[
+            head_dim : 2 * head_dim, plane:
+        ]
+        part_top[at, pair : pair + 1] = store["top"]
+        part_sum[at, pair : pair + 1] = mixed[2 * head_dim : 2 * head_dim + 1]
+        yield
+
+    run_pipeline(units, 2, first, lambda _, store: soften_steps(store), third, lambda _: iter(()))
+
+
+def outside_kernel(
     plane,
     corner,
     own,
@@ -266,6 +383,11 @@
     gain_second,
     qkv,
     table,
+    queries,
+    value_weight,
+    part_mixed,
+    part_top,
+    part_sum,
     out_weight,
     gain_third,
     mlp_up,
@@ -273,126 +395,107 @@
     out,
     key_store,
     value_store,
-    pair_store,
 ):
     tokens, width = own.shape
     planes = tokens // plane
     heads = corner.shape[1]
     pairs = heads // 2
     head_dim = width // heads
-    scale = LOG2E / math.sqrt(head_dim)
     reach = REACH * plane
     group = 128
     gain = gain_second[...]
     place = lax.axis_index("space")
     is_even = place % 2 == 0
-    stream = own[...].astype(jnp.float32)
-    own_normed = rms(stream, gain)
-    key_weight = qkv[:, width : 2 * width]
-    value_weight = qkv[:, 2 * width :].T
-    query_weight = qkv[:, :width].T
-
-    def project(normed, start, count):
-        key_store[pl.ds(start, count)] = mm(normed, key_weight).astype(jnp.bfloat16)
-        value_store[:, pl.ds(start, count)] = mm(value_weight, normed, NT).astype(jnp.bfloat16)
-
-    project(own_normed, reach, tokens)
-    queries = (mm(query_weight, own_normed, NT) * scale).astype(jnp.bfloat16)
-    for source, at_end in ((inner, is_even), (outer, jnp.logical_not(is_even))):
-        start = pl.multiple_of(jnp.where(at_end, reach + tokens, 0), plane)
-        project(rms(source[...].astype(jnp.float32), gain), start, reach)
     z_first = place * planes
     depth = lax.axis_size("space") * planes
-    span = (planes + REACH) * plane
-    reach_keys = SPAN * plane
-    lane = lax.broadcasted_iota(jnp.int32, (1, group), 1)
-    ones = jnp.ones((ROWS, span), jnp.bfloat16)
-    row = lax.broadcasted_iota(jnp.int32, (ROWS, 2 * plane), 0)
-    lane_head = lax.broadcasted_iota(jnp.int32, (ROWS, 2 * plane), 1) // plane
-    block_out = jnp.where(row == lane_head, NEG, 0.0).astype(jnp.bfloat16)
-    pair_values = []
-    for pair in range(pairs):
-        base = pair * 2 * head_dim
-        frame = base // group * group
-        spare = 2 * head_dim if base == frame else 0
-        first_z = [corner[0, 2 * pair + member] for member in range(2)]
-        start = [pl.multiple_of((z + REACH) * plane, plane) for z in first_z]
-        keep = [
-            (
-                (lane >= base + member * head_dim - frame)
-                & (lane < base + (member + 1) * head_dim - frame)
-            ).astype(jnp.bfloat16)
-            for member in range(2)
-        ]
-        for at in range(planes + REACH):
-            flags = jnp.zeros((1, group), jnp.float32)
-            for member in range(2):
-                z = z_first + at + first_z[member]
-                flag = jnp.where((z >= 0) & (z < depth), 0.0, 1.0)
-                flags = jnp.where(lane == spare + member, flag, flags)
-            rows = [pl.ds(pl.multiple_of(start[m] + at * plane, plane), plane) for m in range(2)]
-            pair_store[pair, at * plane : (at + 1) * plane] = (
-                key_store[rows[0], frame : frame + group] * keep[0]
-                + key_store[rows[1], frame : frame + group] * keep[1]
-                + flags.astype(jnp.bfloat16)
+    key_weight = qkv[:, width : 2 * width]
+    for source, at_end in ((inner, is_even), (outer, jnp.logical_not(is_even))):
+        normed = rms(source[...].astype(jnp.float32), gain)
+        rows = pl.ds(pl.multiple_of(jnp.where(at_end, reach, 0), plane), reach)
+        key_store[rows] = mm(normed, key_weight).astype(jnp.bfloat16)
+        value_store[:, rows] = mm(value_weight[...], normed, NT).astype(jnp.bfloat16)
+    rim = list(range(REACH)) + list(range(REACH + planes, 2 * REACH + planes))
+    ones = jnp.ones((ROWS, 2 * reach), jnp.bfloat16)
+    frames = [frame_of(key_store, pair, head_dim, group) for pair in range(pairs)]
+    stacks = [
+        jnp.concatenate([value_store[pair * 2 * head_dim : (pair + 1) * 2 * head_dim], ones], axis=0)
+        for pair in range(pairs)
+    ]
+    units = [(at, pair) for at in range(planes) for pair in range(pairs)]
+
+    def span(at):
+        return min(at, REACH), REACH + max(0, at + SPAN - planes)
+
+    def first(unit, store):
+        at, pair = unit
+        start, stop = span(at)
+        return score_steps(
+            frames[pair][start * plane : stop * plane],
+            block_diagonal(
+                queries[:, at * plane : (at + 1) * plane],
+                pair * 2 * head_dim,
+                head_dim,
+                group,
+            ),
+            table_tiles(table, corner, pair, at, rim[start:stop], plane, z_first, depth),
+            store,
+        )
+
+    def second(unit, store):
+        at, pair = unit
+        before = part_top[at, pair : pair + 1]
+        store["top"] = jnp.maximum(store["top"], before)
+        store["ratio"] = jnp.exp2(before - store["top"])
+        return soften_steps(store)
+
+    parts = []
+
+    def third(unit, store):
+        at, pair = unit
+        start, stop = span(at)
+        mixed = mm(stacks[pair][:, start * plane : stop * plane], store.pop("weights"))
+        ratio = store["ratio"]
+        total = mixed[2 * head_dim : 2 * head_dim + 1] + ratio * part_sum[at, pair : pair + 1]
+        inverse = 1.0 / total
+        ratio = ratio * inverse
+        halves = []
+        for side in range(2):
+            rows = slice(side * head_dim, (side + 1) * head_dim)
+            lanes = slice(side * plane, (side + 1) * plane)
+            base = (pair * 2 + side) * head_dim
+            halves.append(
+                mixed[rows, lanes] * inverse[:, lanes]
+                + part_mixed[at, base : base + head_dim] * ratio[:, lanes]
             )
-        pair_values.append(
-            jnp.concatenate(
-                [
-                    value_store[
-                        base + member * head_dim : base + (member + 1) * head_dim,
-                        pl.ds(start[member], span),
-                    ]
-                    for member in range(2)
-                ]
-                + [ones],
-                axis=0,
-            )
-        )
-    units = [(at, pair) for at in range(planes) for pair in range(pairs)]
-    parts = []
-    residuals = {}
-    hiddens = {}
-
-    def first(unit):
-        at, pair = unit
-        here = slice(at * plane, (at + 1) * plane)
-        return score(
-            pair_store[pair, at * plane : at * plane + reach_keys],
-            block_diagonal(queries[:, here], pair * 2 * head_dim, head_dim, group, block_out),
-            table[pair],
-        )
-
-    def third(unit, weights):
-        at, pair = unit
-        values = pair_values[pair][:, at * plane : at * plane + reach_keys]
-        parts.append(blend(values, weights, head_dim))
-
-    def mix(at):
-        mixed = jnp.concatenate(parts[at * pairs : (at + 1) * pairs], axis=0)
-        here = slice(at * plane, (at + 1) * plane)
-        residuals[at] = stream[here] + mm(mixed, out_weight[...], TN)
-
-    def expand(at):
-        hidden = mm(rms(residuals[at], gain_third[...]), mlp_up[...])
-        hiddens[at] = jax.nn.gelu(hidden, approximate=True).astype(jnp.bfloat16)
-
-    def finish(at):
-        here = slice(at * plane, (at + 1) * plane)
-        out[here] = (residuals[at] + mm(hiddens[at], mlp_down[...])).astype(out.dtype)
-
-    def after(index):
-        at, stage = index // pairs, index % pairs
-        if stage == pairs - 1:
-            mix(at)
-        if at and stage == 0:
-            expand(at - 1)
-        if at and stage == 1:
-            finish(at - 1)
-
-    run_pipeline(units, first, lambda held: soften(*held), third, after)
-    expand(planes - 1)
-    finish(planes - 1)
+        parts.append(jnp.concatenate(halves, axis=0).astype(jnp.bfloat16))
+        yield
+
+    run_pipeline(units, 2, first, second, third, lambda _: iter(()))
+    mixed = [jnp.concatenate(parts[at * pairs : (at + 1) * pairs], axis=0) for at in range(planes)]
+    columns = width
+    block = 2 * plane
+
+    def mlp_steps(start):
+        here = slice(start * plane, start * plane + block)
+        joined = jnp.concatenate(mixed[start : start + 2], axis=1) if 2 > 1 else mixed[start]
+        residual = own[here].astype(jnp.float32) + mm(joined, out_weight[...], TN)
+        normed = rms(residual, gain_third[...])
+        yield
+        hiddens = []
+        for first_column in range(0, mlp_up.shape[1], columns):
+            hidden = mm(normed, mlp_up[:, first_column : first_column + columns])
+            hiddens.append(gelu(hidden.astype(jnp.bfloat16)))
+            yield
+        hidden = jnp.concatenate(hiddens, axis=1)
+        out[here] = (residual + mm(hidden, mlp_down[...])).astype(out.dtype)
+
+    interleave(*(mlp_steps(start) for start in range(0, planes, 2)))
+
+
+def gelu(values):
+    half = values * 0.5
+    cubic = values * (GELU_LINEAR + GELU_CUBIC * (values * values))
+    return half + half * jnp.tanh(cubic)
 
 
 VMEM = pl.BlockSpec(memory_space=pltpu.VMEM)
@@ -464,7 +567,7 @@
         [
             ((3 * width, width), bf16),
             ((heads // 2, tile, 2 * tile), f32),
-            ((heads // 2, SPAN * plane, 2 * plane), f32),
+            ((heads // 2, (SPAN + 1) * plane, 2 * plane), f32),
         ],
         [
             *(
@@ -495,14 +598,16 @@
         bytes_accessed=2**20,
     )
     got = [results[0]] + [swap(results[step], 2 * step) for step in range(1, half)]
-    twins = [swap(block, 1) for block in got]
+    (give,) = call(
+        pack_kernel, [VMEM] * half, [((half * chunk, width), bf16)], [*got], 4
+    )
+    twin = swap(give, 1)
     reach = REACH * plane
-    ext = tokens + 2 * reach
     residual, inner, outer = call(
         functools.partial(gather_kernel, plane, half),
-        [VMEM] * (2 * half),
+        [VMEM] * (half + 1),
         [((tokens, width), bf16), ((reach, width), bf16), ((reach, width), bf16)],
-        [*got, *twins],
+        [*got, twin],
         4,
     )
     count = lax.axis_size("space")
@@ -510,29 +615,43 @@
     odd = [(i, ((i + 1) ^ 1) - 1) for i in range(count) if 0 <= ((i + 1) ^ 1) - 1 < count]
     inner = lax.ppermute(inner, "space", even)
     outer = lax.ppermute(outer, "space", odd)
+    gain = gain_second.reshape(1, width)
+    pairs = heads // 2
+    partial = call(
+        functools.partial(inside_kernel, plane),
+        [SMEM] + [VMEM] * 4,
+        [
+            ((width, tokens), bf16),
+            ((width, width), bf16),
+            ((planes, width, plane), f32),
+            ((planes, pairs, 2 * plane), f32),
+            ((planes, pairs, 2 * plane), f32),
+        ],
+        [corner, residual, gain, window_qkv, window_table],
+        16,
+        flops=2 * tokens * width * 14 * width,
+        bytes_accessed=2**22,
+    )
     (out,) = call(
-        functools.partial(window_kernel, plane),
-        [SMEM] + [VMEM] * 10,
+        functools.partial(outside_kernel, plane),
+        [SMEM] + [VMEM] * 15,
         [((tokens, width), bf16)],
         [
             corner,
             residual,
             inner,
             outer,
-            gain_second.reshape(1, width),
+            gain,
             window_qkv,
             window_table,
+            *partial,
             window_out,
             gain_third.reshape(1, width),
             mlp_up,
             mlp_down,
         ],
-        24,
-        scratch=[
-            pltpu.VMEM((ext, width), bf16),
-            pltpu.VMEM((width, ext), bf16),
-            pltpu.VMEM((heads // 2, (planes + REACH) * plane, 128), bf16),
-        ],
+        20,
+        scratch=[pltpu.VMEM((2 * reach, width), bf16), pltpu.VMEM((width, 2 * reach), bf16)],
         flops=2 * tokens * width * 14 * width,
         bytes_accessed=2**22,
     )

time: 37.5 us -> 34.7 us (0.925)
  waiting for transfers between devices: 14.1 us -> 10.9 us
  Pallas kernels: 11.3 us -> 11.7 us
    ppermute x1, waiting for transfers between devices: 3.47 us -> 0.07 us  [local(): inner = lax.ppermute(inner, 'space', even)]
    pallas_call x4 -> x6, Pallas kernels: 11.3 us -> 11.7 us  [call(): pl.pallas_call(kernel, in_specs=specs, out_specs=[VMEM] * len(shapes), ou...]
    ppermute x11 -> x8, waiting for transfers between devices: 7.46 us -> 7.64 us  [swap(): return lax.ppermute(block, 'phase', [(i, i ^ mask) for i in range(bins)])]
    ppermute x11 -> x8, starting transfers between devices: 7.24 us -> 7.3 us  [swap(): return lax.ppermute(block, 'phase', [(i, i ^ mask) for i in range(bins)])]
  transfers between devices with their start and end apart: 13 -> 10, of which waited for: 9 -> 9; matrix products, arithmetic and copies ran while one was open for 2% -> 2% of each run, Pallas kernels for 5% -> 15%
where the time goes in v2:
time: 34.7 us; the launch traced here: 34.5 us
  Pallas kernels  11.7 us (34%)
  starting transfers between devices  10.9 us (31%)
  waiting for transfers between devices  10.9 us (31%)
  local copies, waits for them, and re-layouts  0.87 us (3%)
    pallas_call x6, Pallas kernels, call(): pl.pallas_call(kernel, in_specs=specs, out_specs=[VMEM] * len(shapes), ou...  11.7 us
    ppermute x8, waiting for transfers between devices, swap(): return lax.ppermute(block, 'phase', [(i, i ^ mask) for i in range(bins)])  7.64 us
    ppermute x8, starting transfers between devices, swap(): return lax.ppermute(block, 'phase', [(i, i ^ mask) for i in range(bins)])  7.3 us
    ppermute x1, waiting for transfers between devices, local(): outer = lax.ppermute(outer, 'space', odd)  3.18 us
    ppermute x1, starting transfers between devices, local(): outer = lax.ppermute(outer, 'space', odd)  1.91 us
    ppermute x1, starting transfers between devices, local(): inner = lax.ppermute(inner, 'space', even)  1.64 us
    another operation x2, local copies, waits for them, and re-layouts, piece(): jnp.stack([lax.dynamic_slice_in_dim(source, start, chunk, axis=0) for sou...  0.83 us
  transfers between devices with their start and end apart: 10, of which 9 were waited for; matrix products, arithmetic and copies ran while one was open for 2% of the time, Pallas kernels for 15%

profile of v2, /device:TPU:16, one launch (start us, length us, event | category | flops | bytes accessed | tf_op | source)
XLA Modules:
  0.0 34.5 jit_solution(16048817992683226152)
XLA Ops:
  0.0 0.0 collective-permute-start
  0.0 0.8 %dynamic-slice_bitcast_fusion.1 = (bf16[1,64,256]{2,1,0:T(8,128)(2,1)S(1)}, bf16[1,64,256]{2,1,0:T(8,128)(2,1)S(1)}, bf16[1,64,256]{2,1,0:T(8,128)(2,1)S(1)}, bf16[1,64,256]{2,1,0:T(8,128)(2,1)S(1)}) fusion(bf16[512,256]{1,0:T(8,128)(2,1)} %bitcast.30, s32[]{:T(128)S(6)} %select_n.19, s32[]{:T(128)S(6)} %select_n.18, s32[]{:T(128)S(6)} %select_n.17, ...), kind=kLoop, calls=%fused_computation.5 | loop fusion | bytes 262160 | tf_op jit(solution)/shard_map/stack | solution.py:556
  0.8 0.9 %collective-permute-done = bf16[512,256]{1,0:T(8,128)(2,1)S(1)} collective-permute-done((bf16[512,256]{1,0:T(8,128)(2,1)}, bf16[512,256]{1,0:T(8,128)(2,1)S(1)}, u32[]{:S(2)}, u32[]{:S(2)}) %collective-permute-start) | collective-permute-done | bytes 262176 | tf_op jit(solution)/shard_map/ppermute | solution.py:549
  1.8 1.6 %collective-permute-start.1 = (bf16[2,64,256]{2,1,0:T(8,128)(2,1)S(1)}, bf16[2,64,256]{2,1,0:T(8,128)(2,1)S(1)}, u32[]{:S(2)}, u32[]{:S(2)}) collective-permute-start(bf16[2,64,256]{2,1,0:T(8,128)(2,1)S(1)} %pad_maximum_fusion.1), channel_id=1, source_target_pairs={{0,8},{4,12},{8,0},{12,4},{16,24},{20,28},{24,16},{28,20},{1,9},{5... | collective-permute-start | bytes 196616 | tf_op jit(solution)/shard_map/ppermute | solution.py:549
  3.3 1.6 %collective-permute-start.2 = (bf16[2,64,256]{2,1,0:T(8,128)(2,1)S(1)}, bf16[2,64,256]{2,1,0:T(8,128)(2,1)S(1)}, u32[]{:S(2)}, u32[]{:S(2)}) collective-permute-start(bf16[2,64,256]{2,1,0:T(8,128)(2,1)S(1)} %pad_maximum_fusion.2), channel_id=1, source_target_pairs={{0,16},{4,20},{8,24},{12,28},{16,0},{20,4},{24,8},{28,12},{1,17},{... | collective-permute-start | bytes 196616 | tf_op jit(solution)/shard_map/ppermute | solution.py:549
  4.9 0.5 %collective-permute-start.3 = (bf16[2,64,256]{2,1,0:T(8,128)(2,1)S(1)}, bf16[2,64,256]{2,1,0:T(8,128)(2,1)S(1)}, u32[]{:S(2)}, u32[]{:S(2)}) collective-permute-start(bf16[2,64,256]{2,1,0:T(8,128)(2,1)S(1)} %pad_maximum_fusion.3._), channel_id=1, source_target_pairs={{0,24},{4,28},{8,16},{12,20},{16,8},{20,12},{24,0},{28,4},{1,25},{... | collective-permute-start | bytes 196616 | tf_op jit(solution)/shard_map/ppermute | solution.py:549
  5.5 0.0 copy-start.3
  5.5 0.0 copy-start.6
  5.5 0.0 copy-start.2
  5.5 0.0 copy-start.5
  5.5 0.0 copy-start.7
  5.5 2.0 %shard_map.136 = (bf16[768,256]{1,0:T(8,128)(2,1)S(1)}, f32[4,128,256]{2,1,0:T(8,128)S(1)}, f32[4,640,256]{2,1,0:T(8,128)S(1)}) custom-call(s32[8]{0:T(128)} %bin_phase_at.1, s32[3,8]{1,0:T(4,128)} %bitcast.22, f32[8,64]{1,0:T(8,128)} %window_bias_at.1, f32[8,8]{1,0:T(8,128)} %phase_bias_at.1, bf16[256,768]{1,0:T(8,128)(2,1)} %phase_qkv_at.1, ...), custom_call_target="tpu_custom_call" | custom-call | flops 2000000000 | bytes 4194304 | tf_op jit(solution)/shard_map/pallas_call | solution.py:508
  7.5 0.0 collective-permute-done.1.refs_1_
  7.5 0.2 collective-permute-done.2.refs_2_
  7.7 2.5 %collective-permute-done.3.refs_3_ = bf16[2,64,256]{2,1,0:T(8,128)(2,1)S(1)} collective-permute-done((bf16[2,64,256]{2,1,0:T(8,128)(2,1)S(1)}, bf16[2,64,256]{2,1,0:T(8,128)(2,1)S(1)}, u32[]{:S(2)}, u32[]{:S(2)}) %collective-permute-start.3) | collective-permute-done | bytes 65568 | tf_op jit(solution)/shard_map/ppermute | solution.py:549
  10.2 0.0 copy-done.3
  10.2 0.0 copy-done.6
  10.2 0.0 copy-start
  10.2 0.0 copy-start.1
  10.2 0.0 copy-start.4
  10.2 0.0 copy-start.8
  10.2 1.7 %shard_map.137 = (bf16[2,64,256]{2,1,0:T(8,128)(2,1)S(1)}, bf16[2,64,256]{2,1,0:T(8,128)(2,1)S(1)}, bf16[2,64,256]{2,1,0:T(8,128)(2,1)S(1)}, bf16[2,64,256]{2,1,0:T(8,128)(2,1)S(1)}) custom-call(bf16[2,64,256]{2,1,0:T(8,128)(2,1)S(1)} %pad_maximum_fusion.refs_0_, bf16[2,64,256]{2,1,0:T(8,128)(2,1)S(1)} %collective-permute-done.1.refs_1_, ...), custom_call_target="tpu_custom_call" | custom-call | flops 335544320 | bytes 1048576 | tf_op jit(solution)/shard_map/pallas_call | solution.py:508
  11.9 0.6 %collective-permute-start.4 = (bf16[2,64,256]{2,1,0:T(8,128)(2,1)S(1)}, bf16[2,64,256]{2,1,0:T(8,128)(2,1)S(1)}, u32[]{:S(2)}, u32[]{:S(2)}) collective-permute-start(bf16[2,64,256]{2,1,0:T(8,128)(2,1)S(1)} %get-tuple-element.23), channel_id=1, source_target_pairs={{0,8},{4,12},{8,0},{12,4},{16,24},{20,28},{24,16},{28,20},{1,9},{5... | collective-permute-start | bytes 196616 | tf_op jit(solution)/shard_map/ppermute | solution.py:549
  12.5 0.5 %collective-permute-start.5 = (bf16[2,64,256]{2,1,0:T(8,128)(2,1)S(1)}, bf16[2,64,256]{2,1,0:T(8,128)(2,1)S(1)}, u32[]{:S(2)}, u32[]{:S(2)}) collective-permute-start(bf16[2,64,256]{2,1,0:T(8,128)(2,1)S(1)} %get-tuple-element.24), channel_id=1, source_target_pairs={{0,16},{4,20},{8,24},{12,28},{16,0},{20,4},{24,8},{28,12},{1,17},{... | collective-permute-start | bytes 196616 | tf_op jit(solution)/shard_map/ppermute | solution.py:549
  13.0 2.4 %collective-permute-start.6 = (bf16[2,64,256]{2,1,0:T(8,128)(2,1)S(1)}, bf16[2,64,256]{2,1,0:T(8,128)(2,1)S(1)}, u32[]{:S(2)}, u32[]{:S(2)}) collective-permute-start(bf16[2,64,256]{2,1,0:T(8,128)(2,1)S(1)} %get-tuple-element.25), channel_id=1, source_target_pairs={{0,24},{4,28},{8,16},{12,20},{16,8},{20,12},{24,0},{28,4},{1,25},{... | collective-permute-start | bytes 196616 | tf_op jit(solution)/shard_map/ppermute | solution.py:549
  15.5 0.8 %collective-permute-done.4.refs_1_ = bf16[2,64,256]{2,1,0:T(8,128)(2,1)S(1)} collective-permute-done((bf16[2,64,256]{2,1,0:T(8,128)(2,1)S(1)}, bf16[2,64,256]{2,1,0:T(8,128)(2,1)S(1)}, u32[]{:S(2)}, u32[]{:S(2)}) %collective-permute-start.4) | collective-permute-done | bytes 65568 | tf_op jit(solution)/shard_map/ppermute | solution.py:549
  16.2 0.5 %collective-permute-done.5.refs_2_ = bf16[2,64,256]{2,1,0:T(8,128)(2,1)S(1)} collective-permute-done((bf16[2,64,256]{2,1,0:T(8,128)(2,1)S(1)}, bf16[2,64,256]{2,1,0:T(8,128)(2,1)S(1)}, u32[]{:S(2)}, u32[]{:S(2)}) %collective-permute-start.5) | collective-permute-done | bytes 65568 | tf_op jit(solution)/shard_map/ppermute | solution.py:549
  16.8 1.4 %collective-permute-done.6.refs_3_ = bf16[2,64,256]{2,1,0:T(8,128)(2,1)S(1)} collective-permute-done((bf16[2,64,256]{2,1,0:T(8,128)(2,1)S(1)}, bf16[2,64,256]{2,1,0:T(8,128)(2,1)S(1)}, u32[]{:S(2)}, u32[]{:S(2)}) %collective-permute-start.6) | collective-permute-done | bytes 65568 | tf_op jit(solution)/shard_map/ppermute | solution.py:549
  18.2 0.1 collective-permute-start.7
  18.3 1.3 %collective-permute-done.7.refs_4_ = bf16[256,256]{1,0:T(8,128)(2,1)S(1)} collective-permute-done((bf16[256,256]{1,0:T(8,128)(2,1)S(1)}, bf16[256,256]{1,0:T(8,128)(2,1)S(1)}, u32[]{:S(2)}, u32[]{:S(2)}) %collective-permute-start.7) | collective-permute-done | bytes 131104 | tf_op jit(solution)/shard_map/ppermute | solution.py:549
  19.6 0.1 shard_map.139
  19.7 1.6 %collective-permute-start.8 = (bf16[384,256]{1,0:T(8,128)(2,1)S(1)}, bf16[384,256]{1,0:T(8,128)(2,1)S(1)}, u32[]{:S(2)}, u32[]{:S(2)}) collective-permute-start(bf16[384,256]{1,0:T(8,128)(2,1)S(1)} %get-tuple-element.27), channel_id=1, source_target_pairs={{0,1},{1,0},{2,3},{3,2},{4,5},{5,4},{6,7},{7,6},{8,9},{9,8},{10,11... | collective-permute-start | bytes 589832 | tf_op jit(solution)/shard_map/ppermute | solution.py:616
  21.3 1.9 %collective-permute-start.9 = (bf16[384,256]{1,0:T(8,128)(2,1)S(1)}, bf16[384,256]{1,0:T(8,128)(2,1)S(1)}, u32[]{:S(2)}, u32[]{:S(2)}) collective-permute-start(bf16[384,256]{1,0:T(8,128)(2,1)S(1)} %get-tuple-element.28), channel_id=1, source_target_pairs={{1,2},{2,1},{5,6},{6,5},{9,10},{10,9},{13,14},{14,13},{17,18},{18,... | collective-permute-start | bytes 589832 | tf_op jit(solution)/shard_map/ppermute | solution.py:617
  23.2 0.0 copy-done.2
  23.2 0.0 copy-done.5
  23.2 0.0 copy-done.7
  23.3 3.4 %shard_map.140 = (bf16[256,512]{1,0:T(8,128)(2,1)S(1)}, bf16[256,256]{1,0:T(8,128)(2,1)S(1)}, f32[4,256,128]{2,1,0:T(8,128)S(1)}, f32[4,4,256]{2,1,0:T(4,128)S(1)}, f32[4,4,256]{2,1,0:T(4,128)S(1)}) custom-call(s32[3,8]{1,0:T(4,128)S(1)} %bitcast.23, bf16[512,256]{1,0:T(8,128)(2,1)S(1)} %get-tuple-element.26.own, f32[1,256]{1,0:T(1,128)S(1)} %bitcast.26, ...), custom_call_target="tpu_custom_call" | custom-call | flops 939524096 | bytes 4194304 | tf_op jit(solution)/shard_map/pallas_call | solution.py:508
  26.6 0.1 collective-permute-done.8.inner
  26.7 3.2 %collective-permute-done.9.outer = bf16[384,256]{1,0:T(8,128)(2,1)S(1)} collective-permute-done((bf16[384,256]{1,0:T(8,128)(2,1)S(1)}, bf16[384,256]{1,0:T(8,128)(2,1)S(1)}, u32[]{:S(2)}, u32[]{:S(2)}) %collective-permute-start.9) | collective-permute-done | bytes 196640 | tf_op jit(solution)/shard_map/ppermute | solution.py:617
  29.9 0.0 copy-done
  29.9 0.0 copy-done.1
  29.9 0.0 copy-done.4
  29.9 0.0 copy-done.8
  29.9 4.6 %shard_map.141 = bf16[512,256]{1,0:T(8,128)(2,1)} custom-call(s32[3,8]{1,0:T(4,128)S(1)} %bitcast.24, bf16[512,256]{1,0:T(8,128)(2,1)S(1)} %get-tuple-element.26.own, bf16[384,256]{1,0:T(8,128)(2,1)S(1)} %collective-permute-done.8.inner, bf16[384,256]{1,0:T(8,128)(2,1)S(1)} %collective-permute-done.9.outer, f32[1,256]{1,0:T(1,128)S(1)} %bitcast.27, ...), custom_call_target="tpu_custom_call" | custom-call | flops 939524096 | bytes 4194304 | tf_op jit(solution)/shard_map/pallas_call | solution.py:508
  (6 shorter events, 0.1 us)
Async XLA Ops:
  0.0 1.7 %collective-permute-start = (bf16[512,256]{1,0:T(8,128)(2,1)}, bf16[512,256]{1,0:T(8,128)(2,1)S(1)}, u32[]{:S(2)}, u32[]{:S(2)}) collective-permute-start(bf16[512,256]{1,0:T(8,128)(2,1)} %bitcast.29), channel_id=1, source_target_pairs={{0,4},{4,0},{8,12},{12,8},{16,20},{20,16},{24,28},{28,24},{1,5},{5... | collective-permute-start | bytes 786440 | tf_op jit(solution)/shard_map/ppermute | solution.py:549
  1.8 5.7 %collective-permute-start.1 = (bf16[2,64,256]{2,1,0:T(8,128)(2,1)S(1)}, bf16[2,64,256]{2,1,0:T(8,128)(2,1)S(1)}, u32[]{:S(2)}, u32[]{:S(2)}) collective-permute-start(bf16[2,64,256]{2,1,0:T(8,128)(2,1)S(1)} %pad_maximum_fusion.1), channel_id=1, source_target_pairs={{0,8},{4,12},{8,0},{12,4},{16,24},{20,28},{24,16},{28,20},{1,9},{5... | collective-permute-start | bytes 196616 | tf_op jit(solution)/shard_map/ppermute | solution.py:549
  3.3 4.3 %collective-permute-start.2 = (bf16[2,64,256]{2,1,0:T(8,128)(2,1)S(1)}, bf16[2,64,256]{2,1,0:T(8,128)(2,1)S(1)}, u32[]{:S(2)}, u32[]{:S(2)}) collective-permute-start(bf16[2,64,256]{2,1,0:T(8,128)(2,1)S(1)} %pad_maximum_fusion.2), channel_id=1, source_target_pairs={{0,16},{4,20},{8,24},{12,28},{16,0},{20,4},{24,8},{28,12},{1,17},{... | collective-permute-start | bytes 196616 | tf_op jit(solution)/shard_map/ppermute | solution.py:549
  4.9 5.2 %collective-permute-start.3 = (bf16[2,64,256]{2,1,0:T(8,128)(2,1)S(1)}, bf16[2,64,256]{2,1,0:T(8,128)(2,1)S(1)}, u32[]{:S(2)}, u32[]{:S(2)}) collective-permute-start(bf16[2,64,256]{2,1,0:T(8,128)(2,1)S(1)} %pad_maximum_fusion.3._), channel_id=1, source_target_pairs={{0,24},{4,28},{8,16},{12,20},{16,8},{20,12},{24,0},{28,4},{1,25},{... | collective-permute-start | bytes 196616 | tf_op jit(solution)/shard_map/ppermute | solution.py:549
  5.5 4.7 %copy-start.3 = (bf16[256,256]{1,0:T(8,128)(2,1)S(1)}, bf16[256,256]{1,0:T(8,128)(2,1)}, u32[]{:S(2)}) copy-start(bf16[256,256]{1,0:T(8,128)(2,1)} %refs_7_.1) | copy-start | bytes 393220
  5.5 4.7 %copy-start.6 = (f32[256]{0:T(256)S(1)}, f32[256]{0:T(256)}, u32[]{:S(2)}) copy-start(f32[256]{0:T(256)} %param.15) | copy-start | bytes 3076
  5.5 17.8 %copy-start.2 = (bf16[256,768]{1,0:T(8,128)(2,1)S(1)}, bf16[256,768]{1,0:T(8,128)(2,1)}, u32[]{:S(2)}) copy-start(bf16[256,768]{1,0:T(8,128)(2,1)} %qkv.3) | copy-start | bytes 1179652
  5.5 17.8 %copy-start.5 = (s32[8,3]{0,1:T(4,128)S(1)}, s32[8,3]{0,1:T(4,128)}, u32[]{:S(2)}) copy-start(s32[8,3]{0,1:T(4,128)} %param.23) | copy-start | bytes 292
  5.5 17.8 %copy-start.7 = (f32[256]{0:T(256)S(1)}, f32[256]{0:T(256)}, u32[]{:S(2)}) copy-start(f32[256]{0:T(256)} %param.20) | copy-start | bytes 3076
  10.2 19.7 %copy-start = (bf16[256,1024]{1,0:T(8,128)(2,1)S(1)}, bf16[256,1024]{1,0:T(8,128)(2,1)}, u32[]{:S(2)}) copy-start(bf16[256,1024]{1,0:T(8,128)(2,1)} %mlp_up.1) | copy-start | bytes 1572868
  10.2 19.7 %copy-start.1 = (bf16[1024,256]{1,0:T(8,128)(2,1)S(1)}, bf16[1024,256]{1,0:T(8,128)(2,1)}, u32[]{:S(2)}) copy-start(bf16[1024,256]{1,0:T(8,128)(2,1)} %mlp_down.1) | copy-start | bytes 1572868
  10.2 19.7 %copy-start.4 = (bf16[256,256]{1,0:T(8,128)(2,1)S(1)}, bf16[256,256]{1,0:T(8,128)(2,1)}, u32[]{:S(2)}) copy-start(bf16[256,256]{1,0:T(8,128)(2,1)} %out_weight.1) | copy-start | bytes 393220
  10.2 19.7 %copy-start.8 = (f32[256]{0:T(256)S(1)}, f32[256]{0:T(256)}, u32[]{:S(2)}) copy-start(f32[256]{0:T(256)} %param.25) | copy-start | bytes 3076
  11.9 4.3 %collective-permute-start.4 = (bf16[2,64,256]{2,1,0:T(8,128)(2,1)S(1)}, bf16[2,64,256]{2,1,0:T(8,128)(2,1)S(1)}, u32[]{:S(2)}, u32[]{:S(2)}) collective-permute-start(bf16[2,64,256]{2,1,0:T(8,128)(2,1)S(1)} %get-tuple-element.23), channel_id=1, source_target_pairs={{0,8},{4,12},{8,0},{12,4},{16,24},{20,28},{24,16},{28,20},{1,9},{5... | collective-permute-start | bytes 196616 | tf_op jit(solution)/shard_map/ppermute | solution.py:549
  12.5 4.3 %collective-permute-start.5 = (bf16[2,64,256]{2,1,0:T(8,128)(2,1)S(1)}, bf16[2,64,256]{2,1,0:T(8,128)(2,1)S(1)}, u32[]{:S(2)}, u32[]{:S(2)}) collective-permute-start(bf16[2,64,256]{2,1,0:T(8,128)(2,1)S(1)} %get-tuple-element.24), channel_id=1, source_target_pairs={{0,16},{4,20},{8,24},{12,28},{16,0},{20,4},{24,8},{28,12},{1,17},{... | collective-permute-start | bytes 196616 | tf_op jit(solution)/shard_map/ppermute | solution.py:549
  13.0 5.2 %collective-permute-start.6 = (bf16[2,64,256]{2,1,0:T(8,128)(2,1)S(1)}, bf16[2,64,256]{2,1,0:T(8,128)(2,1)S(1)}, u32[]{:S(2)}, u32[]{:S(2)}) collective-permute-start(bf16[2,64,256]{2,1,0:T(8,128)(2,1)S(1)} %get-tuple-element.25), channel_id=1, source_target_pairs={{0,24},{4,28},{8,16},{12,20},{16,8},{20,12},{24,0},{28,4},{1,25},{... | collective-permute-start | bytes 196616 | tf_op jit(solution)/shard_map/ppermute | solution.py:549
  18.2 1.4 %collective-permute-start.7 = (bf16[256,256]{1,0:T(8,128)(2,1)S(1)}, bf16[256,256]{1,0:T(8,128)(2,1)S(1)}, u32[]{:S(2)}, u32[]{:S(2)}) collective-permute-start(bf16[256,256]{1,0:T(8,128)(2,1)S(1)} %shard_map.138), channel_id=1, source_target_pairs={{0,4},{4,0},{8,12},{12,8},{16,20},{20,16},{24,28},{28,24},{1,5},{5... | collective-permute-start | bytes 393224 | tf_op jit(solution)/shard_map/ppermute | solution.py:549
  19.7 7.0 %collective-permute-start.8 = (bf16[384,256]{1,0:T(8,128)(2,1)S(1)}, bf16[384,256]{1,0:T(8,128)(2,1)S(1)}, u32[]{:S(2)}, u32[]{:S(2)}) collective-permute-start(bf16[384,256]{1,0:T(8,128)(2,1)S(1)} %get-tuple-element.27), channel_id=1, source_target_pairs={{0,1},{1,0},{2,3},{3,2},{4,5},{5,4},{6,7},{7,6},{8,9},{9,8},{10,11... | collective-permute-start | bytes 589832 | tf_op jit(solution)/shard_map/ppermute | solution.py:616
  21.3 8.6 %collective-permute-start.9 = (bf16[384,256]{1,0:T(8,128)(2,1)S(1)}, bf16[384,256]{1,0:T(8,128)(2,1)S(1)}, u32[]{:S(2)}, u32[]{:S(2)}) collective-permute-start(bf16[384,256]{1,0:T(8,128)(2,1)S(1)} %get-tuple-element.28), channel_id=1, source_target_pairs={{1,2},{2,1},{5,6},{6,5},{9,10},{10,9},{13,14},{14,13},{17,18},{18,... | collective-permute-start | bytes 589832 | tf_op jit(solution)/shard_map/ppermute | solution.py:617

commit v3 on v2

--- a/solution.py
+++ b/solution.py
@@ -32,7 +32,7 @@
 
 
 def prep_kernel(
-    bins,
+    masks,
     extent_x,
     extent_y,
     bin_phase_at,
@@ -73,18 +73,19 @@
     phase_weights[width : 2 * width] = phase_qkv[:, 2 * width :].T
     phase_weights[2 * width :] = phase_qkv[:, width : 2 * width]
     me = lax.axis_index("phase")
+    bins = len(masks)
     tile = ROWS * bins
     slot = lax.broadcasted_iota(jnp.int32, (heads, tile), 1) // ROWS
     query_phase = jnp.zeros((heads, tile), jnp.int32)
-    for member in range(bins):
-        query_phase = jnp.where(slot == member, bin_phase[me ^ member], query_phase)
+    for member, mask in enumerate(masks):
+        query_phase = jnp.where(slot == member, bin_phase[me ^ mask], query_phase)
     same = (
         lax.broadcasted_iota(jnp.int32, (ROWS, tile), 0)
         == lax.broadcasted_iota(jnp.int32, (ROWS, tile), 1) % ROWS
     )
     bias = phase_bias[...] * LOG2E
-    for member in range(bins):
-        gap = bin_phase[me ^ member] - query_phase
+    for member, mask in enumerate(masks):
+        gap = bin_phase[me ^ mask] - query_phase
         gap = jnp.where(gap < 0, gap + bins, gap)
         value = jnp.zeros((heads, tile), jnp.float32)
         for step in range(bins):
@@ -280,15 +281,16 @@
         give[step * chunk : (step + 1) * chunk] = source[1]
 
 
-def gather_kernel(plane, half, *refs):
+def gather_kernel(plane, masks, *refs):
+    half = len(masks) // 2
     got = refs[:half]
     twin, residual, inner, outer = refs[half:]
     me = lax.axis_index("phase")
     chunk = got[0].shape[1]
     for step in range(half):
-        start = pl.multiple_of((me ^ (2 * step)) * chunk, ROWS)
+        start = pl.multiple_of((me ^ masks[2 * step]) * chunk, ROWS)
         residual[pl.ds(start, chunk)] = got[step][0]
-        start = pl.multiple_of((me ^ (2 * step + 1)) * chunk, ROWS)
+        start = pl.multiple_of((me ^ masks[2 * step + 1]) * chunk, ROWS)
         residual[pl.ds(start, chunk)] = twin[step * chunk : (step + 1) * chunk]
     reach = inner.shape[0]
     extra = residual.shape[0] - reach
@@ -557,12 +559,13 @@
             [lax.dynamic_slice_in_dim(source, start, chunk, axis=0) for source in (own, twin)]
         )
 
-    pieces = [piece(2 * step) for step in range(half)]
-    blocks = pieces[:1] + [swap(pieces[step], 2 * step) for step in range(1, half)]
+    masks = [0, 1] + [2 * step + part for step in range(half - 1, 0, -1) for part in range(2)]
+    pieces = [piece(mask) for mask in masks[::2]]
+    blocks = pieces[:1] + [swap(pieces[step], masks[2 * step]) for step in range(1, half)]
     corner = window_corner.T
 
     phase_weights, phase_table, window_table = call(
-        functools.partial(prep_kernel, bins, extent_x, extent_y),
+        functools.partial(prep_kernel, masks, extent_x, extent_y),
         [HBM] * 5 + [ANY],
         [
             ((3 * width, width), bf16),
@@ -597,24 +600,32 @@
         flops=2 * tokens * width * 5 * width,
         bytes_accessed=2**20,
     )
-    got = [results[0]] + [swap(results[step], 2 * step) for step in range(1, half)]
+    got = [results[0]] + [swap(results[step], masks[2 * step]) for step in range(1, half)]
     (give,) = call(
         pack_kernel, [VMEM] * half, [((half * chunk, width), bf16)], [*got], 4
     )
     twin = swap(give, 1)
     reach = REACH * plane
     residual, inner, outer = call(
-        functools.partial(gather_kernel, plane, half),
+        functools.partial(gather_kernel, plane, masks),
         [VMEM] * (half + 1),
         [((tokens, width), bf16), ((reach, width), bf16), ((reach, width), bf16)],
         [*got, twin],
         4,
     )
     count = lax.axis_size("space")
-    even = [(i, i ^ 1) for i in range(count) if i ^ 1 < count]
-    odd = [(i, ((i + 1) ^ 1) - 1) for i in range(count) if 0 <= ((i + 1) ^ 1) - 1 < count]
-    inner = lax.ppermute(inner, "space", even)
-    outer = lax.ppermute(outer, "space", odd)
+
+    def partners(shift):
+        pairs = []
+        for i in range(bins):
+            for place in range(count):
+                other = ((place + shift) ^ 1) - shift
+                target = (i, other) if 0 <= other < count else (i ^ 1, place)
+                pairs.append((i * count + place, target[0] * count + target[1]))
+        return pairs
+
+    inner = lax.ppermute(inner, ("phase", "space"), partners(0))
+    outer = lax.ppermute(outer, ("phase", "space"), partners(1))
     gain = gain_second.reshape(1, width)
     pairs = heads // 2
     partial = call(

time: 34.7 us -> 32.1 us (0.925)
  starting transfers between devices: 10.9 us -> 8.95 us
  waiting for transfers between devices: 10.9 us -> 10.1 us
    ppermute x2, starting transfers between devices: 3.55 us -> 1.65 us  [the longest x1 1.64 us: local(): inner = lax.ppermute(inner, ('phase', 'space'), partners(0))]
    ppermute x8, waiting for transfers between devices: 7.64 us -> 6.83 us  [swap(): return lax.ppermute(block, 'phase', [(i, i ^ mask) for i in range(bins)])]
  transfers between devices with their start and end apart: 10 -> 10, of which waited for: 9 -> 9; matrix products, arithmetic and copies ran while one was open for 2% -> 3% of each run, Pallas kernels for 15% -> 17%
where the time goes in v3:
time: 32.1 us; the launch traced here: 31.8 us
  Pallas kernels  11.7 us (36%)
  waiting for transfers between devices  10.1 us (31%)
  starting transfers between devices  8.95 us (28%)
  local copies, waits for them, and re-layouts  0.87 us (3%)
    pallas_call x6, Pallas kernels, call(): pl.pallas_call(kernel, in_specs=specs, out_specs=[VMEM] * len(shapes), ou...  11.7 us
    ppermute x8, starting transfers between devices, swap(): return lax.ppermute(block, 'phase', [(i, i ^ mask) for i in range(bins)])  7.3 us
    ppermute x8, waiting for transfers between devices, swap(): return lax.ppermute(block, 'phase', [(i, i ^ mask) for i in range(bins)])  6.83 us
    ppermute x1, waiting for transfers between devices, local(): inner = lax.ppermute(inner, ('phase', 'space'), partners(0))  2 us
    ppermute x1, starting transfers between devices, local(): inner = lax.ppermute(inner, ('phase', 'space'), partners(0))  1.64 us
    ppermute x1, waiting for transfers between devices, local(): outer = lax.ppermute(outer, ('phase', 'space'), partners(1))  1.3 us
    another operation x2, local copies, waits for them, and re-layouts, piece(): jnp.stack([lax.dynamic_slice_in_dim(source, start, chunk, axis=0) for sou...  0.83 us
  transfers between devices with their start and end apart: 10, of which 9 were waited for; matrix products, arithmetic and copies ran while one was open for 3% of the time, Pallas kernels for 17%

profile of v3, /device:TPU:16, one launch (start us, length us, event | category | flops | bytes accessed | tf_op | source)
XLA Modules:
  0.0 31.8 jit_solution(6696898393759660717)
XLA Ops:
  0.0 0.0 collective-permute-start
  0.0 0.8 %dynamic-slice_bitcast_fusion.1 = (bf16[1,64,256]{2,1,0:T(8,128)(2,1)S(1)}, bf16[1,64,256]{2,1,0:T(8,128)(2,1)S(1)}, bf16[1,64,256]{2,1,0:T(8,128)(2,1)S(1)}, bf16[1,64,256]{2,1,0:T(8,128)(2,1)S(1)}) fusion(bf16[512,256]{1,0:T(8,128)(2,1)} %bitcast.30, s32[]{:T(128)S(6)} %select_n.19, s32[]{:T(128)S(6)} %select_n.18, s32[]{:T(128)S(6)} %select_n.17, ...), kind=kLoop, calls=%fused_computation.5 | loop fusion | bytes 262160 | tf_op jit(solution)/shard_map/stack | solution.py:558
  0.8 0.9 %collective-permute-done = bf16[512,256]{1,0:T(8,128)(2,1)S(1)} collective-permute-done((bf16[512,256]{1,0:T(8,128)(2,1)}, bf16[512,256]{1,0:T(8,128)(2,1)S(1)}, u32[]{:S(2)}, u32[]{:S(2)}) %collective-permute-start) | collective-permute-done | bytes 262176 | tf_op jit(solution)/shard_map/ppermute | solution.py:551
  1.8 2.5 %collective-permute-start.1 = (bf16[2,64,256]{2,1,0:T(8,128)(2,1)S(1)}, bf16[2,64,256]{2,1,0:T(8,128)(2,1)S(1)}, u32[]{:S(2)}, u32[]{:S(2)}) collective-permute-start(bf16[2,64,256]{2,1,0:T(8,128)(2,1)S(1)} %pad_maximum_fusion.1), channel_id=1, source_target_pairs={{0,24},{4,28},{8,16},{12,20},{16,8},{20,12},{24,0},{28,4},{1,25},{... | collective-permute-start | bytes 196616 | tf_op jit(solution)/shard_map/ppermute | solution.py:551
  4.3 0.6 %collective-permute-start.2 = (bf16[2,64,256]{2,1,0:T(8,128)(2,1)S(1)}, bf16[2,64,256]{2,1,0:T(8,128)(2,1)S(1)}, u32[]{:S(2)}, u32[]{:S(2)}) collective-permute-start(bf16[2,64,256]{2,1,0:T(8,128)(2,1)S(1)} %pad_maximum_fusion.2), channel_id=1, source_target_pairs={{0,16},{4,20},{8,24},{12,28},{16,0},{20,4},{24,8},{28,12},{1,17},{... | collective-permute-start | bytes 196616 | tf_op jit(solution)/shard_map/ppermute | solution.py:551
  4.9 0.6 %collective-permute-start.3 = (bf16[2,64,256]{2,1,0:T(8,128)(2,1)S(1)}, bf16[2,64,256]{2,1,0:T(8,128)(2,1)S(1)}, u32[]{:S(2)}, u32[]{:S(2)}) collective-permute-start(bf16[2,64,256]{2,1,0:T(8,128)(2,1)S(1)} %pad_maximum_fusion.3._), channel_id=1, source_target_pairs={{0,8},{4,12},{8,0},{12,4},{16,24},{20,28},{24,16},{28,20},{1,9},{5... | collective-permute-start | bytes 196616 | tf_op jit(solution)/shard_map/ppermute | solution.py:551
  5.5 0.0 copy-start.3
  5.5 0.0 copy-start.6
  5.5 0.0 copy-start.2
  5.5 0.0 copy-start.5
  5.5 0.0 copy-start.7
  5.5 2.0 %shard_map.136 = (bf16[768,256]{1,0:T(8,128)(2,1)S(1)}, f32[4,128,256]{2,1,0:T(8,128)S(1)}, f32[4,640,256]{2,1,0:T(8,128)S(1)}) custom-call(s32[8]{0:T(128)} %bin_phase_at.1, s32[3,8]{1,0:T(4,128)} %bitcast.22, f32[8,64]{1,0:T(8,128)} %window_bias_at.1, f32[8,8]{1,0:T(8,128)} %phase_bias_at.1, bf16[256,768]{1,0:T(8,128)(2,1)} %phase_qkv_at.1, ...), custom_call_target="tpu_custom_call" | custom-call | flops 2000000000 | bytes 4194304 | tf_op jit(solution)/shard_map/pallas_call | solution.py:510
  7.5 0.0 collective-permute-done.1.refs_1_
  7.5 1.1 %collective-permute-done.2.refs_2_ = bf16[2,64,256]{2,1,0:T(8,128)(2,1)S(1)} collective-permute-done((bf16[2,64,256]{2,1,0:T(8,128)(2,1)S(1)}, bf16[2,64,256]{2,1,0:T(8,128)(2,1)S(1)}, u32[]{:S(2)}, u32[]{:S(2)}) %collective-permute-start.2) | collective-permute-done | bytes 65568 | tf_op jit(solution)/shard_map/ppermute | solution.py:551
  8.6 0.6 %collective-permute-done.3.refs_3_ = bf16[2,64,256]{2,1,0:T(8,128)(2,1)S(1)} collective-permute-done((bf16[2,64,256]{2,1,0:T(8,128)(2,1)S(1)}, bf16[2,64,256]{2,1,0:T(8,128)(2,1)S(1)}, u32[]{:S(2)}, u32[]{:S(2)}) %collective-permute-start.3) | collective-permute-done | bytes 65568 | tf_op jit(solution)/shard_map/ppermute | solution.py:551
  9.2 0.0 copy-done.3
  9.2 0.0 copy-done.6
  9.2 0.0 copy-start
  9.2 0.0 copy-start.1
  9.2 0.0 copy-start.4
  9.2 0.0 copy-start.8
  9.2 1.7 %shard_map.137 = (bf16[2,64,256]{2,1,0:T(8,128)(2,1)S(1)}, bf16[2,64,256]{2,1,0:T(8,128)(2,1)S(1)}, bf16[2,64,256]{2,1,0:T(8,128)(2,1)S(1)}, bf16[2,64,256]{2,1,0:T(8,128)(2,1)S(1)}) custom-call(bf16[2,64,256]{2,1,0:T(8,128)(2,1)S(1)} %pad_maximum_fusion.refs_0_, bf16[2,64,256]{2,1,0:T(8,128)(2,1)S(1)} %collective-permute-done.1.refs_1_, ...), custom_call_target="tpu_custom_call" | custom-call | flops 335544320 | bytes 1048576 | tf_op jit(solution)/shard_map/pallas_call | solution.py:510
  11.0 1.6 %collective-permute-start.4 = (bf16[2,64,256]{2,1,0:T(8,128)(2,1)S(1)}, bf16[2,64,256]{2,1,0:T(8,128)(2,1)S(1)}, u32[]{:S(2)}, u32[]{:S(2)}) collective-permute-start(bf16[2,64,256]{2,1,0:T(8,128)(2,1)S(1)} %get-tuple-element.23), channel_id=1, source_target_pairs={{0,24},{4,28},{8,16},{12,20},{16,8},{20,12},{24,0},{28,4},{1,25},{... | collective-permute-start | bytes 196616 | tf_op jit(solution)/shard_map/ppermute | solution.py:551
  12.5 0.6 %collective-permute-start.5 = (bf16[2,64,256]{2,1,0:T(8,128)(2,1)S(1)}, bf16[2,64,256]{2,1,0:T(8,128)(2,1)S(1)}, u32[]{:S(2)}, u32[]{:S(2)}) collective-permute-start(bf16[2,64,256]{2,1,0:T(8,128)(2,1)S(1)} %get-tuple-element.24), channel_id=1, source_target_pairs={{0,16},{4,20},{8,24},{12,28},{16,0},{20,4},{24,8},{28,12},{1,17},{... | collective-permute-start | bytes 196616 | tf_op jit(solution)/shard_map/ppermute | solution.py:551
  13.1 1.4 %collective-permute-start.6 = (bf16[2,64,256]{2,1,0:T(8,128)(2,1)S(1)}, bf16[2,64,256]{2,1,0:T(8,128)(2,1)S(1)}, u32[]{:S(2)}, u32[]{:S(2)}) collective-permute-start(bf16[2,64,256]{2,1,0:T(8,128)(2,1)S(1)} %get-tuple-element.25), channel_id=1, source_target_pairs={{0,8},{4,12},{8,0},{12,4},{16,24},{20,28},{24,16},{28,20},{1,9},{5... | collective-permute-start | bytes 196616 | tf_op jit(solution)/shard_map/ppermute | solution.py:551
  14.5 1.7 %collective-permute-done.4.refs_1_ = bf16[2,64,256]{2,1,0:T(8,128)(2,1)S(1)} collective-permute-done((bf16[2,64,256]{2,1,0:T(8,128)(2,1)S(1)}, bf16[2,64,256]{2,1,0:T(8,128)(2,1)S(1)}, u32[]{:S(2)}, u32[]{:S(2)}) %collective-permute-start.4) | collective-permute-done | bytes 65568 | tf_op jit(solution)/shard_map/ppermute | solution.py:551
  16.2 0.7 %collective-permute-done.5.refs_2_ = bf16[2,64,256]{2,1,0:T(8,128)(2,1)S(1)} collective-permute-done((bf16[2,64,256]{2,1,0:T(8,128)(2,1)S(1)}, bf16[2,64,256]{2,1,0:T(8,128)(2,1)S(1)}, u32[]{:S(2)}, u32[]{:S(2)}) %collective-permute-start.5) | collective-permute-done | bytes 65568 | tf_op jit(solution)/shard_map/ppermute | solution.py:551
  16.9 0.5 %collective-permute-done.6.refs_3_ = bf16[2,64,256]{2,1,0:T(8,128)(2,1)S(1)} collective-permute-done((bf16[2,64,256]{2,1,0:T(8,128)(2,1)S(1)}, bf16[2,64,256]{2,1,0:T(8,128)(2,1)S(1)}, u32[]{:S(2)}, u32[]{:S(2)}) %collective-permute-start.6) | collective-permute-done | bytes 65568 | tf_op jit(solution)/shard_map/ppermute | solution.py:551
  17.4 0.1 collective-permute-start.7
  17.5 1.3 %collective-permute-done.7.refs_4_ = bf16[256,256]{1,0:T(8,128)(2,1)S(1)} collective-permute-done((bf16[256,256]{1,0:T(8,128)(2,1)S(1)}, bf16[256,256]{1,0:T(8,128)(2,1)S(1)}, u32[]{:S(2)}, u32[]{:S(2)}) %collective-permute-start.7) | collective-permute-done | bytes 131104 | tf_op jit(solution)/shard_map/ppermute | solution.py:551
  18.8 0.1 shard_map.139
  18.9 1.6 %collective-permute-start.8 = (bf16[384,256]{1,0:T(8,128)(2,1)S(1)}, bf16[384,256]{1,0:T(8,128)(2,1)S(1)}, u32[]{:S(2)}, u32[]{:S(2)}) collective-permute-start(bf16[384,256]{1,0:T(8,128)(2,1)S(1)} %get-tuple-element.27), channel_id=1, source_target_pairs={{0,1},{1,0},{2,3},{3,2},{4,5},{5,4},{6,7},{7,6},{8,9},{9,8},{10,11... | collective-permute-start | bytes 589832 | tf_op jit(solution)/shard_map/ppermute | solution.py:627
  20.5 0.0 collective-permute-start.9
  20.5 0.0 copy-done.2
  20.5 0.0 copy-done.5
  20.5 0.0 copy-done.7
  20.5 3.4 %shard_map.140 = (bf16[256,512]{1,0:T(8,128)(2,1)S(1)}, bf16[256,256]{1,0:T(8,128)(2,1)S(1)}, f32[4,256,128]{2,1,0:T(8,128)S(1)}, f32[4,4,256]{2,1,0:T(4,128)S(1)}, f32[4,4,256]{2,1,0:T(4,128)S(1)}) custom-call(s32[3,8]{1,0:T(4,128)S(1)} %bitcast.23, bf16[512,256]{1,0:T(8,128)(2,1)S(1)} %get-tuple-element.26.own, f32[1,256]{1,0:T(1,128)S(1)} %bitcast.26, ...), custom_call_target="tpu_custom_call" | custom-call | flops 939524096 | bytes 4194304 | tf_op jit(solution)/shard_map/pallas_call | solution.py:510
  23.9 2.0 %collective-permute-done.8.inner = bf16[384,256]{1,0:T(8,128)(2,1)S(1)} collective-permute-done((bf16[384,256]{1,0:T(8,128)(2,1)S(1)}, bf16[384,256]{1,0:T(8,128)(2,1)S(1)}, u32[]{:S(2)}, u32[]{:S(2)}) %collective-permute-start.8) | collective-permute-done | bytes 196640 | tf_op jit(solution)/shard_map/ppermute | solution.py:627
  25.9 1.3 %collective-permute-done.9.outer = bf16[384,256]{1,0:T(8,128)(2,1)S(1)} collective-permute-done((bf16[384,256]{1,0:T(8,128)(2,1)S(1)}, bf16[384,256]{1,0:T(8,128)(2,1)S(1)}, u32[]{:S(2)}, u32[]{:S(2)}) %collective-permute-start.9) | collective-permute-done | bytes 196640 | tf_op jit(solution)/shard_map/ppermute | solution.py:628
  27.2 0.0 copy-done
  27.2 0.0 copy-done.1
  27.2 0.0 copy-done.4
  27.2 0.0 copy-done.8
  27.2 4.6 %shard_map.141 = bf16[512,256]{1,0:T(8,128)(2,1)} custom-call(s32[3,8]{1,0:T(4,128)S(1)} %bitcast.24, bf16[512,256]{1,0:T(8,128)(2,1)S(1)} %get-tuple-element.26.own, bf16[384,256]{1,0:T(8,128)(2,1)S(1)} %collective-permute-done.8.inner, bf16[384,256]{1,0:T(8,128)(2,1)S(1)} %collective-permute-done.9.outer, f32[1,256]{1,0:T(1,128)S(1)} %bitcast.27, ...), custom_call_target="tpu_custom_call" | custom-call | flops 939524096 | bytes 4194304 | tf_op jit(solution)/shard_map/pallas_call | solution.py:510
  (6 shorter events, 0.1 us)
Async XLA Ops:
  0.0 1.7 %collective-permute-start = (bf16[512,256]{1,0:T(8,128)(2,1)}, bf16[512,256]{1,0:T(8,128)(2,1)S(1)}, u32[]{:S(2)}, u32[]{:S(2)}) collective-permute-start(bf16[512,256]{1,0:T(8,128)(2,1)} %bitcast.29), channel_id=1, source_target_pairs={{0,4},{4,0},{8,12},{12,8},{16,20},{20,16},{24,28},{28,24},{1,5},{5... | collective-permute-start | bytes 786440 | tf_op jit(solution)/shard_map/ppermute | solution.py:551
  1.8 5.7 %collective-permute-start.1 = (bf16[2,64,256]{2,1,0:T(8,128)(2,1)S(1)}, bf16[2,64,256]{2,1,0:T(8,128)(2,1)S(1)}, u32[]{:S(2)}, u32[]{:S(2)}) collective-permute-start(bf16[2,64,256]{2,1,0:T(8,128)(2,1)S(1)} %pad_maximum_fusion.1), channel_id=1, source_target_pairs={{0,24},{4,28},{8,16},{12,20},{16,8},{20,12},{24,0},{28,4},{1,25},{... | collective-permute-start | bytes 196616 | tf_op jit(solution)/shard_map/ppermute | solution.py:551
  4.3 4.3 %collective-permute-start.2 = (bf16[2,64,256]{2,1,0:T(8,128)(2,1)S(1)}, bf16[2,64,256]{2,1,0:T(8,128)(2,1)S(1)}, u32[]{:S(2)}, u32[]{:S(2)}) collective-permute-start(bf16[2,64,256]{2,1,0:T(8,128)(2,1)S(1)} %pad_maximum_fusion.2), channel_id=1, source_target_pairs={{0,16},{4,20},{8,24},{12,28},{16,0},{20,4},{24,8},{28,12},{1,17},{... | collective-permute-start | bytes 196616 | tf_op jit(solution)/shard_map/ppermute | solution.py:551
  4.9 4.3 %collective-permute-start.3 = (bf16[2,64,256]{2,1,0:T(8,128)(2,1)S(1)}, bf16[2,64,256]{2,1,0:T(8,128)(2,1)S(1)}, u32[]{:S(2)}, u32[]{:S(2)}) collective-permute-start(bf16[2,64,256]{2,1,0:T(8,128)(2,1)S(1)} %pad_maximum_fusion.3._), channel_id=1, source_target_pairs={{0,8},{4,12},{8,0},{12,4},{16,24},{20,28},{24,16},{28,20},{1,9},{5... | collective-permute-start | bytes 196616 | tf_op jit(solution)/shard_map/ppermute | solution.py:551
  5.5 3.7 %copy-start.3 = (bf16[256,256]{1,0:T(8,128)(2,1)S(1)}, bf16[256,256]{1,0:T(8,128)(2,1)}, u32[]{:S(2)}) copy-start(bf16[256,256]{1,0:T(8,128)(2,1)} %refs_7_.1) | copy-start | bytes 393220
  5.5 3.7 %copy-start.6 = (f32[256]{0:T(256)S(1)}, f32[256]{0:T(256)}, u32[]{:S(2)}) copy-start(f32[256]{0:T(256)} %param.15) | copy-start | bytes 3076
  5.5 15.0 %copy-start.2 = (bf16[256,768]{1,0:T(8,128)(2,1)S(1)}, bf16[256,768]{1,0:T(8,128)(2,1)}, u32[]{:S(2)}) copy-start(bf16[256,768]{1,0:T(8,128)(2,1)} %qkv.3) | copy-start | bytes 1179652
  5.5 15.0 %copy-start.5 = (s32[8,3]{0,1:T(4,128)S(1)}, s32[8,3]{0,1:T(4,128)}, u32[]{:S(2)}) copy-start(s32[8,3]{0,1:T(4,128)} %param.23) | copy-start | bytes 292
  5.5 15.0 %copy-start.7 = (f32[256]{0:T(256)S(1)}, f32[256]{0:T(256)}, u32[]{:S(2)}) copy-start(f32[256]{0:T(256)} %param.20) | copy-start | bytes 3076
  9.2 18.0 %copy-start = (bf16[256,1024]{1,0:T(8,128)(2,1)S(1)}, bf16[256,1024]{1,0:T(8,128)(2,1)}, u32[]{:S(2)}) copy-start(bf16[256,1024]{1,0:T(8,128)(2,1)} %mlp_up.1) | copy-start | bytes 1572868
  9.2 18.0 %copy-start.1 = (bf16[1024,256]{1,0:T(8,128)(2,1)S(1)}, bf16[1024,256]{1,0:T(8,128)(2,1)}, u32[]{:S(2)}) copy-start(bf16[1024,256]{1,0:T(8,128)(2,1)} %mlp_down.1) | copy-start | bytes 1572868
  9.2 18.0 %copy-start.4 = (bf16[256,256]{1,0:T(8,128)(2,1)S(1)}, bf16[256,256]{1,0:T(8,128)(2,1)}, u32[]{:S(2)}) copy-start(bf16[256,256]{1,0:T(8,128)(2,1)} %out_weight.1) | copy-start | bytes 393220
  9.2 18.0 %copy-start.8 = (f32[256]{0:T(256)S(1)}, f32[256]{0:T(256)}, u32[]{:S(2)}) copy-start(f32[256]{0:T(256)} %param.25) | copy-start | bytes 3076
  11.0 5.3 %collective-permute-start.4 = (bf16[2,64,256]{2,1,0:T(8,128)(2,1)S(1)}, bf16[2,64,256]{2,1,0:T(8,128)(2,1)S(1)}, u32[]{:S(2)}, u32[]{:S(2)}) collective-permute-start(bf16[2,64,256]{2,1,0:T(8,128)(2,1)S(1)} %get-tuple-element.23), channel_id=1, source_target_pairs={{0,24},{4,28},{8,16},{12,20},{16,8},{20,12},{24,0},{28,4},{1,25},{... | collective-permute-start | bytes 196616 | tf_op jit(solution)/shard_map/ppermute | solution.py:551
  12.5 4.4 %collective-permute-start.5 = (bf16[2,64,256]{2,1,0:T(8,128)(2,1)S(1)}, bf16[2,64,256]{2,1,0:T(8,128)(2,1)S(1)}, u32[]{:S(2)}, u32[]{:S(2)}) collective-permute-start(bf16[2,64,256]{2,1,0:T(8,128)(2,1)S(1)} %get-tuple-element.24), channel_id=1, source_target_pairs={{0,16},{4,20},{8,24},{12,28},{16,0},{20,4},{24,8},{28,12},{1,17},{... | collective-permute-start | bytes 196616 | tf_op jit(solution)/shard_map/ppermute | solution.py:551
  13.1 4.3 %collective-permute-start.6 = (bf16[2,64,256]{2,1,0:T(8,128)(2,1)S(1)}, bf16[2,64,256]{2,1,0:T(8,128)(2,1)S(1)}, u32[]{:S(2)}, u32[]{:S(2)}) collective-permute-start(bf16[2,64,256]{2,1,0:T(8,128)(2,1)S(1)} %get-tuple-element.25), channel_id=1, source_target_pairs={{0,8},{4,12},{8,0},{12,4},{16,24},{20,28},{24,16},{28,20},{1,9},{5... | collective-permute-start | bytes 196616 | tf_op jit(solution)/shard_map/ppermute | solution.py:551
  17.4 1.4 %collective-permute-start.7 = (bf16[256,256]{1,0:T(8,128)(2,1)S(1)}, bf16[256,256]{1,0:T(8,128)(2,1)S(1)}, u32[]{:S(2)}, u32[]{:S(2)}) collective-permute-start(bf16[256,256]{1,0:T(8,128)(2,1)S(1)} %shard_map.138), channel_id=1, source_target_pairs={{0,4},{4,0},{8,12},{12,8},{16,20},{20,16},{24,28},{28,24},{1,5},{5... | collective-permute-start | bytes 393224 | tf_op jit(solution)/shard_map/ppermute | solution.py:551
  18.9 7.0 %collective-permute-start.8 = (bf16[384,256]{1,0:T(8,128)(2,1)S(1)}, bf16[384,256]{1,0:T(8,128)(2,1)S(1)}, u32[]{:S(2)}, u32[]{:S(2)}) collective-permute-start(bf16[384,256]{1,0:T(8,128)(2,1)S(1)} %get-tuple-element.27), channel_id=1, source_target_pairs={{0,1},{1,0},{2,3},{3,2},{4,5},{5,4},{6,7},{7,6},{8,9},{9,8},{10,11... | collective-permute-start | bytes 589832 | tf_op jit(solution)/shard_map/ppermute | solution.py:627
  20.5 6.7 %collective-permute-start.9 = (bf16[384,256]{1,0:T(8,128)(2,1)S(1)}, bf16[384,256]{1,0:T(8,128)(2,1)S(1)}, u32[]{:S(2)}, u32[]{:S(2)}) collective-permute-start(bf16[384,256]{1,0:T(8,128)(2,1)S(1)} %get-tuple-element.28), channel_id=1, source_target_pairs={{0,4},{1,2},{2,1},{3,7},{4,0},{5,6},{6,5},{7,3},{8,12},{9,10},{10,... | collective-permute-start | bytes 589832 | tf_op jit(solution)/shard_map/ppermute | solution.py:628

commit v4 on v3

--- a/solution.py
+++ b/solution.py
@@ -133,8 +133,9 @@
 def score_steps(keys, queries, tiles, store):
     pieces = []
     tops = []
+    whole = mm(keys, queries)
     for start, stop, table in tiles:
-        piece = mm(keys[start:stop], queries) + table
+        piece = whole[start:stop] + table
         pieces.append(piece)
         tops.append(jnp.max(piece.reshape(-1, 8, piece.shape[1]), axis=0))
         yield
@@ -254,24 +255,32 @@
         parts.append(blend(mm(stack, store.pop("weights")), head_dim))
         yield
 
-    def finish(step):
-        mixed = jnp.concatenate(parts[step * pairs : (step + 1) * pairs], axis=0)
-        span = slice(step * tile, (step + 1) * tile)
+    def finish(steps):
+        mixed = jnp.concatenate(
+            [
+                jnp.concatenate(parts[step * pairs : (step + 1) * pairs], axis=0)
+                for step in steps
+            ],
+            axis=1,
+        )
+        span = slice(steps[0] * tile, (steps[-1] + 1) * tile)
         result = (stream[span] + mm(mixed, out_weight[...], TN)).astype(jnp.bfloat16)
-        for slot in range(bins):
-            outs[slot // 2][slot % 2, step * ROWS : (step + 1) * ROWS] = result[
-                slot * ROWS : (slot + 1) * ROWS
-            ]
-
-    size = pairs
-
-    def side(index):
-        if index * size >= pairs and index * size % pairs == 0:
-            yield
-            finish(index * size // pairs - 1)
-
-    run_pipeline(units, size, first, lambda _, store: soften_steps(store), third, side)
-    finish(tiles - 1)
+        for index, step in enumerate(steps):
+            for slot in range(bins):
+                start = index * tile + slot * ROWS
+                outs[slot // 2][slot % 2, step * ROWS : (step + 1) * ROWS] = result[
+                    start : start + ROWS
+                ]
+
+    run_pipeline(
+        units,
+        len(units),
+        first,
+        lambda _, store: soften_steps(store),
+        third,
+        lambda _: iter(()),
+    )
+    finish(range(tiles))
 
 
 def pack_kernel(*refs):

time: 32.1 us -> 31.7 us (0.988)
  Pallas kernels: 11.7 us -> 11.3 us
    pallas_call x6, Pallas kernels: 11.7 us -> 11.3 us  [call(): pl.pallas_call(kernel, in_specs=specs, out_specs=[VMEM] * len(shapes), ou...]
where the time goes in v4:
time: 31.7 us; the launch traced here: 31.3 us
  Pallas kernels  11.3 us (36%)
  waiting for transfers between devices  10 us (32%)
  starting transfers between devices  8.95 us (28%)
  local copies, waits for them, and re-layouts  0.87 us (3%)
    pallas_call x6, Pallas kernels, call(): pl.pallas_call(kernel, in_specs=specs, out_specs=[VMEM] * len(shapes), ou...  11.3 us
    ppermute x8, starting transfers between devices, swap(): return lax.ppermute(block, 'phase', [(i, i ^ mask) for i in range(bins)])  7.3 us
    ppermute x8, waiting for transfers between devices, swap(): return lax.ppermute(block, 'phase', [(i, i ^ mask) for i in range(bins)])  6.83 us
    ppermute x1, waiting for transfers between devices, local(): inner = lax.ppermute(inner, ('phase', 'space'), partners(0))  1.89 us
    ppermute x1, starting transfers between devices, local(): inner = lax.ppermute(inner, ('phase', 'space'), partners(0))  1.64 us
    ppermute x1, waiting for transfers between devices, local(): outer = lax.ppermute(outer, ('phase', 'space'), partners(1))  1.3 us
    another operation x2, local copies, waits for them, and re-layouts, piece(): jnp.stack([lax.dynamic_slice_in_dim(source, start, chunk, axis=0) for sou...  0.83 us
  transfers between devices with their start and end apart: 10, of which 9 were waited for; matrix products, arithmetic and copies ran while one was open for 3% of the time, Pallas kernels for 17%

profile of v4, /device:TPU:16, one launch (start us, length us, event | category | flops | bytes accessed | tf_op | source)
XLA Modules:
  0.0 31.3 jit_solution(13564246668621913181)
XLA Ops:
  0.0 0.0 collective-permute-start
  0.0 0.8 %dynamic-slice_bitcast_fusion.1 = (bf16[1,64,256]{2,1,0:T(8,128)(2,1)S(1)}, bf16[1,64,256]{2,1,0:T(8,128)(2,1)S(1)}, bf16[1,64,256]{2,1,0:T(8,128)(2,1)S(1)}, bf16[1,64,256]{2,1,0:T(8,128)(2,1)S(1)}) fusion(bf16[512,256]{1,0:T(8,128)(2,1)} %bitcast.30, s32[]{:T(128)S(6)} %select_n.19, s32[]{:T(128)S(6)} %select_n.18, s32[]{:T(128)S(6)} %select_n.17, ...), kind=kLoop, calls=%fused_computation.5 | loop fusion | bytes 262160 | tf_op jit(solution)/shard_map/stack | solution.py:567
  0.8 0.9 %collective-permute-done = bf16[512,256]{1,0:T(8,128)(2,1)S(1)} collective-permute-done((bf16[512,256]{1,0:T(8,128)(2,1)}, bf16[512,256]{1,0:T(8,128)(2,1)S(1)}, u32[]{:S(2)}, u32[]{:S(2)}) %collective-permute-start) | collective-permute-done | bytes 262176 | tf_op jit(solution)/shard_map/ppermute | solution.py:560
  1.8 2.5 %collective-permute-start.1 = (bf16[2,64,256]{2,1,0:T(8,128)(2,1)S(1)}, bf16[2,64,256]{2,1,0:T(8,128)(2,1)S(1)}, u32[]{:S(2)}, u32[]{:S(2)}) collective-permute-start(bf16[2,64,256]{2,1,0:T(8,128)(2,1)S(1)} %pad_maximum_fusion.1), channel_id=1, source_target_pairs={{0,24},{4,28},{8,16},{12,20},{16,8},{20,12},{24,0},{28,4},{1,25},{... | collective-permute-start | bytes 196616 | tf_op jit(solution)/shard_map/ppermute | solution.py:560
  4.3 0.6 %collective-permute-start.2 = (bf16[2,64,256]{2,1,0:T(8,128)(2,1)S(1)}, bf16[2,64,256]{2,1,0:T(8,128)(2,1)S(1)}, u32[]{:S(2)}, u32[]{:S(2)}) collective-permute-start(bf16[2,64,256]{2,1,0:T(8,128)(2,1)S(1)} %pad_maximum_fusion.2), channel_id=1, source_target_pairs={{0,16},{4,20},{8,24},{12,28},{16,0},{20,4},{24,8},{28,12},{1,17},{... | collective-permute-start | bytes 196616 | tf_op jit(solution)/shard_map/ppermute | solution.py:560
  4.9 0.6 %collective-permute-start.3 = (bf16[2,64,256]{2,1,0:T(8,128)(2,1)S(1)}, bf16[2,64,256]{2,1,0:T(8,128)(2,1)S(1)}, u32[]{:S(2)}, u32[]{:S(2)}) collective-permute-start(bf16[2,64,256]{2,1,0:T(8,128)(2,1)S(1)} %pad_maximum_fusion.3._), channel_id=1, source_target_pairs={{0,8},{4,12},{8,0},{12,4},{16,24},{20,28},{24,16},{28,20},{1,9},{5... | collective-permute-start | bytes 196616 | tf_op jit(solution)/shard_map/ppermute | solution.py:560
  5.5 0.0 copy-start.3
  5.5 0.0 copy-start.6
  5.5 0.0 copy-start.2
  5.5 0.0 copy-start.5
  5.5 0.0 copy-start.7
  5.5 2.0 %shard_map.136 = (bf16[768,256]{1,0:T(8,128)(2,1)S(1)}, f32[4,128,256]{2,1,0:T(8,128)S(1)}, f32[4,640,256]{2,1,0:T(8,128)S(1)}) custom-call(s32[8]{0:T(128)} %bin_phase_at.1, s32[3,8]{1,0:T(4,128)} %bitcast.22, f32[8,64]{1,0:T(8,128)} %window_bias_at.1, f32[8,8]{1,0:T(8,128)} %phase_bias_at.1, bf16[256,768]{1,0:T(8,128)(2,1)} %phase_qkv_at.1, ...), custom_call_target="tpu_custom_call" | custom-call | flops 2000000000 | bytes 4194304 | tf_op jit(solution)/shard_map/pallas_call | solution.py:519
  7.5 0.0 collective-permute-done.1.refs_1_
  7.5 1.1 %collective-permute-done.2.refs_2_ = bf16[2,64,256]{2,1,0:T(8,128)(2,1)S(1)} collective-permute-done((bf16[2,64,256]{2,1,0:T(8,128)(2,1)S(1)}, bf16[2,64,256]{2,1,0:T(8,128)(2,1)S(1)}, u32[]{:S(2)}, u32[]{:S(2)}) %collective-permute-start.2) | collective-permute-done | bytes 65568 | tf_op jit(solution)/shard_map/ppermute | solution.py:560
  8.6 0.6 %collective-permute-done.3.refs_3_ = bf16[2,64,256]{2,1,0:T(8,128)(2,1)S(1)} collective-permute-done((bf16[2,64,256]{2,1,0:T(8,128)(2,1)S(1)}, bf16[2,64,256]{2,1,0:T(8,128)(2,1)S(1)}, u32[]{:S(2)}, u32[]{:S(2)}) %collective-permute-start.3) | collective-permute-done | bytes 65568 | tf_op jit(solution)/shard_map/ppermute | solution.py:560
  9.2 0.0 copy-done.3
  9.2 0.0 copy-done.6
  9.2 0.0 copy-start
  9.2 0.0 copy-start.1
  9.2 0.0 copy-start.4
  9.2 0.0 copy-start.8
  9.2 1.3 %shard_map.137 = (bf16[2,64,256]{2,1,0:T(8,128)(2,1)S(1)}, bf16[2,64,256]{2,1,0:T(8,128)(2,1)S(1)}, bf16[2,64,256]{2,1,0:T(8,128)(2,1)S(1)}, bf16[2,64,256]{2,1,0:T(8,128)(2,1)S(1)}) custom-call(bf16[2,64,256]{2,1,0:T(8,128)(2,1)S(1)} %pad_maximum_fusion.refs_0_, bf16[2,64,256]{2,1,0:T(8,128)(2,1)S(1)} %collective-permute-done.1.refs_1_, ...), custom_call_target="tpu_custom_call" | custom-call | flops 335544320 | bytes 1048576 | tf_op jit(solution)/shard_map/pallas_call | solution.py:519
  10.5 1.6 %collective-permute-start.4 = (bf16[2,64,256]{2,1,0:T(8,128)(2,1)S(1)}, bf16[2,64,256]{2,1,0:T(8,128)(2,1)S(1)}, u32[]{:S(2)}, u32[]{:S(2)}) collective-permute-start(bf16[2,64,256]{2,1,0:T(8,128)(2,1)S(1)} %get-tuple-element.23), channel_id=1, source_target_pairs={{0,24},{4,28},{8,16},{12,20},{16,8},{20,12},{24,0},{28,4},{1,25},{... | collective-permute-start | bytes 196616 | tf_op jit(solution)/shard_map/ppermute | solution.py:560
  12.1 0.6 %collective-permute-start.5 = (bf16[2,64,256]{2,1,0:T(8,128)(2,1)S(1)}, bf16[2,64,256]{2,1,0:T(8,128)(2,1)S(1)}, u32[]{:S(2)}, u32[]{:S(2)}) collective-permute-start(bf16[2,64,256]{2,1,0:T(8,128)(2,1)S(1)} %get-tuple-element.24), channel_id=1, source_target_pairs={{0,16},{4,20},{8,24},{12,28},{16,0},{20,4},{24,8},{28,12},{1,17},{... | collective-permute-start | bytes 196616 | tf_op jit(solution)/shard_map/ppermute | solution.py:560
  12.7 1.4 %collective-permute-start.6 = (bf16[2,64,256]{2,1,0:T(8,128)(2,1)S(1)}, bf16[2,64,256]{2,1,0:T(8,128)(2,1)S(1)}, u32[]{:S(2)}, u32[]{:S(2)}) collective-permute-start(bf16[2,64,256]{2,1,0:T(8,128)(2,1)S(1)} %get-tuple-element.25), channel_id=1, source_target_pairs={{0,8},{4,12},{8,0},{12,4},{16,24},{20,28},{24,16},{28,20},{1,9},{5... | collective-permute-start | bytes 196616 | tf_op jit(solution)/shard_map/ppermute | solution.py:560
  14.1 1.7 %collective-permute-done.4.refs_1_ = bf16[2,64,256]{2,1,0:T(8,128)(2,1)S(1)} collective-permute-done((bf16[2,64,256]{2,1,0:T(8,128)(2,1)S(1)}, bf16[2,64,256]{2,1,0:T(8,128)(2,1)S(1)}, u32[]{:S(2)}, u32[]{:S(2)}) %collective-permute-start.4) | collective-permute-done | bytes 65568 | tf_op jit(solution)/shard_map/ppermute | solution.py:560
  15.8 0.7 %collective-permute-done.5.refs_2_ = bf16[2,64,256]{2,1,0:T(8,128)(2,1)S(1)} collective-permute-done((bf16[2,64,256]{2,1,0:T(8,128)(2,1)S(1)}, bf16[2,64,256]{2,1,0:T(8,128)(2,1)S(1)}, u32[]{:S(2)}, u32[]{:S(2)}) %collective-permute-start.5) | collective-permute-done | bytes 65568 | tf_op jit(solution)/shard_map/ppermute | solution.py:560
  16.5 0.5 %collective-permute-done.6.refs_3_ = bf16[2,64,256]{2,1,0:T(8,128)(2,1)S(1)} collective-permute-done((bf16[2,64,256]{2,1,0:T(8,128)(2,1)S(1)}, bf16[2,64,256]{2,1,0:T(8,128)(2,1)S(1)}, u32[]{:S(2)}, u32[]{:S(2)}) %collective-permute-start.6) | collective-permute-done | bytes 65568 | tf_op jit(solution)/shard_map/ppermute | solution.py:560
  17.0 0.1 collective-permute-start.7
  17.0 1.3 %collective-permute-done.7.refs_4_ = bf16[256,256]{1,0:T(8,128)(2,1)S(1)} collective-permute-done((bf16[256,256]{1,0:T(8,128)(2,1)S(1)}, bf16[256,256]{1,0:T(8,128)(2,1)S(1)}, u32[]{:S(2)}, u32[]{:S(2)}) %collective-permute-start.7) | collective-permute-done | bytes 131104 | tf_op jit(solution)/shard_map/ppermute | solution.py:560
  18.4 0.1 shard_map.139
  18.4 1.6 %collective-permute-start.8 = (bf16[384,256]{1,0:T(8,128)(2,1)S(1)}, bf16[384,256]{1,0:T(8,128)(2,1)S(1)}, u32[]{:S(2)}, u32[]{:S(2)}) collective-permute-start(bf16[384,256]{1,0:T(8,128)(2,1)S(1)} %get-tuple-element.27), channel_id=1, source_target_pairs={{0,1},{1,0},{2,3},{3,2},{4,5},{5,4},{6,7},{7,6},{8,9},{9,8},{10,11... | collective-permute-start | bytes 589832 | tf_op jit(solution)/shard_map/ppermute | solution.py:636
  20.1 0.0 collective-permute-start.9
  20.1 0.0 copy-done.2
  20.1 0.0 copy-done.5
  20.1 0.0 copy-done.7
  20.1 3.5 %shard_map.140 = (bf16[256,512]{1,0:T(8,128)(2,1)S(1)}, bf16[256,256]{1,0:T(8,128)(2,1)S(1)}, f32[4,256,128]{2,1,0:T(8,128)S(1)}, f32[4,4,256]{2,1,0:T(4,128)S(1)}, f32[4,4,256]{2,1,0:T(4,128)S(1)}) custom-call(s32[3,8]{1,0:T(4,128)S(1)} %bitcast.23, bf16[512,256]{1,0:T(8,128)(2,1)S(1)} %get-tuple-element.26.own, f32[1,256]{1,0:T(1,128)S(1)} %bitcast.26, ...), custom_call_target="tpu_custom_call" | custom-call | flops 939524096 | bytes 4194304 | tf_op jit(solution)/shard_map/pallas_call | solution.py:519
  23.6 1.9 %collective-permute-done.8.inner = bf16[384,256]{1,0:T(8,128)(2,1)S(1)} collective-permute-done((bf16[384,256]{1,0:T(8,128)(2,1)S(1)}, bf16[384,256]{1,0:T(8,128)(2,1)S(1)}, u32[]{:S(2)}, u32[]{:S(2)}) %collective-permute-start.8) | collective-permute-done | bytes 196640 | tf_op jit(solution)/shard_map/ppermute | solution.py:636
  25.5 1.3 %collective-permute-done.9.outer = bf16[384,256]{1,0:T(8,128)(2,1)S(1)} collective-permute-done((bf16[384,256]{1,0:T(8,128)(2,1)S(1)}, bf16[384,256]{1,0:T(8,128)(2,1)S(1)}, u32[]{:S(2)}, u32[]{:S(2)}) %collective-permute-start.9) | collective-permute-done | bytes 196640 | tf_op jit(solution)/shard_map/ppermute | solution.py:637
  26.8 0.0 copy-done
  26.8 0.0 copy-done.1
  26.8 0.0 copy-done.4
  26.8 0.0 copy-done.8
  26.8 4.5 %shard_map.141 = bf16[512,256]{1,0:T(8,128)(2,1)} custom-call(s32[3,8]{1,0:T(4,128)S(1)} %bitcast.24, bf16[512,256]{1,0:T(8,128)(2,1)S(1)} %get-tuple-element.26.own, bf16[384,256]{1,0:T(8,128)(2,1)S(1)} %collective-permute-done.8.inner, bf16[384,256]{1,0:T(8,128)(2,1)S(1)} %collective-permute-done.9.outer, f32[1,256]{1,0:T(1,128)S(1)} %bitcast.27, ...), custom_call_target="tpu_custom_call" | custom-call | flops 939524096 | bytes 4194304 | tf_op jit(solution)/shard_map/pallas_call | solution.py:519
  (6 shorter events, 0.1 us)
Async XLA Ops:
  0.0 1.7 %collective-permute-start = (bf16[512,256]{1,0:T(8,128)(2,1)}, bf16[512,256]{1,0:T(8,128)(2,1)S(1)}, u32[]{:S(2)}, u32[]{:S(2)}) collective-permute-start(bf16[512,256]{1,0:T(8,128)(2,1)} %bitcast.29), channel_id=1, source_target_pairs={{0,4},{4,0},{8,12},{12,8},{16,20},{20,16},{24,28},{28,24},{1,5},{5... | collective-permute-start | bytes 786440 | tf_op jit(solution)/shard_map/ppermute | solution.py:560
  1.8 5.7 %collective-permute-start.1 = (bf16[2,64,256]{2,1,0:T(8,128)(2,1)S(1)}, bf16[2,64,256]{2,1,0:T(8,128)(2,1)S(1)}, u32[]{:S(2)}, u32[]{:S(2)}) collective-permute-start(bf16[2,64,256]{2,1,0:T(8,128)(2,1)S(1)} %pad_maximum_fusion.1), channel_id=1, source_target_pairs={{0,24},{4,28},{8,16},{12,20},{16,8},{20,12},{24,0},{28,4},{1,25},{... | collective-permute-start | bytes 196616 | tf_op jit(solution)/shard_map/ppermute | solution.py:560
  4.3 4.3 %collective-permute-start.2 = (bf16[2,64,256]{2,1,0:T(8,128)(2,1)S(1)}, bf16[2,64,256]{2,1,0:T(8,128)(2,1)S(1)}, u32[]{:S(2)}, u32[]{:S(2)}) collective-permute-start(bf16[2,64,256]{2,1,0:T(8,128)(2,1)S(1)} %pad_maximum_fusion.2), channel_id=1, source_target_pairs={{0,16},{4,20},{8,24},{12,28},{16,0},{20,4},{24,8},{28,12},{1,17},{... | collective-permute-start | bytes 196616 | tf_op jit(solution)/shard_map/ppermute | solution.py:560
  4.9 4.3 %collective-permute-start.3 = (bf16[2,64,256]{2,1,0:T(8,128)(2,1)S(1)}, bf16[2,64,256]{2,1,0:T(8,128)(2,1)S(1)}, u32[]{:S(2)}, u32[]{:S(2)}) collective-permute-start(bf16[2,64,256]{2,1,0:T(8,128)(2,1)S(1)} %pad_maximum_fusion.3._), channel_id=1, source_target_pairs={{0,8},{4,12},{8,0},{12,4},{16,24},{20,28},{24,16},{28,20},{1,9},{5... | collective-permute-start | bytes 196616 | tf_op jit(solution)/shard_map/ppermute | solution.py:560
  5.5 3.7 %copy-start.3 = (bf16[256,256]{1,0:T(8,128)(2,1)S(1)}, bf16[256,256]{1,0:T(8,128)(2,1)}, u32[]{:S(2)}) copy-start(bf16[256,256]{1,0:T(8,128)(2,1)} %refs_7_.1) | copy-start | bytes 393220
  5.5 3.7 %copy-start.6 = (f32[256]{0:T(256)S(1)}, f32[256]{0:T(256)}, u32[]{:S(2)}) copy-start(f32[256]{0:T(256)} %param.15) | copy-start | bytes 3076
  5.5 14.6 %copy-start.2 = (bf16[256,768]{1,0:T(8,128)(2,1)S(1)}, bf16[256,768]{1,0:T(8,128)(2,1)}, u32[]{:S(2)}) copy-start(bf16[256,768]{1,0:T(8,128)(2,1)} %qkv.3) | copy-start | bytes 1179652
  5.5 14.6 %copy-start.5 = (s32[8,3]{0,1:T(4,128)S(1)}, s32[8,3]{0,1:T(4,128)}, u32[]{:S(2)}) copy-start(s32[8,3]{0,1:T(4,128)} %param.23) | copy-start | bytes 292
  5.5 14.6 %copy-start.7 = (f32[256]{0:T(256)S(1)}, f32[256]{0:T(256)}, u32[]{:S(2)}) copy-start(f32[256]{0:T(256)} %param.20) | copy-start | bytes 3076
  9.2 17.6 %copy-start = (bf16[256,1024]{1,0:T(8,128)(2,1)S(1)}, bf16[256,1024]{1,0:T(8,128)(2,1)}, u32[]{:S(2)}) copy-start(bf16[256,1024]{1,0:T(8,128)(2,1)} %mlp_up.1) | copy-start | bytes 1572868
  9.2 17.6 %copy-start.1 = (bf16[1024,256]{1,0:T(8,128)(2,1)S(1)}, bf16[1024,256]{1,0:T(8,128)(2,1)}, u32[]{:S(2)}) copy-start(bf16[1024,256]{1,0:T(8,128)(2,1)} %mlp_down.1) | copy-start | bytes 1572868
  9.2 17.5 %copy-start.4 = (bf16[256,256]{1,0:T(8,128)(2,1)S(1)}, bf16[256,256]{1,0:T(8,128)(2,1)}, u32[]{:S(2)}) copy-start(bf16[256,256]{1,0:T(8,128)(2,1)} %out_weight.1) | copy-start | bytes 393220
  9.2 17.5 %copy-start.8 = (f32[256]{0:T(256)S(1)}, f32[256]{0:T(256)}, u32[]{:S(2)}) copy-start(f32[256]{0:T(256)} %param.25) | copy-start | bytes 3076
  10.5 5.3 %collective-permute-start.4 = (bf16[2,64,256]{2,1,0:T(8,128)(2,1)S(1)}, bf16[2,64,256]{2,1,0:T(8,128)(2,1)S(1)}, u32[]{:S(2)}, u32[]{:S(2)}) collective-permute-start(bf16[2,64,256]{2,1,0:T(8,128)(2,1)S(1)} %get-tuple-element.23), channel_id=1, source_target_pairs={{0,24},{4,28},{8,16},{12,20},{16,8},{20,12},{24,0},{28,4},{1,25},{... | collective-permute-start | bytes 196616 | tf_op jit(solution)/shard_map/ppermute | solution.py:560
  12.1 4.4 %collective-permute-start.5 = (bf16[2,64,256]{2,1,0:T(8,128)(2,1)S(1)}, bf16[2,64,256]{2,1,0:T(8,128)(2,1)S(1)}, u32[]{:S(2)}, u32[]{:S(2)}) collective-permute-start(bf16[2,64,256]{2,1,0:T(8,128)(2,1)S(1)} %get-tuple-element.24), channel_id=1, source_target_pairs={{0,16},{4,20},{8,24},{12,28},{16,0},{20,4},{24,8},{28,12},{1,17},{... | collective-permute-start | bytes 196616 | tf_op jit(solution)/shard_map/ppermute | solution.py:560
  12.7 4.3 %collective-permute-start.6 = (bf16[2,64,256]{2,1,0:T(8,128)(2,1)S(1)}, bf16[2,64,256]{2,1,0:T(8,128)(2,1)S(1)}, u32[]{:S(2)}, u32[]{:S(2)}) collective-permute-start(bf16[2,64,256]{2,1,0:T(8,128)(2,1)S(1)} %get-tuple-element.25), channel_id=1, source_target_pairs={{0,8},{4,12},{8,0},{12,4},{16,24},{20,28},{24,16},{28,20},{1,9},{5... | collective-permute-start | bytes 196616 | tf_op jit(solution)/shard_map/ppermute | solution.py:560
  17.0 1.4 %collective-permute-start.7 = (bf16[256,256]{1,0:T(8,128)(2,1)S(1)}, bf16[256,256]{1,0:T(8,128)(2,1)S(1)}, u32[]{:S(2)}, u32[]{:S(2)}) collective-permute-start(bf16[256,256]{1,0:T(8,128)(2,1)S(1)} %shard_map.138), channel_id=1, source_target_pairs={{0,4},{4,0},{8,12},{12,8},{16,20},{20,16},{24,28},{28,24},{1,5},{5... | collective-permute-start | bytes 393224 | tf_op jit(solution)/shard_map/ppermute | solution.py:560
  18.4 7.0 %collective-permute-start.8 = (bf16[384,256]{1,0:T(8,128)(2,1)S(1)}, bf16[384,256]{1,0:T(8,128)(2,1)S(1)}, u32[]{:S(2)}, u32[]{:S(2)}) collective-permute-start(bf16[384,256]{1,0:T(8,128)(2,1)S(1)} %get-tuple-element.27), channel_id=1, source_target_pairs={{0,1},{1,0},{2,3},{3,2},{4,5},{5,4},{6,7},{7,6},{8,9},{9,8},{10,11... | collective-permute-start | bytes 589832 | tf_op jit(solution)/shard_map/ppermute | solution.py:636
  20.1 6.7 %collective-permute-start.9 = (bf16[384,256]{1,0:T(8,128)(2,1)S(1)}, bf16[384,256]{1,0:T(8,128)(2,1)S(1)}, u32[]{:S(2)}, u32[]{:S(2)}) collective-permute-start(bf16[384,256]{1,0:T(8,128)(2,1)S(1)} %get-tuple-element.28), channel_id=1, source_target_pairs={{0,4},{1,2},{2,1},{3,7},{4,0},{5,6},{6,5},{7,3},{8,12},{9,10},{10,... | collective-permute-start | bytes 589832 | tf_op jit(solution)/shard_map/ppermute | solution.py:637

commit v5 on v4

--- a/solution.py
+++ b/solution.py
@@ -210,7 +210,7 @@
 def phase_kernel(bins, heads, *refs):
     blocks = refs[: bins // 2]
     gain, weights_in, table, out_weight = refs[bins // 2 : bins // 2 + 4]
-    outs = refs[bins // 2 + 4 :]
+    passed, *kept = refs[bins // 2 + 4 :]
     chunk, width = blocks[0].shape[1:]
     head_dim = width // heads
     scale = LOG2E / math.sqrt(head_dim)
@@ -268,9 +268,8 @@
         for index, step in enumerate(steps):
             for slot in range(bins):
                 start = index * tile + slot * ROWS
-                outs[slot // 2][slot % 2, step * ROWS : (step + 1) * ROWS] = result[
-                    start : start + ROWS
-                ]
+                target = passed.at[slot // 2] if slot % 2 else kept[slot // 2]
+                target[step * ROWS : (step + 1) * ROWS] = result[start : start + ROWS]
 
     run_pipeline(
         units,
@@ -283,24 +282,22 @@
     finish(range(tiles))
 
 
-def pack_kernel(*refs):
-    give = refs[-1]
-    chunk = refs[0].shape[1]
-    for step, source in enumerate(refs[:-1]):
-        give[step * chunk : (step + 1) * chunk] = source[1]
+def join_kernel(taken, *refs):
+    half = len(refs) // 2
+    for step in range(half):
+        refs[half + step][0] = refs[step][...]
+        refs[half + step][1] = taken[step]
 
 
 def gather_kernel(plane, masks, *refs):
     half = len(masks) // 2
     got = refs[:half]
-    twin, residual, inner, outer = refs[half:]
+    residual, inner, outer = refs[half:]
     me = lax.axis_index("phase")
     chunk = got[0].shape[1]
-    for step in range(half):
-        start = pl.multiple_of((me ^ masks[2 * step]) * chunk, ROWS)
-        residual[pl.ds(start, chunk)] = got[step][0]
-        start = pl.multiple_of((me ^ masks[2 * step + 1]) * chunk, ROWS)
-        residual[pl.ds(start, chunk)] = twin[step * chunk : (step + 1) * chunk]
+    for slot, mask in enumerate(masks):
+        start = pl.multiple_of((me ^ mask) * chunk, ROWS)
+        residual[pl.ds(start, chunk)] = got[slot // 2][slot % 2]
     reach = inner.shape[0]
     extra = residual.shape[0] - reach
     odd = lax.axis_index("space") % 2
@@ -600,26 +597,29 @@
         flops=2 * 10**9,
         bytes_accessed=4 * 2**20,
     )
-    results = call(
+    passed, *kept = call(
         functools.partial(phase_kernel, bins, heads),
         [VMEM] * (half + 4),
-        [((2, chunk, width), bf16)] * half,
+        [((half, chunk, width), bf16)] + [((chunk, width), bf16)] * half,
         [*blocks, gain_first.reshape(1, width), phase_weights, phase_table, phase_out],
         12,
         flops=2 * tokens * width * 5 * width,
         bytes_accessed=2**20,
     )
+    results = call(
+        join_kernel,
+        [VMEM] * (half + 1),
+        [((2, chunk, width), bf16)] * half,
+        [swap(passed, 1), *kept],
+        4,
+    )
     got = [results[0]] + [swap(results[step], masks[2 * step]) for step in range(1, half)]
-    (give,) = call(
-        pack_kernel, [VMEM] * half, [((half * chunk, width), bf16)], [*got], 4
-    )
-    twin = swap(give, 1)
     reach = REACH * plane
     residual, inner, outer = call(
         functools.partial(gather_kernel, plane, masks),
-        [VMEM] * (half + 1),
+        [VMEM] * half,
         [((tokens, width), bf16), ((reach, width), bf16), ((reach, width), bf16)],
-        [*got, twin],
+        got,
         4,
     )
     count = lax.axis_size("space")

time: 31.7 us -> 31.6 us (level)
  no operation moved by 1% of the time
where the time goes in v5:
time: 31.6 us; the launch traced here: 31.2 us
  Pallas kernels  11.3 us (36%)
  waiting for transfers between devices  9.92 us (31%)
  starting transfers between devices  8.95 us (28%)
  local copies, waits for them, and re-layouts  0.87 us (3%)
    pallas_call x6, Pallas kernels, call(): pl.pallas_call(kernel, in_specs=specs, out_specs=[VMEM] * len(shapes), ou...  11.3 us
    ppermute x8, starting transfers between devices, swap(): return lax.ppermute(block, 'phase', [(i, i ^ mask) for i in range(bins)])  7.3 us
    ppermute x8, waiting for transfers between devices, swap(): return lax.ppermute(block, 'phase', [(i, i ^ mask) for i in range(bins)])  6.98 us
    ppermute x1, waiting for transfers between devices, local(): inner = lax.ppermute(inner, ('phase', 'space'), partners(0))  1.65 us
    ppermute x1, starting transfers between devices, local(): inner = lax.ppermute(inner, ('phase', 'space'), partners(0))  1.64 us
    ppermute x1, waiting for transfers between devices, local(): outer = lax.ppermute(outer, ('phase', 'space'), partners(1))  1.3 us
    another operation x2, local copies, waits for them, and re-layouts, piece(): jnp.stack([lax.dynamic_slice_in_dim(source, start, chunk, axis=0) for sou...  0.83 us
  transfers between devices with their start and end apart: 10, of which 9 were waited for; matrix products, arithmetic and copies ran while one was open for 3% of the time, Pallas kernels for 17%

profile of v5, /device:TPU:16, one launch (start us, length us, event | category | flops | bytes accessed | tf_op | source)
XLA Modules:
  0.0 31.2 jit_solution(1848408175821957656)
XLA Ops:
  0.0 0.0 collective-permute-start
  0.0 0.8 %dynamic-slice_bitcast_fusion.1 = (bf16[1,64,256]{2,1,0:T(8,128)(2,1)S(1)}, bf16[1,64,256]{2,1,0:T(8,128)(2,1)S(1)}, bf16[1,64,256]{2,1,0:T(8,128)(2,1)S(1)}, bf16[1,64,256]{2,1,0:T(8,128)(2,1)S(1)}) fusion(bf16[512,256]{1,0:T(8,128)(2,1)} %bitcast.30, s32[]{:T(128)S(6)} %select_n.19, s32[]{:T(128)S(6)} %select_n.18, s32[]{:T(128)S(6)} %select_n.17, ...), kind=kLoop, calls=%fused_computation.5 | loop fusion | bytes 262160 | tf_op jit(solution)/shard_map/stack | solution.py:564
  0.8 0.9 %collective-permute-done = bf16[512,256]{1,0:T(8,128)(2,1)S(1)} collective-permute-done((bf16[512,256]{1,0:T(8,128)(2,1)}, bf16[512,256]{1,0:T(8,128)(2,1)S(1)}, u32[]{:S(2)}, u32[]{:S(2)}) %collective-permute-start) | collective-permute-done | bytes 262176 | tf_op jit(solution)/shard_map/ppermute | solution.py:557
  1.8 2.5 %collective-permute-start.1 = (bf16[2,64,256]{2,1,0:T(8,128)(2,1)S(1)}, bf16[2,64,256]{2,1,0:T(8,128)(2,1)S(1)}, u32[]{:S(2)}, u32[]{:S(2)}) collective-permute-start(bf16[2,64,256]{2,1,0:T(8,128)(2,1)S(1)} %pad_maximum_fusion.1), channel_id=1, source_target_pairs={{0,24},{4,28},{8,16},{12,20},{16,8},{20,12},{24,0},{28,4},{1,25},{... | collective-permute-start | bytes 196616 | tf_op jit(solution)/shard_map/ppermute | solution.py:557
  4.3 0.6 %collective-permute-start.2 = (bf16[2,64,256]{2,1,0:T(8,128)(2,1)S(1)}, bf16[2,64,256]{2,1,0:T(8,128)(2,1)S(1)}, u32[]{:S(2)}, u32[]{:S(2)}) collective-permute-start(bf16[2,64,256]{2,1,0:T(8,128)(2,1)S(1)} %pad_maximum_fusion.2), channel_id=1, source_target_pairs={{0,16},{4,20},{8,24},{12,28},{16,0},{20,4},{24,8},{28,12},{1,17},{... | collective-permute-start | bytes 196616 | tf_op jit(solution)/shard_map/ppermute | solution.py:557
  4.9 0.6 %collective-permute-start.3 = (bf16[2,64,256]{2,1,0:T(8,128)(2,1)S(1)}, bf16[2,64,256]{2,1,0:T(8,128)(2,1)S(1)}, u32[]{:S(2)}, u32[]{:S(2)}) collective-permute-start(bf16[2,64,256]{2,1,0:T(8,128)(2,1)S(1)} %pad_maximum_fusion.3._), channel_id=1, source_target_pairs={{0,8},{4,12},{8,0},{12,4},{16,24},{20,28},{24,16},{28,20},{1,9},{5... | collective-permute-start | bytes 196616 | tf_op jit(solution)/shard_map/ppermute | solution.py:557
  5.5 0.0 copy-start.3
  5.5 0.0 copy-start.6
  5.5 0.0 copy-start.2
  5.5 0.0 copy-start.5
  5.5 0.0 copy-start.7
  5.5 2.0 %shard_map.136 = (bf16[768,256]{1,0:T(8,128)(2,1)S(1)}, f32[4,128,256]{2,1,0:T(8,128)S(1)}, f32[4,640,256]{2,1,0:T(8,128)S(1)}) custom-call(s32[8]{0:T(128)} %bin_phase_at.1, s32[3,8]{1,0:T(4,128)} %bitcast.22, f32[8,64]{1,0:T(8,128)} %window_bias_at.1, f32[8,8]{1,0:T(8,128)} %phase_bias_at.1, bf16[256,768]{1,0:T(8,128)(2,1)} %phase_qkv_at.1, ...), custom_call_target="tpu_custom_call" | custom-call | flops 2000000000 | bytes 4194304 | tf_op jit(solution)/shard_map/pallas_call | solution.py:516
  7.5 0.0 collective-permute-done.1.refs_1_
  7.5 1.1 %collective-permute-done.2.refs_2_ = bf16[2,64,256]{2,1,0:T(8,128)(2,1)S(1)} collective-permute-done((bf16[2,64,256]{2,1,0:T(8,128)(2,1)S(1)}, bf16[2,64,256]{2,1,0:T(8,128)(2,1)S(1)}, u32[]{:S(2)}, u32[]{:S(2)}) %collective-permute-start.2) | collective-permute-done | bytes 65568 | tf_op jit(solution)/shard_map/ppermute | solution.py:557
  8.6 0.6 %collective-permute-done.3.refs_3_ = bf16[2,64,256]{2,1,0:T(8,128)(2,1)S(1)} collective-permute-done((bf16[2,64,256]{2,1,0:T(8,128)(2,1)S(1)}, bf16[2,64,256]{2,1,0:T(8,128)(2,1)S(1)}, u32[]{:S(2)}, u32[]{:S(2)}) %collective-permute-start.3) | collective-permute-done | bytes 65568 | tf_op jit(solution)/shard_map/ppermute | solution.py:557
  9.2 0.0 copy-done.3
  9.2 0.0 copy-done.6
  9.2 0.0 copy-start
  9.2 0.0 copy-start.1
  9.2 0.0 copy-start.4
  9.2 0.0 copy-start.8
  9.2 1.3 %shard_map.137 = (bf16[4,64,256]{2,1,0:T(8,128)(2,1)S(1)}, bf16[64,256]{1,0:T(8,128)(2,1)S(1)}, bf16[64,256]{1,0:T(8,128)(2,1)S(1)}, bf16[64,256]{1,0:T(8,128)(2,1)S(1)}, bf16[64,256]{1,0:T(8,128)(2,1)S(1)}) custom-call(bf16[2,64,256]{2,1,0:T(8,128)(2,1)S(1)} %pad_maximum_fusion.refs_0_, bf16[2,64,256]{2,1,0:T(8,128)(2,1)S(1)} %collective-permute-done.1.refs_1_, ...), custom_call_target="tpu_custom_call" | custom-call | flops 335544320 | bytes 1048576 | tf_op jit(solution)/shard_map/pallas_call | solution.py:516
  10.5 0.1 collective-permute-start.4
  10.6 1.3 %collective-permute-done.4.taken = bf16[4,64,256]{2,1,0:T(8,128)(2,1)S(1)} collective-permute-done((bf16[4,64,256]{2,1,0:T(8,128)(2,1)S(1)}, bf16[4,64,256]{2,1,0:T(8,128)(2,1)S(1)}, u32[]{:S(2)}, u32[]{:S(2)}) %collective-permute-start.4) | collective-permute-done | bytes 131104 | tf_op jit(solution)/shard_map/ppermute | solution.py:557
  12.0 1.6 %collective-permute-start.5 = (bf16[2,64,256]{2,1,0:T(8,128)(2,1)S(1)}, bf16[2,64,256]{2,1,0:T(8,128)(2,1)S(1)}, u32[]{:S(2)}, u32[]{:S(2)}) collective-permute-start(bf16[2,64,256]{2,1,0:T(8,128)(2,1)S(1)} %get-tuple-element.33), channel_id=1, source_target_pairs={{0,24},{4,28},{8,16},{12,20},{16,8},{20,12},{24,0},{28,4},{1,25},{... | collective-permute-start | bytes 196616 | tf_op jit(solution)/shard_map/ppermute | solution.py:557
  13.5 0.6 %collective-permute-start.6 = (bf16[2,64,256]{2,1,0:T(8,128)(2,1)S(1)}, bf16[2,64,256]{2,1,0:T(8,128)(2,1)S(1)}, u32[]{:S(2)}, u32[]{:S(2)}) collective-permute-start(bf16[2,64,256]{2,1,0:T(8,128)(2,1)S(1)} %get-tuple-element.34), channel_id=1, source_target_pairs={{0,16},{4,20},{8,24},{12,28},{16,0},{20,4},{24,8},{28,12},{1,17},{... | collective-permute-start | bytes 196616 | tf_op jit(solution)/shard_map/ppermute | solution.py:557
  14.1 1.4 %collective-permute-start.7 = (bf16[2,64,256]{2,1,0:T(8,128)(2,1)S(1)}, bf16[2,64,256]{2,1,0:T(8,128)(2,1)S(1)}, u32[]{:S(2)}, u32[]{:S(2)}) collective-permute-start(bf16[2,64,256]{2,1,0:T(8,128)(2,1)S(1)} %get-tuple-element.35), channel_id=1, source_target_pairs={{0,8},{4,12},{8,0},{12,4},{16,24},{20,28},{24,16},{28,20},{1,9},{5... | collective-permute-start | bytes 196616 | tf_op jit(solution)/shard_map/ppermute | solution.py:557
  15.5 1.8 %collective-permute-done.5.refs_1_ = bf16[2,64,256]{2,1,0:T(8,128)(2,1)S(1)} collective-permute-done((bf16[2,64,256]{2,1,0:T(8,128)(2,1)S(1)}, bf16[2,64,256]{2,1,0:T(8,128)(2,1)S(1)}, u32[]{:S(2)}, u32[]{:S(2)}) %collective-permute-start.5) | collective-permute-done | bytes 65568 | tf_op jit(solution)/shard_map/ppermute | solution.py:557
  17.3 1.2 %collective-permute-done.6.refs_2_ = bf16[2,64,256]{2,1,0:T(8,128)(2,1)S(1)} collective-permute-done((bf16[2,64,256]{2,1,0:T(8,128)(2,1)S(1)}, bf16[2,64,256]{2,1,0:T(8,128)(2,1)S(1)}, u32[]{:S(2)}, u32[]{:S(2)}) %collective-permute-start.6) | collective-permute-done | bytes 65568 | tf_op jit(solution)/shard_map/ppermute | solution.py:557
  18.5 0.1 collective-permute-done.7.refs_3_
  18.5 0.1 shard_map.139
  18.6 1.6 %collective-permute-start.8 = (bf16[384,256]{1,0:T(8,128)(2,1)S(1)}, bf16[384,256]{1,0:T(8,128)(2,1)S(1)}, u32[]{:S(2)}, u32[]{:S(2)}) collective-permute-start(bf16[384,256]{1,0:T(8,128)(2,1)S(1)} %get-tuple-element.37), channel_id=1, source_target_pairs={{0,1},{1,0},{2,3},{3,2},{4,5},{5,4},{6,7},{7,6},{8,9},{9,8},{10,11... | collective-permute-start | bytes 589832 | tf_op jit(solution)/shard_map/ppermute | solution.py:636
  20.2 0.0 collective-permute-start.9
  20.2 0.0 copy-done.2
  20.2 0.0 copy-done.5
  20.2 0.0 copy-done.7
  20.3 3.4 %shard_map.140 = (bf16[256,512]{1,0:T(8,128)(2,1)S(1)}, bf16[256,256]{1,0:T(8,128)(2,1)S(1)}, f32[4,256,128]{2,1,0:T(8,128)S(1)}, f32[4,4,256]{2,1,0:T(4,128)S(1)}, f32[4,4,256]{2,1,0:T(4,128)S(1)}) custom-call(s32[3,8]{1,0:T(4,128)S(1)} %bitcast.23, bf16[512,256]{1,0:T(8,128)(2,1)S(1)} %get-tuple-element.36.own, f32[1,256]{1,0:T(1,128)S(1)} %bitcast.26, ...), custom_call_target="tpu_custom_call" | custom-call | flops 939524096 | bytes 4194304 | tf_op jit(solution)/shard_map/pallas_call | solution.py:516
  23.7 1.6 %collective-permute-done.8.inner = bf16[384,256]{1,0:T(8,128)(2,1)S(1)} collective-permute-done((bf16[384,256]{1,0:T(8,128)(2,1)S(1)}, bf16[384,256]{1,0:T(8,128)(2,1)S(1)}, u32[]{:S(2)}, u32[]{:S(2)}) %collective-permute-start.8) | collective-permute-done | bytes 196640 | tf_op jit(solution)/shard_map/ppermute | solution.py:636
  25.4 1.3 %collective-permute-done.9.outer = bf16[384,256]{1,0:T(8,128)(2,1)S(1)} collective-permute-done((bf16[384,256]{1,0:T(8,128)(2,1)S(1)}, bf16[384,256]{1,0:T(8,128)(2,1)S(1)}, u32[]{:S(2)}, u32[]{:S(2)}) %collective-permute-start.9) | collective-permute-done | bytes 196640 | tf_op jit(solution)/shard_map/ppermute | solution.py:637
  26.7 0.0 copy-done
  26.7 0.0 copy-done.1
  26.7 0.0 copy-done.4
  26.7 0.0 copy-done.8
  26.7 4.5 %shard_map.141 = bf16[512,256]{1,0:T(8,128)(2,1)} custom-call(s32[3,8]{1,0:T(4,128)S(1)} %bitcast.24, bf16[512,256]{1,0:T(8,128)(2,1)S(1)} %get-tuple-element.36.own, bf16[384,256]{1,0:T(8,128)(2,1)S(1)} %collective-permute-done.8.inner, bf16[384,256]{1,0:T(8,128)(2,1)S(1)} %collective-permute-done.9.outer, f32[1,256]{1,0:T(1,128)S(1)} %bitcast.27, ...), custom_call_target="tpu_custom_call" | custom-call | flops 939524096 | bytes 4194304 | tf_op jit(solution)/shard_map/pallas_call | solution.py:516
  (6 shorter events, 0.1 us)
Async XLA Ops:
  0.0 1.7 %collective-permute-start = (bf16[512,256]{1,0:T(8,128)(2,1)}, bf16[512,256]{1,0:T(8,128)(2,1)S(1)}, u32[]{:S(2)}, u32[]{:S(2)}) collective-permute-start(bf16[512,256]{1,0:T(8,128)(2,1)} %bitcast.29), channel_id=1, source_target_pairs={{0,4},{4,0},{8,12},{12,8},{16,20},{20,16},{24,28},{28,24},{1,5},{5... | collective-permute-start | bytes 786440 | tf_op jit(solution)/shard_map/ppermute | solution.py:557
  1.8 5.7 %collective-permute-start.1 = (bf16[2,64,256]{2,1,0:T(8,128)(2,1)S(1)}, bf16[2,64,256]{2,1,0:T(8,128)(2,1)S(1)}, u32[]{:S(2)}, u32[]{:S(2)}) collective-permute-start(bf16[2,64,256]{2,1,0:T(8,128)(2,1)S(1)} %pad_maximum_fusion.1), channel_id=1, source_target_pairs={{0,24},{4,28},{8,16},{12,20},{16,8},{20,12},{24,0},{28,4},{1,25},{... | collective-permute-start | bytes 196616 | tf_op jit(solution)/shard_map/ppermute | solution.py:557
  4.3 4.3 %collective-permute-start.2 = (bf16[2,64,256]{2,1,0:T(8,128)(2,1)S(1)}, bf16[2,64,256]{2,1,0:T(8,128)(2,1)S(1)}, u32[]{:S(2)}, u32[]{:S(2)}) collective-permute-start(bf16[2,64,256]{2,1,0:T(8,128)(2,1)S(1)} %pad_maximum_fusion.2), channel_id=1, source_target_pairs={{0,16},{4,20},{8,24},{12,28},{16,0},{20,4},{24,8},{28,12},{1,17},{... | collective-permute-start | bytes 196616 | tf_op jit(solution)/shard_map/ppermute | solution.py:557
  4.9 4.3 %collective-permute-start.3 = (bf16[2,64,256]{2,1,0:T(8,128)(2,1)S(1)}, bf16[2,64,256]{2,1,0:T(8,128)(2,1)S(1)}, u32[]{:S(2)}, u32[]{:S(2)}) collective-permute-start(bf16[2,64,256]{2,1,0:T(8,128)(2,1)S(1)} %pad_maximum_fusion.3._), channel_id=1, source_target_pairs={{0,8},{4,12},{8,0},{12,4},{16,24},{20,28},{24,16},{28,20},{1,9},{5... | collective-permute-start | bytes 196616 | tf_op jit(solution)/shard_map/ppermute | solution.py:557
  5.5 3.7 %copy-start.3 = (bf16[256,256]{1,0:T(8,128)(2,1)S(1)}, bf16[256,256]{1,0:T(8,128)(2,1)}, u32[]{:S(2)}) copy-start(bf16[256,256]{1,0:T(8,128)(2,1)} %refs_7_.1) | copy-start | bytes 393220
  5.5 3.7 %copy-start.6 = (f32[256]{0:T(256)S(1)}, f32[256]{0:T(256)}, u32[]{:S(2)}) copy-start(f32[256]{0:T(256)} %param.15) | copy-start | bytes 3076
  5.5 14.8 %copy-start.2 = (bf16[256,768]{1,0:T(8,128)(2,1)S(1)}, bf16[256,768]{1,0:T(8,128)(2,1)}, u32[]{:S(2)}) copy-start(bf16[256,768]{1,0:T(8,128)(2,1)} %qkv.3) | copy-start | bytes 1179652
  5.5 14.8 %copy-start.5 = (s32[8,3]{0,1:T(4,128)S(1)}, s32[8,3]{0,1:T(4,128)}, u32[]{:S(2)}) copy-start(s32[8,3]{0,1:T(4,128)} %param.23) | copy-start | bytes 292
  5.5 14.8 %copy-start.7 = (f32[256]{0:T(256)S(1)}, f32[256]{0:T(256)}, u32[]{:S(2)}) copy-start(f32[256]{0:T(256)} %param.20) | copy-start | bytes 3076
  9.2 17.5 %copy-start = (bf16[256,1024]{1,0:T(8,128)(2,1)S(1)}, bf16[256,1024]{1,0:T(8,128)(2,1)}, u32[]{:S(2)}) copy-start(bf16[256,1024]{1,0:T(8,128)(2,1)} %mlp_up.1) | copy-start | bytes 1572868
  9.2 17.5 %copy-start.1 = (bf16[1024,256]{1,0:T(8,128)(2,1)S(1)}, bf16[1024,256]{1,0:T(8,128)(2,1)}, u32[]{:S(2)}) copy-start(bf16[1024,256]{1,0:T(8,128)(2,1)} %mlp_down.1) | copy-start | bytes 1572868
  9.2 17.4 %copy-start.4 = (bf16[256,256]{1,0:T(8,128)(2,1)S(1)}, bf16[256,256]{1,0:T(8,128)(2,1)}, u32[]{:S(2)}) copy-start(bf16[256,256]{1,0:T(8,128)(2,1)} %out_weight.1) | copy-start | bytes 393220
  9.2 17.4 %copy-start.8 = (f32[256]{0:T(256)S(1)}, f32[256]{0:T(256)}, u32[]{:S(2)}) copy-start(f32[256]{0:T(256)} %param.25) | copy-start | bytes 3076
  10.5 1.4 %collective-permute-start.4 = (bf16[4,64,256]{2,1,0:T(8,128)(2,1)S(1)}, bf16[4,64,256]{2,1,0:T(8,128)(2,1)S(1)}, u32[]{:S(2)}, u32[]{:S(2)}) collective-permute-start(bf16[4,64,256]{2,1,0:T(8,128)(2,1)S(1)} %get-tuple-element.27), channel_id=1, source_target_pairs={{0,4},{4,0},{8,12},{12,8},{16,20},{20,16},{24,28},{28,24},{1,5},{5... | collective-permute-start | bytes 393224 | tf_op jit(solution)/shard_map/ppermute | solution.py:557
  12.0 5.3 %collective-permute-start.5 = (bf16[2,64,256]{2,1,0:T(8,128)(2,1)S(1)}, bf16[2,64,256]{2,1,0:T(8,128)(2,1)S(1)}, u32[]{:S(2)}, u32[]{:S(2)}) collective-permute-start(bf16[2,64,256]{2,1,0:T(8,128)(2,1)S(1)} %get-tuple-element.33), channel_id=1, source_target_pairs={{0,24},{4,28},{8,16},{12,20},{16,8},{20,12},{24,0},{28,4},{1,25},{... | collective-permute-start | bytes 196616 | tf_op jit(solution)/shard_map/ppermute | solution.py:557
  13.5 5.0 %collective-permute-start.6 = (bf16[2,64,256]{2,1,0:T(8,128)(2,1)S(1)}, bf16[2,64,256]{2,1,0:T(8,128)(2,1)S(1)}, u32[]{:S(2)}, u32[]{:S(2)}) collective-permute-start(bf16[2,64,256]{2,1,0:T(8,128)(2,1)S(1)} %get-tuple-element.34), channel_id=1, source_target_pairs={{0,16},{4,20},{8,24},{12,28},{16,0},{20,4},{24,8},{28,12},{1,17},{... | collective-permute-start | bytes 196616 | tf_op jit(solution)/shard_map/ppermute | solution.py:557
  14.1 4.4 %collective-permute-start.7 = (bf16[2,64,256]{2,1,0:T(8,128)(2,1)S(1)}, bf16[2,64,256]{2,1,0:T(8,128)(2,1)S(1)}, u32[]{:S(2)}, u32[]{:S(2)}) collective-permute-start(bf16[2,64,256]{2,1,0:T(8,128)(2,1)S(1)} %get-tuple-element.35), channel_id=1, source_target_pairs={{0,8},{4,12},{8,0},{12,4},{16,24},{20,28},{24,16},{28,20},{1,9},{5... | collective-permute-start | bytes 196616 | tf_op jit(solution)/shard_map/ppermute | solution.py:557
  18.6 6.8 %collective-permute-start.8 = (bf16[384,256]{1,0:T(8,128)(2,1)S(1)}, bf16[384,256]{1,0:T(8,128)(2,1)S(1)}, u32[]{:S(2)}, u32[]{:S(2)}) collective-permute-start(bf16[384,256]{1,0:T(8,128)(2,1)S(1)} %get-tuple-element.37), channel_id=1, source_target_pairs={{0,1},{1,0},{2,3},{3,2},{4,5},{5,4},{6,7},{7,6},{8,9},{9,8},{10,11... | collective-permute-start | bytes 589832 | tf_op jit(solution)/shard_map/ppermute | solution.py:636
  20.2 6.4 %collective-permute-start.9 = (bf16[384,256]{1,0:T(8,128)(2,1)S(1)}, bf16[384,256]{1,0:T(8,128)(2,1)S(1)}, u32[]{:S(2)}, u32[]{:S(2)}) collective-permute-start(bf16[384,256]{1,0:T(8,128)(2,1)S(1)} %get-tuple-element.38), channel_id=1, source_target_pairs={{0,4},{1,2},{2,1},{3,7},{4,0},{5,6},{6,5},{7,3},{8,12},{9,10},{10,... | collective-permute-start | bytes 589832 | tf_op jit(solution)/shard_map/ppermute | solution.py:637

commit v6 on v5

--- a/solution.py
+++ b/solution.py
@@ -417,11 +417,16 @@
     z_first = place * planes
     depth = lax.axis_size("space") * planes
     key_weight = qkv[:, width : 2 * width]
-    for source, at_end in ((inner, is_even), (outer, jnp.logical_not(is_even))):
-        normed = rms(source[...].astype(jnp.float32), gain)
+    normed = jnp.concatenate(
+        [rms(source[...].astype(jnp.float32), gain) for source in (inner, outer)], axis=0
+    )
+    keys = mm(normed, key_weight).astype(jnp.bfloat16)
+    values = mm(value_weight[...], normed, NT).astype(jnp.bfloat16)
+    for index, at_end in enumerate((is_even, jnp.logical_not(is_even))):
         rows = pl.ds(pl.multiple_of(jnp.where(at_end, reach, 0), plane), reach)
-        key_store[rows] = mm(normed, key_weight).astype(jnp.bfloat16)
-        value_store[:, rows] = mm(value_weight[...], normed, NT).astype(jnp.bfloat16)
+        part = slice(index * reach, (index + 1) * reach)
+        key_store[rows] = keys[part]
+        value_store[:, rows] = values[:, part]
     rim = list(range(REACH)) + list(range(REACH + planes, 2 * REACH + planes))
     ones = jnp.ones((ROWS, 2 * reach), jnp.bfloat16)
     frames = [frame_of(key_store, pair, head_dim, group) for pair in range(pairs)]
@@ -480,21 +485,16 @@
 
     run_pipeline(units, 2, first, second, third, lambda _: iter(()))
     mixed = [jnp.concatenate(parts[at * pairs : (at + 1) * pairs], axis=0) for at in range(planes)]
-    columns = width
     block = 2 * plane
 
     def mlp_steps(start):
         here = slice(start * plane, start * plane + block)
-        joined = jnp.concatenate(mixed[start : start + 2], axis=1) if 2 > 1 else mixed[start]
+        joined = jnp.concatenate(mixed[start : start + 2], axis=1)
         residual = own[here].astype(jnp.float32) + mm(joined, out_weight[...], TN)
         normed = rms(residual, gain_third[...])
         yield
-        hiddens = []
-        for first_column in range(0, mlp_up.shape[1], columns):
-            hidden = mm(normed, mlp_up[:, first_column : first_column + columns])
-            hiddens.append(gelu(hidden.astype(jnp.bfloat16)))
-            yield
-        hidden = jnp.concatenate(hiddens, axis=1)
+        hidden = gelu(mm(normed, mlp_up[...]).astype(jnp.bfloat16))
+        yield
         out[here] = (residual + mm(hidden, mlp_down[...])).astype(out.dtype)
 
     interleave(*(mlp_steps(start) for start in range(0, planes, 2)))

time: 31.6 us -> 31.4 us (level)
  no operation moved by 1% of the time
where the time goes in v6:
time: 31.4 us; the launch traced here: 31 us
  Pallas kernels  11.1 us (35%)
  waiting for transfers between devices  9.92 us (32%)
  starting transfers between devices  8.95 us (29%)
  local copies, waits for them, and re-layouts  0.87 us (3%)
    pallas_call x6, Pallas kernels, call(): pl.pallas_call(kernel, in_specs=specs, out_specs=[VMEM] * len(shapes), ou...  11.1 us
    ppermute x8, starting transfers between devices, swap(): return lax.ppermute(block, 'phase', [(i, i ^ mask) for i in range(bins)])  7.3 us
    ppermute x8, waiting for transfers between devices, swap(): return lax.ppermute(block, 'phase', [(i, i ^ mask) for i in range(bins)])  6.98 us
    ppermute x1, waiting for transfers between devices, local(): inner = lax.ppermute(inner, ('phase', 'space'), partners(0))  1.65 us
    ppermute x1, starting transfers between devices, local(): inner = lax.ppermute(inner, ('phase', 'space'), partners(0))  1.64 us
    ppermute x1, waiting for transfers between devices, local(): outer = lax.ppermute(outer, ('phase', 'space'), partners(1))  1.3 us
    another operation x2, local copies, waits for them, and re-layouts, piece(): jnp.stack([lax.dynamic_slice_in_dim(source, start, chunk, axis=0) for sou...  0.83 us
  transfers between devices with their start and end apart: 10, of which 9 were waited for; matrix products, arithmetic and copies ran while one was open for 3% of the time, Pallas kernels for 17%

profile of v6, /device:TPU:16, one launch (start us, length us, event | category | flops | bytes accessed | tf_op | source)
XLA Modules:
  0.0 31.0 jit_solution(9474501754499042156)
XLA Ops:
  0.0 0.0 collective-permute-start
  0.0 0.8 %dynamic-slice_bitcast_fusion.1 = (bf16[1,64,256]{2,1,0:T(8,128)(2,1)S(1)}, bf16[1,64,256]{2,1,0:T(8,128)(2,1)S(1)}, bf16[1,64,256]{2,1,0:T(8,128)(2,1)S(1)}, bf16[1,64,256]{2,1,0:T(8,128)(2,1)S(1)}) fusion(bf16[512,256]{1,0:T(8,128)(2,1)} %bitcast.30, s32[]{:T(128)S(6)} %select_n.19, s32[]{:T(128)S(6)} %select_n.18, s32[]{:T(128)S(6)} %select_n.17, ...), kind=kLoop, calls=%fused_computation.5 | loop fusion | bytes 262160 | tf_op jit(solution)/shard_map/stack | solution.py:564
  0.8 0.9 %collective-permute-done = bf16[512,256]{1,0:T(8,128)(2,1)S(1)} collective-permute-done((bf16[512,256]{1,0:T(8,128)(2,1)}, bf16[512,256]{1,0:T(8,128)(2,1)S(1)}, u32[]{:S(2)}, u32[]{:S(2)}) %collective-permute-start) | collective-permute-done | bytes 262176 | tf_op jit(solution)/shard_map/ppermute | solution.py:557
  1.8 2.5 %collective-permute-start.1 = (bf16[2,64,256]{2,1,0:T(8,128)(2,1)S(1)}, bf16[2,64,256]{2,1,0:T(8,128)(2,1)S(1)}, u32[]{:S(2)}, u32[]{:S(2)}) collective-permute-start(bf16[2,64,256]{2,1,0:T(8,128)(2,1)S(1)} %pad_maximum_fusion.1), channel_id=1, source_target_pairs={{0,24},{4,28},{8,16},{12,20},{16,8},{20,12},{24,0},{28,4},{1,25},{... | collective-permute-start | bytes 196616 | tf_op jit(solution)/shard_map/ppermute | solution.py:557
  4.3 0.6 %collective-permute-start.2 = (bf16[2,64,256]{2,1,0:T(8,128)(2,1)S(1)}, bf16[2,64,256]{2,1,0:T(8,128)(2,1)S(1)}, u32[]{:S(2)}, u32[]{:S(2)}) collective-permute-start(bf16[2,64,256]{2,1,0:T(8,128)(2,1)S(1)} %pad_maximum_fusion.2), channel_id=1, source_target_pairs={{0,16},{4,20},{8,24},{12,28},{16,0},{20,4},{24,8},{28,12},{1,17},{... | collective-permute-start | bytes 196616 | tf_op jit(solution)/shard_map/ppermute | solution.py:557
  4.9 0.6 %collective-permute-start.3 = (bf16[2,64,256]{2,1,0:T(8,128)(2,1)S(1)}, bf16[2,64,256]{2,1,0:T(8,128)(2,1)S(1)}, u32[]{:S(2)}, u32[]{:S(2)}) collective-permute-start(bf16[2,64,256]{2,1,0:T(8,128)(2,1)S(1)} %pad_maximum_fusion.3._), channel_id=1, source_target_pairs={{0,8},{4,12},{8,0},{12,4},{16,24},{20,28},{24,16},{28,20},{1,9},{5... | collective-permute-start | bytes 196616 | tf_op jit(solution)/shard_map/ppermute | solution.py:557
  5.5 0.0 copy-start.3
  5.5 0.0 copy-start.6
  5.5 0.0 copy-start.2
  5.5 0.0 copy-start.5
  5.5 0.0 copy-start.7
  5.5 2.0 %shard_map.136 = (bf16[768,256]{1,0:T(8,128)(2,1)S(1)}, f32[4,128,256]{2,1,0:T(8,128)S(1)}, f32[4,640,256]{2,1,0:T(8,128)S(1)}) custom-call(s32[8]{0:T(128)} %bin_phase_at.1, s32[3,8]{1,0:T(4,128)} %bitcast.22, f32[8,64]{1,0:T(8,128)} %window_bias_at.1, f32[8,8]{1,0:T(8,128)} %phase_bias_at.1, bf16[256,768]{1,0:T(8,128)(2,1)} %phase_qkv_at.1, ...), custom_call_target="tpu_custom_call" | custom-call | flops 2000000000 | bytes 4194304 | tf_op jit(solution)/shard_map/pallas_call | solution.py:516
  7.5 0.0 collective-permute-done.1.refs_1_
  7.5 1.1 %collective-permute-done.2.refs_2_ = bf16[2,64,256]{2,1,0:T(8,128)(2,1)S(1)} collective-permute-done((bf16[2,64,256]{2,1,0:T(8,128)(2,1)S(1)}, bf16[2,64,256]{2,1,0:T(8,128)(2,1)S(1)}, u32[]{:S(2)}, u32[]{:S(2)}) %collective-permute-start.2) | collective-permute-done | bytes 65568 | tf_op jit(solution)/shard_map/ppermute | solution.py:557
  8.6 0.6 %collective-permute-done.3.refs_3_ = bf16[2,64,256]{2,1,0:T(8,128)(2,1)S(1)} collective-permute-done((bf16[2,64,256]{2,1,0:T(8,128)(2,1)S(1)}, bf16[2,64,256]{2,1,0:T(8,128)(2,1)S(1)}, u32[]{:S(2)}, u32[]{:S(2)}) %collective-permute-start.3) | collective-permute-done | bytes 65568 | tf_op jit(solution)/shard_map/ppermute | solution.py:557
  9.2 0.0 copy-done.3
  9.2 0.0 copy-done.6
  9.2 0.0 copy-start
  9.2 0.0 copy-start.1
  9.2 0.0 copy-start.4
  9.2 0.0 copy-start.8
  9.2 1.3 %shard_map.137 = (bf16[4,64,256]{2,1,0:T(8,128)(2,1)S(1)}, bf16[64,256]{1,0:T(8,128)(2,1)S(1)}, bf16[64,256]{1,0:T(8,128)(2,1)S(1)}, bf16[64,256]{1,0:T(8,128)(2,1)S(1)}, bf16[64,256]{1,0:T(8,128)(2,1)S(1)}) custom-call(bf16[2,64,256]{2,1,0:T(8,128)(2,1)S(1)} %pad_maximum_fusion.refs_0_, bf16[2,64,256]{2,1,0:T(8,128)(2,1)S(1)} %collective-permute-done.1.refs_1_, ...), custom_call_target="tpu_custom_call" | custom-call | flops 335544320 | bytes 1048576 | tf_op jit(solution)/shard_map/pallas_call | solution.py:516
  10.5 0.1 collective-permute-start.4
  10.6 1.3 %collective-permute-done.4.taken = bf16[4,64,256]{2,1,0:T(8,128)(2,1)S(1)} collective-permute-done((bf16[4,64,256]{2,1,0:T(8,128)(2,1)S(1)}, bf16[4,64,256]{2,1,0:T(8,128)(2,1)S(1)}, u32[]{:S(2)}, u32[]{:S(2)}) %collective-permute-start.4) | collective-permute-done | bytes 131104 | tf_op jit(solution)/shard_map/ppermute | solution.py:557
  12.0 1.6 %collective-permute-start.5 = (bf16[2,64,256]{2,1,0:T(8,128)(2,1)S(1)}, bf16[2,64,256]{2,1,0:T(8,128)(2,1)S(1)}, u32[]{:S(2)}, u32[]{:S(2)}) collective-permute-start(bf16[2,64,256]{2,1,0:T(8,128)(2,1)S(1)} %get-tuple-element.33), channel_id=1, source_target_pairs={{0,24},{4,28},{8,16},{12,20},{16,8},{20,12},{24,0},{28,4},{1,25},{... | collective-permute-start | bytes 196616 | tf_op jit(solution)/shard_map/ppermute | solution.py:557
  13.5 0.6 %collective-permute-start.6 = (bf16[2,64,256]{2,1,0:T(8,128)(2,1)S(1)}, bf16[2,64,256]{2,1,0:T(8,128)(2,1)S(1)}, u32[]{:S(2)}, u32[]{:S(2)}) collective-permute-start(bf16[2,64,256]{2,1,0:T(8,128)(2,1)S(1)} %get-tuple-element.34), channel_id=1, source_target_pairs={{0,16},{4,20},{8,24},{12,28},{16,0},{20,4},{24,8},{28,12},{1,17},{... | collective-permute-start | bytes 196616 | tf_op jit(solution)/shard_map/ppermute | solution.py:557
  14.1 1.4 %collective-permute-start.7 = (bf16[2,64,256]{2,1,0:T(8,128)(2,1)S(1)}, bf16[2,64,256]{2,1,0:T(8,128)(2,1)S(1)}, u32[]{:S(2)}, u32[]{:S(2)}) collective-permute-start(bf16[2,64,256]{2,1,0:T(8,128)(2,1)S(1)} %get-tuple-element.35), channel_id=1, source_target_pairs={{0,8},{4,12},{8,0},{12,4},{16,24},{20,28},{24,16},{28,20},{1,9},{5... | collective-permute-start | bytes 196616 | tf_op jit(solution)/shard_map/ppermute | solution.py:557
  15.5 1.8 %collective-permute-done.5.refs_1_ = bf16[2,64,256]{2,1,0:T(8,128)(2,1)S(1)} collective-permute-done((bf16[2,64,256]{2,1,0:T(8,128)(2,1)S(1)}, bf16[2,64,256]{2,1,0:T(8,128)(2,1)S(1)}, u32[]{:S(2)}, u32[]{:S(2)}) %collective-permute-start.5) | collective-permute-done | bytes 65568 | tf_op jit(solution)/shard_map/ppermute | solution.py:557
  17.3 1.2 %collective-permute-done.6.refs_2_ = bf16[2,64,256]{2,1,0:T(8,128)(2,1)S(1)} collective-permute-done((bf16[2,64,256]{2,1,0:T(8,128)(2,1)S(1)}, bf16[2,64,256]{2,1,0:T(8,128)(2,1)S(1)}, u32[]{:S(2)}, u32[]{:S(2)}) %collective-permute-start.6) | collective-permute-done | bytes 65568 | tf_op jit(solution)/shard_map/ppermute | solution.py:557
  18.5 0.1 collective-permute-done.7.refs_3_
  18.5 0.1 shard_map.139
  18.6 1.6 %collective-permute-start.8 = (bf16[384,256]{1,0:T(8,128)(2,1)S(1)}, bf16[384,256]{1,0:T(8,128)(2,1)S(1)}, u32[]{:S(2)}, u32[]{:S(2)}) collective-permute-start(bf16[384,256]{1,0:T(8,128)(2,1)S(1)} %get-tuple-element.37), channel_id=1, source_target_pairs={{0,1},{1,0},{2,3},{3,2},{4,5},{5,4},{6,7},{7,6},{8,9},{9,8},{10,11... | collective-permute-start | bytes 589832 | tf_op jit(solution)/shard_map/ppermute | solution.py:636
  20.2 0.0 collective-permute-start.9
  20.2 0.0 copy-done.2
  20.2 0.0 copy-done.5
  20.2 0.0 copy-done.7
  20.3 3.4 %shard_map.140 = (bf16[256,512]{1,0:T(8,128)(2,1)S(1)}, bf16[256,256]{1,0:T(8,128)(2,1)S(1)}, f32[4,256,128]{2,1,0:T(8,128)S(1)}, f32[4,4,256]{2,1,0:T(4,128)S(1)}, f32[4,4,256]{2,1,0:T(4,128)S(1)}) custom-call(s32[3,8]{1,0:T(4,128)S(1)} %bitcast.23, bf16[512,256]{1,0:T(8,128)(2,1)S(1)} %get-tuple-element.36.own, f32[1,256]{1,0:T(1,128)S(1)} %bitcast.26, ...), custom_call_target="tpu_custom_call" | custom-call | flops 939524096 | bytes 4194304 | tf_op jit(solution)/shard_map/pallas_call | solution.py:516
  23.7 1.6 %collective-permute-done.8.inner = bf16[384,256]{1,0:T(8,128)(2,1)S(1)} collective-permute-done((bf16[384,256]{1,0:T(8,128)(2,1)S(1)}, bf16[384,256]{1,0:T(8,128)(2,1)S(1)}, u32[]{:S(2)}, u32[]{:S(2)}) %collective-permute-start.8) | collective-permute-done | bytes 196640 | tf_op jit(solution)/shard_map/ppermute | solution.py:636
  25.4 1.3 %collective-permute-done.9.outer = bf16[384,256]{1,0:T(8,128)(2,1)S(1)} collective-permute-done((bf16[384,256]{1,0:T(8,128)(2,1)S(1)}, bf16[384,256]{1,0:T(8,128)(2,1)S(1)}, u32[]{:S(2)}, u32[]{:S(2)}) %collective-permute-start.9) | collective-permute-done | bytes 196640 | tf_op jit(solution)/shard_map/ppermute | solution.py:637
  26.7 0.0 copy-done
  26.7 0.0 copy-done.1
  26.7 0.0 copy-done.4
  26.7 0.0 copy-done.8
  26.7 4.4 %shard_map.141 = bf16[512,256]{1,0:T(8,128)(2,1)} custom-call(s32[3,8]{1,0:T(4,128)S(1)} %bitcast.24, bf16[512,256]{1,0:T(8,128)(2,1)S(1)} %get-tuple-element.36.own, bf16[384,256]{1,0:T(8,128)(2,1)S(1)} %collective-permute-done.8.inner, bf16[384,256]{1,0:T(8,128)(2,1)S(1)} %collective-permute-done.9.outer, f32[1,256]{1,0:T(1,128)S(1)} %bitcast.27, ...), custom_call_target="tpu_custom_call" | custom-call | flops 939524096 | bytes 4194304 | tf_op jit(solution)/shard_map/pallas_call | solution.py:516
  (6 shorter events, 0.1 us)
Async XLA Ops:
  0.0 1.7 %collective-permute-start = (bf16[512,256]{1,0:T(8,128)(2,1)}, bf16[512,256]{1,0:T(8,128)(2,1)S(1)}, u32[]{:S(2)}, u32[]{:S(2)}) collective-permute-start(bf16[512,256]{1,0:T(8,128)(2,1)} %bitcast.29), channel_id=1, source_target_pairs={{0,4},{4,0},{8,12},{12,8},{16,20},{20,16},{24,28},{28,24},{1,5},{5... | collective-permute-start | bytes 786440 | tf_op jit(solution)/shard_map/ppermute | solution.py:557
  1.8 5.7 %collective-permute-start.1 = (bf16[2,64,256]{2,1,0:T(8,128)(2,1)S(1)}, bf16[2,64,256]{2,1,0:T(8,128)(2,1)S(1)}, u32[]{:S(2)}, u32[]{:S(2)}) collective-permute-start(bf16[2,64,256]{2,1,0:T(8,128)(2,1)S(1)} %pad_maximum_fusion.1), channel_id=1, source_target_pairs={{0,24},{4,28},{8,16},{12,20},{16,8},{20,12},{24,0},{28,4},{1,25},{... | collective-permute-start | bytes 196616 | tf_op jit(solution)/shard_map/ppermute | solution.py:557
  4.3 4.3 %collective-permute-start.2 = (bf16[2,64,256]{2,1,0:T(8,128)(2,1)S(1)}, bf16[2,64,256]{2,1,0:T(8,128)(2,1)S(1)}, u32[]{:S(2)}, u32[]{:S(2)}) collective-permute-start(bf16[2,64,256]{2,1,0:T(8,128)(2,1)S(1)} %pad_maximum_fusion.2), channel_id=1, source_target_pairs={{0,16},{4,20},{8,24},{12,28},{16,0},{20,4},{24,8},{28,12},{1,17},{... | collective-permute-start | bytes 196616 | tf_op jit(solution)/shard_map/ppermute | solution.py:557
  4.9 4.3 %collective-permute-start.3 = (bf16[2,64,256]{2,1,0:T(8,128)(2,1)S(1)}, bf16[2,64,256]{2,1,0:T(8,128)(2,1)S(1)}, u32[]{:S(2)}, u32[]{:S(2)}) collective-permute-start(bf16[2,64,256]{2,1,0:T(8,128)(2,1)S(1)} %pad_maximum_fusion.3._), channel_id=1, source_target_pairs={{0,8},{4,12},{8,0},{12,4},{16,24},{20,28},{24,16},{28,20},{1,9},{5... | collective-permute-start | bytes 196616 | tf_op jit(solution)/shard_map/ppermute | solution.py:557
  5.5 3.7 %copy-start.3 = (bf16[256,256]{1,0:T(8,128)(2,1)S(1)}, bf16[256,256]{1,0:T(8,128)(2,1)}, u32[]{:S(2)}) copy-start(bf16[256,256]{1,0:T(8,128)(2,1)} %refs_7_.1) | copy-start | bytes 393220
  5.5 3.7 %copy-start.6 = (f32[256]{0:T(256)S(1)}, f32[256]{0:T(256)}, u32[]{:S(2)}) copy-start(f32[256]{0:T(256)} %param.15) | copy-start | bytes 3076
  5.5 14.8 %copy-start.2 = (bf16[256,768]{1,0:T(8,128)(2,1)S(1)}, bf16[256,768]{1,0:T(8,128)(2,1)}, u32[]{:S(2)}) copy-start(bf16[256,768]{1,0:T(8,128)(2,1)} %qkv.3) | copy-start | bytes 1179652
  5.5 14.8 %copy-start.5 = (s32[8,3]{0,1:T(4,128)S(1)}, s32[8,3]{0,1:T(4,128)}, u32[]{:S(2)}) copy-start(s32[8,3]{0,1:T(4,128)} %param.23) | copy-start | bytes 292
  5.5 14.8 %copy-start.7 = (f32[256]{0:T(256)S(1)}, f32[256]{0:T(256)}, u32[]{:S(2)}) copy-start(f32[256]{0:T(256)} %param.20) | copy-start | bytes 3076
  9.2 17.5 %copy-start = (bf16[256,1024]{1,0:T(8,128)(2,1)S(1)}, bf16[256,1024]{1,0:T(8,128)(2,1)}, u32[]{:S(2)}) copy-start(bf16[256,1024]{1,0:T(8,128)(2,1)} %mlp_up.1) | copy-start | bytes 1572868
  9.2 17.5 %copy-start.1 = (bf16[1024,256]{1,0:T(8,128)(2,1)S(1)}, bf16[1024,256]{1,0:T(8,128)(2,1)}, u32[]{:S(2)}) copy-start(bf16[1024,256]{1,0:T(8,128)(2,1)} %mlp_down.1) | copy-start | bytes 1572868
  9.2 17.4 %copy-start.4 = (bf16[256,256]{1,0:T(8,128)(2,1)S(1)}, bf16[256,256]{1,0:T(8,128)(2,1)}, u32[]{:S(2)}) copy-start(bf16[256,256]{1,0:T(8,128)(2,1)} %out_weight.1) | copy-start | bytes 393220
  9.2 17.4 %copy-start.8 = (f32[256]{0:T(256)S(1)}, f32[256]{0:T(256)}, u32[]{:S(2)}) copy-start(f32[256]{0:T(256)} %param.25) | copy-start | bytes 3076
  10.5 1.4 %collective-permute-start.4 = (bf16[4,64,256]{2,1,0:T(8,128)(2,1)S(1)}, bf16[4,64,256]{2,1,0:T(8,128)(2,1)S(1)}, u32[]{:S(2)}, u32[]{:S(2)}) collective-permute-start(bf16[4,64,256]{2,1,0:T(8,128)(2,1)S(1)} %get-tuple-element.27), channel_id=1, source_target_pairs={{0,4},{4,0},{8,12},{12,8},{16,20},{20,16},{24,28},{28,24},{1,5},{5... | collective-permute-start | bytes 393224 | tf_op jit(solution)/shard_map/ppermute | solution.py:557
  12.0 5.3 %collective-permute-start.5 = (bf16[2,64,256]{2,1,0:T(8,128)(2,1)S(1)}, bf16[2,64,256]{2,1,0:T(8,128)(2,1)S(1)}, u32[]{:S(2)}, u32[]{:S(2)}) collective-permute-start(bf16[2,64,256]{2,1,0:T(8,128)(2,1)S(1)} %get-tuple-element.33), channel_id=1, source_target_pairs={{0,24},{4,28},{8,16},{12,20},{16,8},{20,12},{24,0},{28,4},{1,25},{... | collective-permute-start | bytes 196616 | tf_op jit(solution)/shard_map/ppermute | solution.py:557
  13.5 5.0 %collective-permute-start.6 = (bf16[2,64,256]{2,1,0:T(8,128)(2,1)S(1)}, bf16[2,64,256]{2,1,0:T(8,128)(2,1)S(1)}, u32[]{:S(2)}, u32[]{:S(2)}) collective-permute-start(bf16[2,64,256]{2,1,0:T(8,128)(2,1)S(1)} %get-tuple-element.34), channel_id=1, source_target_pairs={{0,16},{4,20},{8,24},{12,28},{16,0},{20,4},{24,8},{28,12},{1,17},{... | collective-permute-start | bytes 196616 | tf_op jit(solution)/shard_map/ppermute | solution.py:557
  14.1 4.4 %collective-permute-start.7 = (bf16[2,64,256]{2,1,0:T(8,128)(2,1)S(1)}, bf16[2,64,256]{2,1,0:T(8,128)(2,1)S(1)}, u32[]{:S(2)}, u32[]{:S(2)}) collective-permute-start(bf16[2,64,256]{2,1,0:T(8,128)(2,1)S(1)} %get-tuple-element.35), channel_id=1, source_target_pairs={{0,8},{4,12},{8,0},{12,4},{16,24},{20,28},{24,16},{28,20},{1,9},{5... | collective-permute-start | bytes 196616 | tf_op jit(solution)/shard_map/ppermute | solution.py:557
  18.6 6.8 %collective-permute-start.8 = (bf16[384,256]{1,0:T(8,128)(2,1)S(1)}, bf16[384,256]{1,0:T(8,128)(2,1)S(1)}, u32[]{:S(2)}, u32[]{:S(2)}) collective-permute-start(bf16[384,256]{1,0:T(8,128)(2,1)S(1)} %get-tuple-element.37), channel_id=1, source_target_pairs={{0,1},{1,0},{2,3},{3,2},{4,5},{5,4},{6,7},{7,6},{8,9},{9,8},{10,11... | collective-permute-start | bytes 589832 | tf_op jit(solution)/shard_map/ppermute | solution.py:636
  20.2 6.4 %collective-permute-start.9 = (bf16[384,256]{1,0:T(8,128)(2,1)S(1)}, bf16[384,256]{1,0:T(8,128)(2,1)S(1)}, u32[]{:S(2)}, u32[]{:S(2)}) collective-permute-start(bf16[384,256]{1,0:T(8,128)(2,1)S(1)} %get-tuple-element.38), channel_id=1, source_target_pairs={{0,4},{1,2},{2,1},{3,7},{4,0},{5,6},{6,5},{7,3},{8,12},{9,10},{10,... | collective-permute-start | bytes 589832 | tf_op jit(solution)/shard_map/ppermute | solution.py:637

commit v7 on v6

--- a/solution.py
+++ b/solution.py
@@ -503,7 +503,7 @@
 def gelu(values):
     half = values * 0.5
     cubic = values * (GELU_LINEAR + GELU_CUBIC * (values * values))
-    return half + half * jnp.tanh(cubic)
+    return half * (1.0 + jnp.tanh(cubic))
 
 
 VMEM = pl.BlockSpec(memory_space=pltpu.VMEM)
@@ -565,7 +565,7 @@
             [lax.dynamic_slice_in_dim(source, start, chunk, axis=0) for source in (own, twin)]
         )
 
-    masks = [0, 1] + [2 * step + part for step in range(half - 1, 0, -1) for part in range(2)]
+    masks = [0, 1] + [2 * step + part for step in [half - 1, *range(1, half - 1)] for part in range(2)]
     pieces = [piece(mask) for mask in masks[::2]]
     blocks = pieces[:1] + [swap(pieces[step], masks[2 * step]) for step in range(1, half)]
     corner = window_corner.T

time: 31.4 us -> 31 us (0.987)
  waiting for transfers between devices: 9.92 us -> 9.52 us
    ppermute x1, waiting for transfers between devices: 1.65 us -> 1.26 us  [local(): inner = lax.ppermute(inner, ('phase', 'space'), partners(0))]
  transfers between devices with their start and end apart: 10 -> 10, of which waited for: 9 -> 9; matrix products, arithmetic and copies ran while one was open for 3% -> 3% of each run, Pallas kernels for 17% -> 18%
where the time goes in v7:
time: 31 us; the launch traced here: 30.6 us
  Pallas kernels  11.1 us (36%)
  waiting for transfers between devices  9.52 us (31%)
  starting transfers between devices  8.95 us (29%)
  local copies, waits for them, and re-layouts  0.87 us (3%)
    pallas_call x6, Pallas kernels, call(): pl.pallas_call(kernel, in_specs=specs, out_specs=[VMEM] * len(shapes), ou...  11.1 us
    ppermute x8, starting transfers between devices, swap(): return lax.ppermute(block, 'phase', [(i, i ^ mask) for i in range(bins)])  7.3 us
    ppermute x8, waiting for transfers between devices, swap(): return lax.ppermute(block, 'phase', [(i, i ^ mask) for i in range(bins)])  6.95 us
    ppermute x1, starting transfers between devices, local(): inner = lax.ppermute(inner, ('phase', 'space'), partners(0))  1.64 us
    ppermute x1, waiting for transfers between devices, local(): outer = lax.ppermute(outer, ('phase', 'space'), partners(1))  1.3 us
    ppermute x1, waiting for transfers between devices, local(): inner = lax.ppermute(inner, ('phase', 'space'), partners(0))  1.26 us
    another operation x2, local copies, waits for them, and re-layouts, piece(): jnp.stack([lax.dynamic_slice_in_dim(source, start, chunk, axis=0) for sou...  0.83 us
  transfers between devices with their start and end apart: 10, of which 9 were waited for; matrix products, arithmetic and copies ran while one was open for 3% of the time, Pallas kernels for 18%

profile of v7, /device:TPU:16, one launch (start us, length us, event | category | flops | bytes accessed | tf_op | source)
XLA Modules:
  0.0 30.6 jit_solution(16947016999059052615)
XLA Ops:
  0.0 0.0 collective-permute-start
  0.0 0.8 %dynamic-slice_bitcast_fusion.1 = (bf16[1,64,256]{2,1,0:T(8,128)(2,1)S(1)}, bf16[1,64,256]{2,1,0:T(8,128)(2,1)S(1)}, bf16[1,64,256]{2,1,0:T(8,128)(2,1)S(1)}, bf16[1,64,256]{2,1,0:T(8,128)(2,1)S(1)}) fusion(bf16[512,256]{1,0:T(8,128)(2,1)} %bitcast.30, s32[]{:T(128)S(6)} %select_n.19, s32[]{:T(128)S(6)} %select_n.18, s32[]{:T(128)S(6)} %select_n.17, ...), kind=kLoop, calls=%fused_computation.5 | loop fusion | bytes 262160 | tf_op jit(solution)/shard_map/stack | solution.py:564
  0.8 0.9 %collective-permute-done = bf16[512,256]{1,0:T(8,128)(2,1)S(1)} collective-permute-done((bf16[512,256]{1,0:T(8,128)(2,1)}, bf16[512,256]{1,0:T(8,128)(2,1)S(1)}, u32[]{:S(2)}, u32[]{:S(2)}) %collective-permute-start) | collective-permute-done | bytes 262176 | tf_op jit(solution)/shard_map/ppermute | solution.py:557
  1.8 2.5 %collective-permute-start.1 = (bf16[2,64,256]{2,1,0:T(8,128)(2,1)S(1)}, bf16[2,64,256]{2,1,0:T(8,128)(2,1)S(1)}, u32[]{:S(2)}, u32[]{:S(2)}) collective-permute-start(bf16[2,64,256]{2,1,0:T(8,128)(2,1)S(1)} %pad_maximum_fusion.1), channel_id=1, source_target_pairs={{0,24},{4,28},{8,16},{12,20},{16,8},{20,12},{24,0},{28,4},{1,25},{... | collective-permute-start | bytes 196616 | tf_op jit(solution)/shard_map/ppermute | solution.py:557
  4.3 0.6 %collective-permute-start.2 = (bf16[2,64,256]{2,1,0:T(8,128)(2,1)S(1)}, bf16[2,64,256]{2,1,0:T(8,128)(2,1)S(1)}, u32[]{:S(2)}, u32[]{:S(2)}) collective-permute-start(bf16[2,64,256]{2,1,0:T(8,128)(2,1)S(1)} %pad_maximum_fusion.2), channel_id=1, source_target_pairs={{0,8},{4,12},{8,0},{12,4},{16,24},{20,28},{24,16},{28,20},{1,9},{5... | collective-permute-start | bytes 196616 | tf_op jit(solution)/shard_map/ppermute | solution.py:557
  4.9 0.6 %collective-permute-start.3 = (bf16[2,64,256]{2,1,0:T(8,128)(2,1)S(1)}, bf16[2,64,256]{2,1,0:T(8,128)(2,1)S(1)}, u32[]{:S(2)}, u32[]{:S(2)}) collective-permute-start(bf16[2,64,256]{2,1,0:T(8,128)(2,1)S(1)} %pad_maximum_fusion.3._), channel_id=1, source_target_pairs={{0,16},{4,20},{8,24},{12,28},{16,0},{20,4},{24,8},{28,12},{1,17},{... | collective-permute-start | bytes 196616 | tf_op jit(solution)/shard_map/ppermute | solution.py:557
  5.5 0.0 copy-start.3
  5.5 0.0 copy-start.6
  5.5 0.0 copy-start.2
  5.5 0.0 copy-start.5
  5.5 0.0 copy-start.7
  5.5 2.0 %shard_map.136 = (bf16[768,256]{1,0:T(8,128)(2,1)S(1)}, f32[4,128,256]{2,1,0:T(8,128)S(1)}, f32[4,640,256]{2,1,0:T(8,128)S(1)}) custom-call(s32[8]{0:T(128)} %bin_phase_at.1, s32[3,8]{1,0:T(4,128)} %bitcast.22, f32[8,64]{1,0:T(8,128)} %window_bias_at.1, f32[8,8]{1,0:T(8,128)} %phase_bias_at.1, bf16[256,768]{1,0:T(8,128)(2,1)} %phase_qkv_at.1, ...), custom_call_target="tpu_custom_call" | custom-call | flops 2000000000 | bytes 4194304 | tf_op jit(solution)/shard_map/pallas_call | solution.py:516
  7.5 0.0 collective-permute-done.1.refs_1_
  7.5 1.1 %collective-permute-done.2.refs_2_ = bf16[2,64,256]{2,1,0:T(8,128)(2,1)S(1)} collective-permute-done((bf16[2,64,256]{2,1,0:T(8,128)(2,1)S(1)}, bf16[2,64,256]{2,1,0:T(8,128)(2,1)S(1)}, u32[]{:S(2)}, u32[]{:S(2)}) %collective-permute-start.2) | collective-permute-done | bytes 65568 | tf_op jit(solution)/shard_map/ppermute | solution.py:557
  8.6 0.6 %collective-permute-done.3.refs_3_ = bf16[2,64,256]{2,1,0:T(8,128)(2,1)S(1)} collective-permute-done((bf16[2,64,256]{2,1,0:T(8,128)(2,1)S(1)}, bf16[2,64,256]{2,1,0:T(8,128)(2,1)S(1)}, u32[]{:S(2)}, u32[]{:S(2)}) %collective-permute-start.3) | collective-permute-done | bytes 65568 | tf_op jit(solution)/shard_map/ppermute | solution.py:557
  9.2 0.0 copy-done.3
  9.2 0.0 copy-done.6
  9.2 0.0 copy-start
  9.2 0.0 copy-start.1
  9.2 0.0 copy-start.4
  9.3 0.0 copy-start.8
  9.3 1.3 %shard_map.137 = (bf16[4,64,256]{2,1,0:T(8,128)(2,1)S(1)}, bf16[64,256]{1,0:T(8,128)(2,1)S(1)}, bf16[64,256]{1,0:T(8,128)(2,1)S(1)}, bf16[64,256]{1,0:T(8,128)(2,1)S(1)}, bf16[64,256]{1,0:T(8,128)(2,1)S(1)}) custom-call(bf16[2,64,256]{2,1,0:T(8,128)(2,1)S(1)} %pad_maximum_fusion.refs_0_, bf16[2,64,256]{2,1,0:T(8,128)(2,1)S(1)} %collective-permute-done.1.refs_1_, ...), custom_call_target="tpu_custom_call" | custom-call | flops 335544320 | bytes 1048576 | tf_op jit(solution)/shard_map/pallas_call | solution.py:516
  10.6 0.1 collective-permute-start.4
  10.6 1.3 %collective-permute-done.4.taken = bf16[4,64,256]{2,1,0:T(8,128)(2,1)S(1)} collective-permute-done((bf16[4,64,256]{2,1,0:T(8,128)(2,1)S(1)}, bf16[4,64,256]{2,1,0:T(8,128)(2,1)S(1)}, u32[]{:S(2)}, u32[]{:S(2)}) %collective-permute-start.4) | collective-permute-done | bytes 131104 | tf_op jit(solution)/shard_map/ppermute | solution.py:557
  12.0 1.6 %collective-permute-start.5 = (bf16[2,64,256]{2,1,0:T(8,128)(2,1)S(1)}, bf16[2,64,256]{2,1,0:T(8,128)(2,1)S(1)}, u32[]{:S(2)}, u32[]{:S(2)}) collective-permute-start(bf16[2,64,256]{2,1,0:T(8,128)(2,1)S(1)} %get-tuple-element.33), channel_id=1, source_target_pairs={{0,24},{4,28},{8,16},{12,20},{16,8},{20,12},{24,0},{28,4},{1,25},{... | collective-permute-start | bytes 196616 | tf_op jit(solution)/shard_map/ppermute | solution.py:557
  13.6 0.5 %collective-permute-start.6 = (bf16[2,64,256]{2,1,0:T(8,128)(2,1)S(1)}, bf16[2,64,256]{2,1,0:T(8,128)(2,1)S(1)}, u32[]{:S(2)}, u32[]{:S(2)}) collective-permute-start(bf16[2,64,256]{2,1,0:T(8,128)(2,1)S(1)} %get-tuple-element.34), channel_id=1, source_target_pairs={{0,8},{4,12},{8,0},{12,4},{16,24},{20,28},{24,16},{28,20},{1,9},{5... | collective-permute-start | bytes 196616 | tf_op jit(solution)/shard_map/ppermute | solution.py:557
  14.1 1.5 %collective-permute-start.7 = (bf16[2,64,256]{2,1,0:T(8,128)(2,1)S(1)}, bf16[2,64,256]{2,1,0:T(8,128)(2,1)S(1)}, u32[]{:S(2)}, u32[]{:S(2)}) collective-permute-start(bf16[2,64,256]{2,1,0:T(8,128)(2,1)S(1)} %get-tuple-element.35), channel_id=1, source_target_pairs={{0,16},{4,20},{8,24},{12,28},{16,0},{20,4},{24,8},{28,12},{1,17},{... | collective-permute-start | bytes 196616 | tf_op jit(solution)/shard_map/ppermute | solution.py:557
  15.5 2.1 %collective-permute-done.5.refs_1_ = bf16[2,64,256]{2,1,0:T(8,128)(2,1)S(1)} collective-permute-done((bf16[2,64,256]{2,1,0:T(8,128)(2,1)S(1)}, bf16[2,64,256]{2,1,0:T(8,128)(2,1)S(1)}, u32[]{:S(2)}, u32[]{:S(2)}) %collective-permute-start.5) | collective-permute-done | bytes 65568 | tf_op jit(solution)/shard_map/ppermute | solution.py:557
  17.6 0.2 collective-permute-done.6.refs_2_
  17.8 0.7 %collective-permute-done.7.refs_3_ = bf16[2,64,256]{2,1,0:T(8,128)(2,1)S(1)} collective-permute-done((bf16[2,64,256]{2,1,0:T(8,128)(2,1)S(1)}, bf16[2,64,256]{2,1,0:T(8,128)(2,1)S(1)}, u32[]{:S(2)}, u32[]{:S(2)}) %collective-permute-start.7) | collective-permute-done | bytes 65568 | tf_op jit(solution)/shard_map/ppermute | solution.py:557
  18.5 0.1 shard_map.139
  18.6 1.6 %collective-permute-start.8 = (bf16[384,256]{1,0:T(8,128)(2,1)S(1)}, bf16[384,256]{1,0:T(8,128)(2,1)S(1)}, u32[]{:S(2)}, u32[]{:S(2)}) collective-permute-start(bf16[384,256]{1,0:T(8,128)(2,1)S(1)} %get-tuple-element.37), channel_id=1, source_target_pairs={{0,1},{1,0},{2,3},{3,2},{4,5},{5,4},{6,7},{7,6},{8,9},{9,8},{10,11... | collective-permute-start | bytes 589832 | tf_op jit(solution)/shard_map/ppermute | solution.py:636
  20.2 0.0 collective-permute-start.9
  20.2 0.0 copy-done.2
  20.2 0.0 copy-done.5
  20.2 0.0 copy-done.7
  20.2 3.4 %shard_map.140 = (bf16[256,512]{1,0:T(8,128)(2,1)S(1)}, bf16[256,256]{1,0:T(8,128)(2,1)S(1)}, f32[4,256,128]{2,1,0:T(8,128)S(1)}, f32[4,4,256]{2,1,0:T(4,128)S(1)}, f32[4,4,256]{2,1,0:T(4,128)S(1)}) custom-call(s32[3,8]{1,0:T(4,128)S(1)} %bitcast.23, bf16[512,256]{1,0:T(8,128)(2,1)S(1)} %get-tuple-element.36.own, f32[1,256]{1,0:T(1,128)S(1)} %bitcast.26, ...), custom_call_target="tpu_custom_call" | custom-call | flops 939524096 | bytes 4194304 | tf_op jit(solution)/shard_map/pallas_call | solution.py:516
  23.7 1.3 %collective-permute-done.8.inner = bf16[384,256]{1,0:T(8,128)(2,1)S(1)} collective-permute-done((bf16[384,256]{1,0:T(8,128)(2,1)S(1)}, bf16[384,256]{1,0:T(8,128)(2,1)S(1)}, u32[]{:S(2)}, u32[]{:S(2)}) %collective-permute-start.8) | collective-permute-done | bytes 196640 | tf_op jit(solution)/shard_map/ppermute | solution.py:636
  24.9 1.3 %collective-permute-done.9.outer = bf16[384,256]{1,0:T(8,128)(2,1)S(1)} collective-permute-done((bf16[384,256]{1,0:T(8,128)(2,1)S(1)}, bf16[384,256]{1,0:T(8,128)(2,1)S(1)}, u32[]{:S(2)}, u32[]{:S(2)}) %collective-permute-start.9) | collective-permute-done | bytes 196640 | tf_op jit(solution)/shard_map/ppermute | solution.py:637
  26.2 0.0 copy-done
  26.2 0.0 copy-done.1
  26.2 0.0 copy-done.4
  26.3 0.0 copy-done.8
  26.3 4.4 %shard_map.141 = bf16[512,256]{1,0:T(8,128)(2,1)} custom-call(s32[3,8]{1,0:T(4,128)S(1)} %bitcast.24, bf16[512,256]{1,0:T(8,128)(2,1)S(1)} %get-tuple-element.36.own, bf16[384,256]{1,0:T(8,128)(2,1)S(1)} %collective-permute-done.8.inner, bf16[384,256]{1,0:T(8,128)(2,1)S(1)} %collective-permute-done.9.outer, f32[1,256]{1,0:T(1,128)S(1)} %bitcast.27, ...), custom_call_target="tpu_custom_call" | custom-call | flops 939524096 | bytes 4194304 | tf_op jit(solution)/shard_map/pallas_call | solution.py:516
  (6 shorter events, 0.1 us)
Async XLA Ops:
  0.0 1.7 %collective-permute-start = (bf16[512,256]{1,0:T(8,128)(2,1)}, bf16[512,256]{1,0:T(8,128)(2,1)S(1)}, u32[]{:S(2)}, u32[]{:S(2)}) collective-permute-start(bf16[512,256]{1,0:T(8,128)(2,1)} %bitcast.29), channel_id=1, source_target_pairs={{0,4},{4,0},{8,12},{12,8},{16,20},{20,16},{24,28},{28,24},{1,5},{5... | collective-permute-start | bytes 786440 | tf_op jit(solution)/shard_map/ppermute | solution.py:557
  1.8 5.7 %collective-permute-start.1 = (bf16[2,64,256]{2,1,0:T(8,128)(2,1)S(1)}, bf16[2,64,256]{2,1,0:T(8,128)(2,1)S(1)}, u32[]{:S(2)}, u32[]{:S(2)}) collective-permute-start(bf16[2,64,256]{2,1,0:T(8,128)(2,1)S(1)} %pad_maximum_fusion.1), channel_id=1, source_target_pairs={{0,24},{4,28},{8,16},{12,20},{16,8},{20,12},{24,0},{28,4},{1,25},{... | collective-permute-start | bytes 196616 | tf_op jit(solution)/shard_map/ppermute | solution.py:557
  4.3 4.3 %collective-permute-start.2 = (bf16[2,64,256]{2,1,0:T(8,128)(2,1)S(1)}, bf16[2,64,256]{2,1,0:T(8,128)(2,1)S(1)}, u32[]{:S(2)}, u32[]{:S(2)}) collective-permute-start(bf16[2,64,256]{2,1,0:T(8,128)(2,1)S(1)} %pad_maximum_fusion.2), channel_id=1, source_target_pairs={{0,8},{4,12},{8,0},{12,4},{16,24},{20,28},{24,16},{28,20},{1,9},{5... | collective-permute-start | bytes 196616 | tf_op jit(solution)/shard_map/ppermute | solution.py:557
  4.9 4.3 %collective-permute-start.3 = (bf16[2,64,256]{2,1,0:T(8,128)(2,1)S(1)}, bf16[2,64,256]{2,1,0:T(8,128)(2,1)S(1)}, u32[]{:S(2)}, u32[]{:S(2)}) collective-permute-start(bf16[2,64,256]{2,1,0:T(8,128)(2,1)S(1)} %pad_maximum_fusion.3._), channel_id=1, source_target_pairs={{0,16},{4,20},{8,24},{12,28},{16,0},{20,4},{24,8},{28,12},{1,17},{... | collective-permute-start | bytes 196616 | tf_op jit(solution)/shard_map/ppermute | solution.py:557
  5.5 3.8 %copy-start.3 = (bf16[256,256]{1,0:T(8,128)(2,1)S(1)}, bf16[256,256]{1,0:T(8,128)(2,1)}, u32[]{:S(2)}) copy-start(bf16[256,256]{1,0:T(8,128)(2,1)} %refs_7_.1) | copy-start | bytes 393220
  5.5 3.8 %copy-start.6 = (f32[256]{0:T(256)S(1)}, f32[256]{0:T(256)}, u32[]{:S(2)}) copy-start(f32[256]{0:T(256)} %param.15) | copy-start | bytes 3076
  5.5 14.7 %copy-start.2 = (bf16[256,768]{1,0:T(8,128)(2,1)S(1)}, bf16[256,768]{1,0:T(8,128)(2,1)}, u32[]{:S(2)}) copy-start(bf16[256,768]{1,0:T(8,128)(2,1)} %qkv.3) | copy-start | bytes 1179652
  5.5 14.7 %copy-start.5 = (s32[8,3]{0,1:T(4,128)S(1)}, s32[8,3]{0,1:T(4,128)}, u32[]{:S(2)}) copy-start(s32[8,3]{0,1:T(4,128)} %param.23) | copy-start | bytes 292
  5.5 14.7 %copy-start.7 = (f32[256]{0:T(256)S(1)}, f32[256]{0:T(256)}, u32[]{:S(2)}) copy-start(f32[256]{0:T(256)} %param.20) | copy-start | bytes 3076
  9.2 17.0 %copy-start = (bf16[256,1024]{1,0:T(8,128)(2,1)S(1)}, bf16[256,1024]{1,0:T(8,128)(2,1)}, u32[]{:S(2)}) copy-start(bf16[256,1024]{1,0:T(8,128)(2,1)} %mlp_up.1) | copy-start | bytes 1572868
  9.2 17.0 %copy-start.1 = (bf16[1024,256]{1,0:T(8,128)(2,1)S(1)}, bf16[1024,256]{1,0:T(8,128)(2,1)}, u32[]{:S(2)}) copy-start(bf16[1024,256]{1,0:T(8,128)(2,1)} %mlp_down.1) | copy-start | bytes 1572868
  9.2 17.0 %copy-start.4 = (bf16[256,256]{1,0:T(8,128)(2,1)S(1)}, bf16[256,256]{1,0:T(8,128)(2,1)}, u32[]{:S(2)}) copy-start(bf16[256,256]{1,0:T(8,128)(2,1)} %out_weight.1) | copy-start | bytes 393220
  9.3 17.0 %copy-start.8 = (f32[256]{0:T(256)S(1)}, f32[256]{0:T(256)}, u32[]{:S(2)}) copy-start(f32[256]{0:T(256)} %param.25) | copy-start | bytes 3076
  10.6 1.4 %collective-permute-start.4 = (bf16[4,64,256]{2,1,0:T(8,128)(2,1)S(1)}, bf16[4,64,256]{2,1,0:T(8,128)(2,1)S(1)}, u32[]{:S(2)}, u32[]{:S(2)}) collective-permute-start(bf16[4,64,256]{2,1,0:T(8,128)(2,1)S(1)} %get-tuple-element.27), channel_id=1, source_target_pairs={{0,4},{4,0},{8,12},{12,8},{16,20},{20,16},{24,28},{28,24},{1,5},{5... | collective-permute-start | bytes 393224 | tf_op jit(solution)/shard_map/ppermute | solution.py:557
  12.0 5.6 %collective-permute-start.5 = (bf16[2,64,256]{2,1,0:T(8,128)(2,1)S(1)}, bf16[2,64,256]{2,1,0:T(8,128)(2,1)S(1)}, u32[]{:S(2)}, u32[]{:S(2)}) collective-permute-start(bf16[2,64,256]{2,1,0:T(8,128)(2,1)S(1)} %get-tuple-element.33), channel_id=1, source_target_pairs={{0,24},{4,28},{8,16},{12,20},{16,8},{20,12},{24,0},{28,4},{1,25},{... | collective-permute-start | bytes 196616 | tf_op jit(solution)/shard_map/ppermute | solution.py:557
  13.6 4.3 %collective-permute-start.6 = (bf16[2,64,256]{2,1,0:T(8,128)(2,1)S(1)}, bf16[2,64,256]{2,1,0:T(8,128)(2,1)S(1)}, u32[]{:S(2)}, u32[]{:S(2)}) collective-permute-start(bf16[2,64,256]{2,1,0:T(8,128)(2,1)S(1)} %get-tuple-element.34), channel_id=1, source_target_pairs={{0,8},{4,12},{8,0},{12,4},{16,24},{20,28},{24,16},{28,20},{1,9},{5... | collective-permute-start | bytes 196616 | tf_op jit(solution)/shard_map/ppermute | solution.py:557
  14.1 4.4 %collective-permute-start.7 = (bf16[2,64,256]{2,1,0:T(8,128)(2,1)S(1)}, bf16[2,64,256]{2,1,0:T(8,128)(2,1)S(1)}, u32[]{:S(2)}, u32[]{:S(2)}) collective-permute-start(bf16[2,64,256]{2,1,0:T(8,128)(2,1)S(1)} %get-tuple-element.35), channel_id=1, source_target_pairs={{0,16},{4,20},{8,24},{12,28},{16,0},{20,4},{24,8},{28,12},{1,17},{... | collective-permute-start | bytes 196616 | tf_op jit(solution)/shard_map/ppermute | solution.py:557
  18.6 6.4 %collective-permute-start.8 = (bf16[384,256]{1,0:T(8,128)(2,1)S(1)}, bf16[384,256]{1,0:T(8,128)(2,1)S(1)}, u32[]{:S(2)}, u32[]{:S(2)}) collective-permute-start(bf16[384,256]{1,0:T(8,128)(2,1)S(1)} %get-tuple-element.37), channel_id=1, source_target_pairs={{0,1},{1,0},{2,3},{3,2},{4,5},{5,4},{6,7},{7,6},{8,9},{9,8},{10,11... | collective-permute-start | bytes 589832 | tf_op jit(solution)/shard_map/ppermute | solution.py:636
  20.2 6.0 %collective-permute-start.9 = (bf16[384,256]{1,0:T(8,128)(2,1)S(1)}, bf16[384,256]{1,0:T(8,128)(2,1)S(1)}, u32[]{:S(2)}, u32[]{:S(2)}) collective-permute-start(bf16[384,256]{1,0:T(8,128)(2,1)S(1)} %get-tuple-element.38), channel_id=1, source_target_pairs={{0,4},{1,2},{2,1},{3,7},{4,0},{5,6},{6,5},{7,3},{8,12},{9,10},{10,... | collective-permute-start | bytes 589832 | tf_op jit(solution)/shard_map/ppermute | solution.py:637

commit v8 on v7

--- a/solution.py
+++ b/solution.py
@@ -130,12 +130,12 @@
                 ] = block
 
 
-def score_steps(keys, queries, tiles, store):
+def score_steps(keys, queries, tiles, store, whole=True):
     pieces = []
     tops = []
-    whole = mm(keys, queries)
+    joint = mm(keys, queries) if whole else None
     for start, stop, table in tiles:
-        piece = whole[start:stop] + table
+        piece = (joint[start:stop] if whole else mm(keys[start:stop], queries)) + table
         pieces.append(piece)
         tops.append(jnp.max(piece.reshape(-1, 8, piece.shape[1]), axis=0))
         yield
@@ -365,6 +365,7 @@
             ),
             table_tiles(table, corner, pair, at, members, plane, z_first, depth),
             store,
+            whole=False,
         )
 
     def third(unit, store):

time: 31 us -> 31 us (level)
  transfers between devices with their start and end apart: 10 -> 10, of which waited for: 9 -> 9; matrix products, arithmetic and copies ran while one was open for 3% -> 3% of each run, Pallas kernels for 18% -> 17%
where the time goes in v8:
time: 31 us; the launch traced here: 30.6 us
  Pallas kernels  11 us (35%)
  waiting for transfers between devices  9.62 us (31%)
  starting transfers between devices  8.95 us (29%)
  local copies, waits for them, and re-layouts  0.87 us (3%)
    pallas_call x6, Pallas kernels, call(): pl.pallas_call(kernel, in_specs=specs, out_specs=[VMEM] * len(shapes), ou...  11 us
    ppermute x8, starting transfers between devices, swap(): return lax.ppermute(block, 'phase', [(i, i ^ mask) for i in range(bins)])  7.3 us
    ppermute x8, waiting for transfers between devices, swap(): return lax.ppermute(block, 'phase', [(i, i ^ mask) for i in range(bins)])  6.95 us
    ppermute x1, starting transfers between devices, local(): inner = lax.ppermute(inner, ('phase', 'space'), partners(0))  1.64 us
    ppermute x1, waiting for transfers between devices, local(): inner = lax.ppermute(inner, ('phase', 'space'), partners(0))  1.36 us
    ppermute x1, waiting for transfers between devices, local(): outer = lax.ppermute(outer, ('phase', 'space'), partners(1))  1.3 us
    another operation x2, local copies, waits for them, and re-layouts, piece(): jnp.stack([lax.dynamic_slice_in_dim(source, start, chunk, axis=0) for sou...  0.83 us
  transfers between devices with their start and end apart: 10, of which 9 were waited for; matrix products, arithmetic and copies ran while one was open for 3% of the time, Pallas kernels for 17%

profile of v8, /device:TPU:16, one launch (start us, length us, event | category | flops | bytes accessed | tf_op | source)
XLA Modules:
  0.0 30.6 jit_solution(14847118916021505753)
XLA Ops:
  0.0 0.0 collective-permute-start
  0.0 0.8 %dynamic-slice_bitcast_fusion.1 = (bf16[1,64,256]{2,1,0:T(8,128)(2,1)S(1)}, bf16[1,64,256]{2,1,0:T(8,128)(2,1)S(1)}, bf16[1,64,256]{2,1,0:T(8,128)(2,1)S(1)}, bf16[1,64,256]{2,1,0:T(8,128)(2,1)S(1)}) fusion(bf16[512,256]{1,0:T(8,128)(2,1)} %bitcast.30, s32[]{:T(128)S(6)} %select_n.19, s32[]{:T(128)S(6)} %select_n.18, s32[]{:T(128)S(6)} %select_n.17, ...), kind=kLoop, calls=%fused_computation.5 | loop fusion | bytes 262160 | tf_op jit(solution)/shard_map/stack | solution.py:565
  0.8 0.9 %collective-permute-done = bf16[512,256]{1,0:T(8,128)(2,1)S(1)} collective-permute-done((bf16[512,256]{1,0:T(8,128)(2,1)}, bf16[512,256]{1,0:T(8,128)(2,1)S(1)}, u32[]{:S(2)}, u32[]{:S(2)}) %collective-permute-start) | collective-permute-done | bytes 262176 | tf_op jit(solution)/shard_map/ppermute | solution.py:558
  1.8 2.5 %collective-permute-start.1 = (bf16[2,64,256]{2,1,0:T(8,128)(2,1)S(1)}, bf16[2,64,256]{2,1,0:T(8,128)(2,1)S(1)}, u32[]{:S(2)}, u32[]{:S(2)}) collective-permute-start(bf16[2,64,256]{2,1,0:T(8,128)(2,1)S(1)} %pad_maximum_fusion.1), channel_id=1, source_target_pairs={{0,24},{4,28},{8,16},{12,20},{16,8},{20,12},{24,0},{28,4},{1,25},{... | collective-permute-start | bytes 196616 | tf_op jit(solution)/shard_map/ppermute | solution.py:558
  4.3 0.6 %collective-permute-start.2 = (bf16[2,64,256]{2,1,0:T(8,128)(2,1)S(1)}, bf16[2,64,256]{2,1,0:T(8,128)(2,1)S(1)}, u32[]{:S(2)}, u32[]{:S(2)}) collective-permute-start(bf16[2,64,256]{2,1,0:T(8,128)(2,1)S(1)} %pad_maximum_fusion.2), channel_id=1, source_target_pairs={{0,8},{4,12},{8,0},{12,4},{16,24},{20,28},{24,16},{28,20},{1,9},{5... | collective-permute-start | bytes 196616 | tf_op jit(solution)/shard_map/ppermute | solution.py:558
  4.9 0.6 %collective-permute-start.3 = (bf16[2,64,256]{2,1,0:T(8,128)(2,1)S(1)}, bf16[2,64,256]{2,1,0:T(8,128)(2,1)S(1)}, u32[]{:S(2)}, u32[]{:S(2)}) collective-permute-start(bf16[2,64,256]{2,1,0:T(8,128)(2,1)S(1)} %pad_maximum_fusion.3._), channel_id=1, source_target_pairs={{0,16},{4,20},{8,24},{12,28},{16,0},{20,4},{24,8},{28,12},{1,17},{... | collective-permute-start | bytes 196616 | tf_op jit(solution)/shard_map/ppermute | solution.py:558
  5.5 0.0 copy-start.3
  5.5 0.0 copy-start.6
  5.5 0.0 copy-start.2
  5.5 0.0 copy-start.5
  5.5 0.0 copy-start.7
  5.5 2.0 %shard_map.136 = (bf16[768,256]{1,0:T(8,128)(2,1)S(1)}, f32[4,128,256]{2,1,0:T(8,128)S(1)}, f32[4,640,256]{2,1,0:T(8,128)S(1)}) custom-call(s32[8]{0:T(128)} %bin_phase_at.1, s32[3,8]{1,0:T(4,128)} %bitcast.22, f32[8,64]{1,0:T(8,128)} %window_bias_at.1, f32[8,8]{1,0:T(8,128)} %phase_bias_at.1, bf16[256,768]{1,0:T(8,128)(2,1)} %phase_qkv_at.1, ...), custom_call_target="tpu_custom_call" | custom-call | flops 2000000000 | bytes 4194304 | tf_op jit(solution)/shard_map/pallas_call | solution.py:517
  7.5 0.0 collective-permute-done.1.refs_1_
  7.5 1.1 %collective-permute-done.2.refs_2_ = bf16[2,64,256]{2,1,0:T(8,128)(2,1)S(1)} collective-permute-done((bf16[2,64,256]{2,1,0:T(8,128)(2,1)S(1)}, bf16[2,64,256]{2,1,0:T(8,128)(2,1)S(1)}, u32[]{:S(2)}, u32[]{:S(2)}) %collective-permute-start.2) | collective-permute-done | bytes 65568 | tf_op jit(solution)/shard_map/ppermute | solution.py:558
  8.6 0.6 %collective-permute-done.3.refs_3_ = bf16[2,64,256]{2,1,0:T(8,128)(2,1)S(1)} collective-permute-done((bf16[2,64,256]{2,1,0:T(8,128)(2,1)S(1)}, bf16[2,64,256]{2,1,0:T(8,128)(2,1)S(1)}, u32[]{:S(2)}, u32[]{:S(2)}) %collective-permute-start.3) | collective-permute-done | bytes 65568 | tf_op jit(solution)/shard_map/ppermute | solution.py:558
  9.2 0.0 copy-done.3
  9.2 0.0 copy-done.6
  9.2 0.0 copy-start
  9.2 0.0 copy-start.1
  9.2 0.0 copy-start.4
  9.3 0.0 copy-start.8
  9.3 1.3 %shard_map.137 = (bf16[4,64,256]{2,1,0:T(8,128)(2,1)S(1)}, bf16[64,256]{1,0:T(8,128)(2,1)S(1)}, bf16[64,256]{1,0:T(8,128)(2,1)S(1)}, bf16[64,256]{1,0:T(8,128)(2,1)S(1)}, bf16[64,256]{1,0:T(8,128)(2,1)S(1)}) custom-call(bf16[2,64,256]{2,1,0:T(8,128)(2,1)S(1)} %pad_maximum_fusion.refs_0_, bf16[2,64,256]{2,1,0:T(8,128)(2,1)S(1)} %collective-permute-done.1.refs_1_, ...), custom_call_target="tpu_custom_call" | custom-call | flops 335544320 | bytes 1048576 | tf_op jit(solution)/shard_map/pallas_call | solution.py:517
  10.6 0.1 collective-permute-start.4
  10.6 1.3 %collective-permute-done.4.taken = bf16[4,64,256]{2,1,0:T(8,128)(2,1)S(1)} collective-permute-done((bf16[4,64,256]{2,1,0:T(8,128)(2,1)S(1)}, bf16[4,64,256]{2,1,0:T(8,128)(2,1)S(1)}, u32[]{:S(2)}, u32[]{:S(2)}) %collective-permute-start.4) | collective-permute-done | bytes 131104 | tf_op jit(solution)/shard_map/ppermute | solution.py:558
  12.0 1.6 %collective-permute-start.5 = (bf16[2,64,256]{2,1,0:T(8,128)(2,1)S(1)}, bf16[2,64,256]{2,1,0:T(8,128)(2,1)S(1)}, u32[]{:S(2)}, u32[]{:S(2)}) collective-permute-start(bf16[2,64,256]{2,1,0:T(8,128)(2,1)S(1)} %get-tuple-element.33), channel_id=1, source_target_pairs={{0,24},{4,28},{8,16},{12,20},{16,8},{20,12},{24,0},{28,4},{1,25},{... | collective-permute-start | bytes 196616 | tf_op jit(solution)/shard_map/ppermute | solution.py:558
  13.6 0.5 %collective-permute-start.6 = (bf16[2,64,256]{2,1,0:T(8,128)(2,1)S(1)}, bf16[2,64,256]{2,1,0:T(8,128)(2,1)S(1)}, u32[]{:S(2)}, u32[]{:S(2)}) collective-permute-start(bf16[2,64,256]{2,1,0:T(8,128)(2,1)S(1)} %get-tuple-element.34), channel_id=1, source_target_pairs={{0,8},{4,12},{8,0},{12,4},{16,24},{20,28},{24,16},{28,20},{1,9},{5... | collective-permute-start | bytes 196616 | tf_op jit(solution)/shard_map/ppermute | solution.py:558
  14.1 1.5 %collective-permute-start.7 = (bf16[2,64,256]{2,1,0:T(8,128)(2,1)S(1)}, bf16[2,64,256]{2,1,0:T(8,128)(2,1)S(1)}, u32[]{:S(2)}, u32[]{:S(2)}) collective-permute-start(bf16[2,64,256]{2,1,0:T(8,128)(2,1)S(1)} %get-tuple-element.35), channel_id=1, source_target_pairs={{0,16},{4,20},{8,24},{12,28},{16,0},{20,4},{24,8},{28,12},{1,17},{... | collective-permute-start | bytes 196616 | tf_op jit(solution)/shard_map/ppermute | solution.py:558
  15.5 2.1 %collective-permute-done.5.refs_1_ = bf16[2,64,256]{2,1,0:T(8,128)(2,1)S(1)} collective-permute-done((bf16[2,64,256]{2,1,0:T(8,128)(2,1)S(1)}, bf16[2,64,256]{2,1,0:T(8,128)(2,1)S(1)}, u32[]{:S(2)}, u32[]{:S(2)}) %collective-permute-start.5) | collective-permute-done | bytes 65568 | tf_op jit(solution)/shard_map/ppermute | solution.py:558
  17.6 0.2 collective-permute-done.6.refs_2_
  17.8 0.7 %collective-permute-done.7.refs_3_ = bf16[2,64,256]{2,1,0:T(8,128)(2,1)S(1)} collective-permute-done((bf16[2,64,256]{2,1,0:T(8,128)(2,1)S(1)}, bf16[2,64,256]{2,1,0:T(8,128)(2,1)S(1)}, u32[]{:S(2)}, u32[]{:S(2)}) %collective-permute-start.7) | collective-permute-done | bytes 65568 | tf_op jit(solution)/shard_map/ppermute | solution.py:558
  18.5 0.1 shard_map.139
  18.6 1.6 %collective-permute-start.8 = (bf16[384,256]{1,0:T(8,128)(2,1)S(1)}, bf16[384,256]{1,0:T(8,128)(2,1)S(1)}, u32[]{:S(2)}, u32[]{:S(2)}) collective-permute-start(bf16[384,256]{1,0:T(8,128)(2,1)S(1)} %get-tuple-element.37), channel_id=1, source_target_pairs={{0,1},{1,0},{2,3},{3,2},{4,5},{5,4},{6,7},{7,6},{8,9},{9,8},{10,11... | collective-permute-start | bytes 589832 | tf_op jit(solution)/shard_map/ppermute | solution.py:637
  20.2 0.0 collective-permute-start.9
  20.2 0.0 copy-done.2
  20.2 0.0 copy-done.5
  20.2 0.0 copy-done.7
  20.2 3.3 %shard_map.140 = (bf16[256,512]{1,0:T(8,128)(2,1)S(1)}, bf16[256,256]{1,0:T(8,128)(2,1)S(1)}, f32[4,256,128]{2,1,0:T(8,128)S(1)}, f32[4,4,256]{2,1,0:T(4,128)S(1)}, f32[4,4,256]{2,1,0:T(4,128)S(1)}) custom-call(s32[3,8]{1,0:T(4,128)S(1)} %bitcast.23, bf16[512,256]{1,0:T(8,128)(2,1)S(1)} %get-tuple-element.36.own, f32[1,256]{1,0:T(1,128)S(1)} %bitcast.26, ...), custom_call_target="tpu_custom_call" | custom-call | flops 939524096 | bytes 4194304 | tf_op jit(solution)/shard_map/pallas_call | solution.py:517
  23.6 1.4 %collective-permute-done.8.inner = bf16[384,256]{1,0:T(8,128)(2,1)S(1)} collective-permute-done((bf16[384,256]{1,0:T(8,128)(2,1)S(1)}, bf16[384,256]{1,0:T(8,128)(2,1)S(1)}, u32[]{:S(2)}, u32[]{:S(2)}) %collective-permute-start.8) | collective-permute-done | bytes 196640 | tf_op jit(solution)/shard_map/ppermute | solution.py:637
  24.9 1.3 %collective-permute-done.9.outer = bf16[384,256]{1,0:T(8,128)(2,1)S(1)} collective-permute-done((bf16[384,256]{1,0:T(8,128)(2,1)S(1)}, bf16[384,256]{1,0:T(8,128)(2,1)S(1)}, u32[]{:S(2)}, u32[]{:S(2)}) %collective-permute-start.9) | collective-permute-done | bytes 196640 | tf_op jit(solution)/shard_map/ppermute | solution.py:638
  26.2 0.0 copy-done
  26.2 0.0 copy-done.1
  26.2 0.0 copy-done.4
  26.3 0.0 copy-done.8
  26.3 4.4 %shard_map.141 = bf16[512,256]{1,0:T(8,128)(2,1)} custom-call(s32[3,8]{1,0:T(4,128)S(1)} %bitcast.24, bf16[512,256]{1,0:T(8,128)(2,1)S(1)} %get-tuple-element.36.own, bf16[384,256]{1,0:T(8,128)(2,1)S(1)} %collective-permute-done.8.inner, bf16[384,256]{1,0:T(8,128)(2,1)S(1)} %collective-permute-done.9.outer, f32[1,256]{1,0:T(1,128)S(1)} %bitcast.27, ...), custom_call_target="tpu_custom_call" | custom-call | flops 939524096 | bytes 4194304 | tf_op jit(solution)/shard_map/pallas_call | solution.py:517
  (6 shorter events, 0.1 us)
Async XLA Ops:
  0.0 1.7 %collective-permute-start = (bf16[512,256]{1,0:T(8,128)(2,1)}, bf16[512,256]{1,0:T(8,128)(2,1)S(1)}, u32[]{:S(2)}, u32[]{:S(2)}) collective-permute-start(bf16[512,256]{1,0:T(8,128)(2,1)} %bitcast.29), channel_id=1, source_target_pairs={{0,4},{4,0},{8,12},{12,8},{16,20},{20,16},{24,28},{28,24},{1,5},{5... | collective-permute-start | bytes 786440 | tf_op jit(solution)/shard_map/ppermute | solution.py:558
  1.8 5.7 %collective-permute-start.1 = (bf16[2,64,256]{2,1,0:T(8,128)(2,1)S(1)}, bf16[2,64,256]{2,1,0:T(8,128)(2,1)S(1)}, u32[]{:S(2)}, u32[]{:S(2)}) collective-permute-start(bf16[2,64,256]{2,1,0:T(8,128)(2,1)S(1)} %pad_maximum_fusion.1), channel_id=1, source_target_pairs={{0,24},{4,28},{8,16},{12,20},{16,8},{20,12},{24,0},{28,4},{1,25},{... | collective-permute-start | bytes 196616 | tf_op jit(solution)/shard_map/ppermute | solution.py:558
  4.3 4.3 %collective-permute-start.2 = (bf16[2,64,256]{2,1,0:T(8,128)(2,1)S(1)}, bf16[2,64,256]{2,1,0:T(8,128)(2,1)S(1)}, u32[]{:S(2)}, u32[]{:S(2)}) collective-permute-start(bf16[2,64,256]{2,1,0:T(8,128)(2,1)S(1)} %pad_maximum_fusion.2), channel_id=1, source_target_pairs={{0,8},{4,12},{8,0},{12,4},{16,24},{20,28},{24,16},{28,20},{1,9},{5... | collective-permute-start | bytes 196616 | tf_op jit(solution)/shard_map/ppermute | solution.py:558
  4.9 4.3 %collective-permute-start.3 = (bf16[2,64,256]{2,1,0:T(8,128)(2,1)S(1)}, bf16[2,64,256]{2,1,0:T(8,128)(2,1)S(1)}, u32[]{:S(2)}, u32[]{:S(2)}) collective-permute-start(bf16[2,64,256]{2,1,0:T(8,128)(2,1)S(1)} %pad_maximum_fusion.3._), channel_id=1, source_target_pairs={{0,16},{4,20},{8,24},{12,28},{16,0},{20,4},{24,8},{28,12},{1,17},{... | collective-permute-start | bytes 196616 | tf_op jit(solution)/shard_map/ppermute | solution.py:558
  5.5 3.8 %copy-start.3 = (bf16[256,256]{1,0:T(8,128)(2,1)S(1)}, bf16[256,256]{1,0:T(8,128)(2,1)}, u32[]{:S(2)}) copy-start(bf16[256,256]{1,0:T(8,128)(2,1)} %refs_7_.1) | copy-start | bytes 393220
  5.5 3.8 %copy-start.6 = (f32[256]{0:T(256)S(1)}, f32[256]{0:T(256)}, u32[]{:S(2)}) copy-start(f32[256]{0:T(256)} %param.15) | copy-start | bytes 3076
  5.5 14.7 %copy-start.2 = (bf16[256,768]{1,0:T(8,128)(2,1)S(1)}, bf16[256,768]{1,0:T(8,128)(2,1)}, u32[]{:S(2)}) copy-start(bf16[256,768]{1,0:T(8,128)(2,1)} %qkv.3) | copy-start | bytes 1179652
  5.5 14.7 %copy-start.5 = (s32[8,3]{0,1:T(4,128)S(1)}, s32[8,3]{0,1:T(4,128)}, u32[]{:S(2)}) copy-start(s32[8,3]{0,1:T(4,128)} %param.23) | copy-start | bytes 292
  5.5 14.7 %copy-start.7 = (f32[256]{0:T(256)S(1)}, f32[256]{0:T(256)}, u32[]{:S(2)}) copy-start(f32[256]{0:T(256)} %param.20) | copy-start | bytes 3076
  9.2 17.0 %copy-start = (bf16[256,1024]{1,0:T(8,128)(2,1)S(1)}, bf16[256,1024]{1,0:T(8,128)(2,1)}, u32[]{:S(2)}) copy-start(bf16[256,1024]{1,0:T(8,128)(2,1)} %mlp_up.1) | copy-start | bytes 1572868
  9.2 17.0 %copy-start.1 = (bf16[1024,256]{1,0:T(8,128)(2,1)S(1)}, bf16[1024,256]{1,0:T(8,128)(2,1)}, u32[]{:S(2)}) copy-start(bf16[1024,256]{1,0:T(8,128)(2,1)} %mlp_down.1) | copy-start | bytes 1572868
  9.2 17.0 %copy-start.4 = (bf16[256,256]{1,0:T(8,128)(2,1)S(1)}, bf16[256,256]{1,0:T(8,128)(2,1)}, u32[]{:S(2)}) copy-start(bf16[256,256]{1,0:T(8,128)(2,1)} %out_weight.1) | copy-start | bytes 393220
  9.3 17.0 %copy-start.8 = (f32[256]{0:T(256)S(1)}, f32[256]{0:T(256)}, u32[]{:S(2)}) copy-start(f32[256]{0:T(256)} %param.25) | copy-start | bytes 3076
  10.6 1.4 %collective-permute-start.4 = (bf16[4,64,256]{2,1,0:T(8,128)(2,1)S(1)}, bf16[4,64,256]{2,1,0:T(8,128)(2,1)S(1)}, u32[]{:S(2)}, u32[]{:S(2)}) collective-permute-start(bf16[4,64,256]{2,1,0:T(8,128)(2,1)S(1)} %get-tuple-element.27), channel_id=1, source_target_pairs={{0,4},{4,0},{8,12},{12,8},{16,20},{20,16},{24,28},{28,24},{1,5},{5... | collective-permute-start | bytes 393224 | tf_op jit(solution)/shard_map/ppermute | solution.py:558
  12.0 5.6 %collective-permute-start.5 = (bf16[2,64,256]{2,1,0:T(8,128)(2,1)S(1)}, bf16[2,64,256]{2,1,0:T(8,128)(2,1)S(1)}, u32[]{:S(2)}, u32[]{:S(2)}) collective-permute-start(bf16[2,64,256]{2,1,0:T(8,128)(2,1)S(1)} %get-tuple-element.33), channel_id=1, source_target_pairs={{0,24},{4,28},{8,16},{12,20},{16,8},{20,12},{24,0},{28,4},{1,25},{... | collective-permute-start | bytes 196616 | tf_op jit(solution)/shard_map/ppermute | solution.py:558
  13.6 4.3 %collective-permute-start.6 = (bf16[2,64,256]{2,1,0:T(8,128)(2,1)S(1)}, bf16[2,64,256]{2,1,0:T(8,128)(2,1)S(1)}, u32[]{:S(2)}, u32[]{:S(2)}) collective-permute-start(bf16[2,64,256]{2,1,0:T(8,128)(2,1)S(1)} %get-tuple-element.34), channel_id=1, source_target_pairs={{0,8},{4,12},{8,0},{12,4},{16,24},{20,28},{24,16},{28,20},{1,9},{5... | collective-permute-start | bytes 196616 | tf_op jit(solution)/shard_map/ppermute | solution.py:558
  14.1 4.4 %collective-permute-start.7 = (bf16[2,64,256]{2,1,0:T(8,128)(2,1)S(1)}, bf16[2,64,256]{2,1,0:T(8,128)(2,1)S(1)}, u32[]{:S(2)}, u32[]{:S(2)}) collective-permute-start(bf16[2,64,256]{2,1,0:T(8,128)(2,1)S(1)} %get-tuple-element.35), channel_id=1, source_target_pairs={{0,16},{4,20},{8,24},{12,28},{16,0},{20,4},{24,8},{28,12},{1,17},{... | collective-permute-start | bytes 196616 | tf_op jit(solution)/shard_map/ppermute | solution.py:558
  18.6 6.4 %collective-permute-start.8 = (bf16[384,256]{1,0:T(8,128)(2,1)S(1)}, bf16[384,256]{1,0:T(8,128)(2,1)S(1)}, u32[]{:S(2)}, u32[]{:S(2)}) collective-permute-start(bf16[384,256]{1,0:T(8,128)(2,1)S(1)} %get-tuple-element.37), channel_id=1, source_target_pairs={{0,1},{1,0},{2,3},{3,2},{4,5},{5,4},{6,7},{7,6},{8,9},{9,8},{10,11... | collective-permute-start | bytes 589832 | tf_op jit(solution)/shard_map/ppermute | solution.py:637
  20.2 6.0 %collective-permute-start.9 = (bf16[384,256]{1,0:T(8,128)(2,1)S(1)}, bf16[384,256]{1,0:T(8,128)(2,1)S(1)}, u32[]{:S(2)}, u32[]{:S(2)}) collective-permute-start(bf16[384,256]{1,0:T(8,128)(2,1)S(1)} %get-tuple-element.38), channel_id=1, source_target_pairs={{0,4},{1,2},{2,1},{3,7},{4,0},{5,6},{6,5},{7,3},{8,12},{9,10},{10,... | collective-permute-start | bytes 589832 | tf_op jit(solution)/shard_map/ppermute | solution.py:638
